TPU v7x, 128 devices: a whole 4x4x4 slice. The times are simulated.
128 devices in a mesh: seq: 32 (over y_lo, z, x), head: 4 (over y_hi, core).
Axes of the slice: x: 4, y: 4 (y_hi: 2, y_lo: 2; y = y_hi * 2 + y_lo), z: 4, core: 2. Of those that a mesh axis runs over, the one named last changes fastest.
Arguments:
- queries: bfloat16 [8192, 1536], P('seq', 'head'), may hold values from -6 to 6
- keys: bfloat16 [8192, 1536], P('seq', 'head'), may hold values from -6 to 6
- values: bfloat16 [8192, 1536], P('seq', 'head'), may hold values from -6 to 6
- text_keys: bfloat16 [512, 1536], P('seq', 'head'), may hold values from -6 to 6
- text_values: bfloat16 [512, 1536], P('seq', 'head'), may hold values from -6 to 6
- head_bias: float32 [12], P('head'), may hold values from 2 to 4
- out_weight: bfloat16 [1536, 3072], P('head'), may hold values from -0.15625 to 0.15625
- grad_out: bfloat16 [8192, 3072], P('seq', 'head'), may hold values from -6 to 6
- clip_lengths: int32 [4], replicated, may hold values from 1 to 4096, 8192 in all
- tile_mask: int32 [128, 128], replicated, may hold values 0 or 1
- caption_order: int32 [512], replicated, may hold values from 0 to 511, each once
Outputs:
- out: bfloat16 [8192, 3072], P('seq', 'head')
- grad_queries: bfloat16 [8192, 1536], P('seq', 'head')
- grad_keys: bfloat16 [8192, 1536], P('seq', 'head')
- grad_values: bfloat16 [8192, 1536], P('seq', 'head')
- grad_text_keys: bfloat16 [512, 1536], P('seq', 'head')
- grad_text_values: bfloat16 [512, 1536], P('seq', 'head')
Inputs may be any that keep to these rules, and one draw needn't show every extreme that they name: `clip_lengths`: the 4 clip lengths sum to 8192, and the longest clip has exactly 4096 tokens. `tile_mask`: 0/1 entries. Each caption row appears once; clip c's caption is the rows caption_order[c * 128] to caption_order[(c + 1) * 128 - 1].
All inputs are finite; a program needn't handle non-finite values.
Results may differ from a plain program's by a relative error of at most 0.015.
Values may be sent and summed in bfloat16 or wider, within the bound.
A program may use at most 192 MiB of HBM per device.

v0:
```python
import jax
import jax.numpy as jnp
from jax import lax
from jax.sharding import PartitionSpec as P


def clip_ids(position, clip_ends):
    return jnp.sum((position[:, None] >= clip_ends[None, :]).astype(jnp.int32), axis=1)


def one_hot_rows(index, column_count):
    return (index[:, None] == jnp.arange(column_count, dtype=jnp.int32)[None, :]).astype(
        jnp.bfloat16
    )


def contract_last(left_side, right_side):
    return lax.dot_general(
        left_side, right_side, (((1,), (1,)), ((), ())), preferred_element_type=jnp.float32
    )


def shards(
    queries,
    keys,
    values,
    text_keys,
    text_values,
    head_bias,
    out_weight,
    grad_out,
    clip_lengths,
    tile_mask,
    caption_order,
):
    tok_rows = queries.shape[0]
    feature_cols = queries.shape[1]
    heads_here = head_bias.shape[0]
    head_size = feature_cols // heads_here
    factor = head_size ** (-0.5)
    total_rows = tok_rows * lax.axis_size("seq")
    seq_index = lax.axis_index("seq")
    tile_count = tile_mask.shape[0]
    tile_rows = total_rows // tile_count
    clip_count = clip_lengths.shape[0]
    text_total = caption_order.shape[0]
    caption = text_total // clip_count
    text_here = text_keys.shape[0]
    clip_ends = jnp.cumsum(clip_lengths)
    tile_index = jnp.arange(tile_count, dtype=jnp.int32)
    tile_on = ((tile_mask > 0) | (tile_index[:, None] == tile_index[None, :])).astype(jnp.bfloat16)
    clip_index = jnp.arange(clip_count, dtype=jnp.int32)
    text_index = jnp.arange(text_total, dtype=jnp.int32)
    caption_clip = jnp.sum(
        jnp.where(
            caption_order[:, None] == text_index[None, :], (text_index // caption)[:, None], 0
        ),
        axis=0,
    )

    def offsets(clip_id):
        lengths_here = jnp.sum(
            jnp.where(clip_id[:, None] == clip_index[None, :], clip_lengths[None, :], 0), axis=1
        )
        return jnp.log((lengths_here + caption).astype(jnp.float32))

    def pair_keep(query_pos, key_pos):
        rows_on = jnp.dot(
            one_hot_rows(query_pos // tile_rows, tile_count),
            tile_on,
            preferred_element_type=jnp.float32,
        ).astype(jnp.bfloat16)
        hits = contract_last(rows_on, one_hot_rows(key_pos // tile_rows, tile_count))
        return (hits > 0.5) & (
            clip_ids(query_pos, clip_ends)[:, None] == clip_ids(key_pos, clip_ends)[None, :]
        )

    def sigmoid_weights(query_heads, key_heads, query_offset, keep_pairs):
        scores = (
            jnp.einsum("qhd,khd->hqk", query_heads, key_heads, preferred_element_type=jnp.float32)
            * factor
        )
        scores = scores + head_bias[:, None, None] - query_offset[None, :, None]
        return jnp.where(keep_pairs[None], jax.nn.sigmoid(scores), 0.0)

    def score_grads(grad_heads, value_heads, weights, keep_pairs):
        product = jnp.einsum(
            "qhd,khd->hqk", grad_heads, value_heads, preferred_element_type=jnp.float32
        )
        return jnp.where(keep_pairs[None], product * weights * (1.0 - weights), 0.0).astype(
            jnp.bfloat16
        )

    grad_attn = contract_last(
        lax.all_gather(grad_out, "head", axis=1, tiled=True), out_weight
    ).astype(jnp.bfloat16)
    query_heads = queries.reshape(tok_rows, heads_here, head_size)
    grad_heads = grad_attn.reshape(tok_rows, heads_here, head_size)
    my_pos = seq_index * tok_rows + jnp.arange(tok_rows, dtype=jnp.int32)
    my_clip = clip_ids(my_pos, clip_ends)
    my_offset = offsets(my_clip)
    text_key_all, text_value_all = (
        lax.all_gather(text_keys, "seq", axis=0, tiled=True),
        lax.all_gather(text_values, "seq", axis=0, tiled=True),
    )
    text_key_heads = text_key_all.reshape(text_total, heads_here, head_size)
    text_value_heads = text_value_all.reshape(text_total, heads_here, head_size)
    text_keep = my_clip[:, None] == caption_clip[None, :]
    text_weights = sigmoid_weights(query_heads, text_key_heads, my_offset, text_keep)
    text_rounded = text_weights.astype(jnp.bfloat16)
    text_grads = score_grads(grad_heads, text_value_heads, text_weights, text_keep)
    attn_start = jnp.einsum(
        "hqk,khd->qhd", text_rounded, text_value_heads, preferred_element_type=jnp.float32
    )
    query_grad_start = jnp.einsum(
        "hqk,khd->qhd", text_grads, text_key_heads, preferred_element_type=jnp.float32
    )
    initial = (attn_start, query_grad_start)
    key_piece = lax.all_gather(keys, "seq", axis=0, tiled=True)
    value_piece = lax.all_gather(values, "seq", axis=0, tiled=True)
    row_count = key_piece.shape[0]
    key_heads = key_piece.reshape(row_count, heads_here, head_size)
    value_heads = value_piece.reshape(row_count, heads_here, head_size)
    keep_pairs = pair_keep(my_pos, jnp.arange(row_count, dtype=jnp.int32))
    weights = sigmoid_weights(query_heads, key_heads, my_offset, keep_pairs)
    rounded = weights.astype(jnp.bfloat16)
    grads_here = score_grads(grad_heads, value_heads, weights, keep_pairs)
    attn_sum = initial[0] + jnp.einsum(
        "hqk,khd->qhd", rounded, value_heads, preferred_element_type=jnp.float32
    )
    query_sum = initial[1] + jnp.einsum(
        "hqk,khd->qhd", grads_here, key_heads, preferred_element_type=jnp.float32
    )
    own_keys = keys.reshape(tok_rows, heads_here, head_size)
    own_values = values.reshape(tok_rows, heads_here, head_size)
    own_text_keys = text_keys.reshape(text_here, heads_here, head_size)
    own_text_values = text_values.reshape(text_here, heads_here, head_size)
    own_caption = lax.dynamic_slice_in_dim(caption_clip, seq_index * text_here, text_here, 0)
    query_piece = lax.all_gather(queries, "seq", axis=0, tiled=True)
    grad_piece = lax.all_gather(grad_attn, "seq", axis=0, tiled=True)
    row_count = query_piece.shape[0]
    piece_queries = query_piece.reshape(row_count, heads_here, head_size)
    piece_grads = grad_piece.reshape(row_count, heads_here, head_size)
    piece_pos = jnp.arange(row_count, dtype=jnp.int32)
    piece_clip = clip_ids(piece_pos, clip_ends)
    piece_offset = offsets(piece_clip)
    keep_pairs = pair_keep(piece_pos, my_pos)
    keep_caption = piece_clip[:, None] == own_caption[None, :]
    weights = sigmoid_weights(piece_queries, own_keys, piece_offset, keep_pairs)
    grads_here = score_grads(piece_grads, own_values, weights, keep_pairs)
    caption_weights = sigmoid_weights(piece_queries, own_text_keys, piece_offset, keep_caption)
    caption_grads = score_grads(piece_grads, own_text_values, caption_weights, keep_caption)
    key_grad = jnp.einsum(
        "hqk,qhd->khd", grads_here, piece_queries, preferred_element_type=jnp.float32
    )
    value_grad = jnp.einsum(
        "hqk,qhd->khd",
        weights.astype(jnp.bfloat16),
        piece_grads,
        preferred_element_type=jnp.float32,
    )
    text_key_grad = jnp.einsum(
        "hqk,qhd->khd", caption_grads, piece_queries, preferred_element_type=jnp.float32
    )
    text_value_grad = jnp.einsum(
        "hqk,qhd->khd",
        caption_weights.astype(jnp.bfloat16),
        piece_grads,
        preferred_element_type=jnp.float32,
    )
    attn = attn_sum.astype(jnp.bfloat16).reshape(tok_rows, feature_cols)
    out = lax.psum_scatter(
        jnp.dot(attn, out_weight, preferred_element_type=jnp.float32).astype(jnp.bfloat16),
        "head",
        scatter_dimension=1,
        tiled=True,
    )
    grad_queries = (query_sum * factor).astype(jnp.bfloat16).reshape(tok_rows, feature_cols)
    grad_keys = (key_grad * factor).astype(jnp.bfloat16).reshape(tok_rows, feature_cols)
    grad_values = value_grad.astype(jnp.bfloat16).reshape(tok_rows, feature_cols)
    grad_text_keys = (text_key_grad * factor).astype(jnp.bfloat16).reshape(text_here, feature_cols)
    grad_text_values = text_value_grad.astype(jnp.bfloat16).reshape(text_here, feature_cols)
    return (out, grad_queries, grad_keys, grad_values, grad_text_keys, grad_text_values)


def solution(mesh):
    in_specs = (
        P("seq", "head"),
        P("seq", "head"),
        P("seq", "head"),
        P("seq", "head"),
        P("seq", "head"),
        P("head"),
        P("head", None),
        P("seq", "head"),
        P(),
        P(),
        P(),
    )
    out_specs = (
        P("seq", "head"),
        P("seq", "head"),
        P("seq", "head"),
        P("seq", "head"),
        P("seq", "head"),
        P("seq", "head"),
    )
    return jax.shard_map(shards, mesh=mesh, in_specs=in_specs, out_specs=out_specs, check_vma=False)
```

profile of v0, /device:TPU:0, one launch (start us, length us, event | category | flops | bytes accessed | tf_op | source)
XLA Modules:
  0.0 734.3 jit_solution(18181088595945762800)
XLA Ops:
  12.4 1.8 copy.104
  14.1 85.3 %all_gather.22 = bf16[512,384]{1,0:T(8,128)(2,1)S(1)} all-gather(bf16[16,384]{1,0:T(8,128)(2,1)} %param.15), channel_id=1, replica_groups=mesh['seq'=32,'head'=4] {'seq'}, dimensions={0}, use_global_device_ids=true | all-gather | bytes 405504 | tf_op jit(solution)/shard_map/all_gather | solution.py:104
  99.7 78.3 %all_gather.21 = bf16[512,384]{1,0:T(8,128)(2,1)S(1)} all-gather(bf16[16,384]{1,0:T(8,128)(2,1)} %param.14), channel_id=1, replica_groups=mesh['seq'=32,'head'=4] {'seq'}, dimensions={0}, use_global_device_ids=true | all-gather | bytes 405504 | tf_op jit(solution)/shard_map/all_gather | solution.py:103
  183.5 3.1 convolution_convert_fusion.2
  187.0 2.9 divide_select_fusion.2
  189.9 4.1 fusion.15
  194.0 4.2 fusion.14
  199.1 2.0 all-gather.8.cloned.1.call-done
  201.1 8.6 %copy.97 = bf16[8192,384]{0,1:T(8,128)(2,1)} copy(bf16[8192,384]{1,0:T(8,128)(2,1)} %all-gather.8.cloned.1.call-done) | data formatting | bytes 12582912 | tf_op jit(solution)/shard_map/all_gather | solution.py:120
  209.7 145.9 %all-gather.6.cloned.1.call-done = bf16[8192,384]{0,1:T(8,128)(2,1)} async-done(((bf16[256,384]{0,1:T(8,128)(2,1)}), bf16[8192,384]{0,1:T(8,128)(2,1)}) %all-gather.6.cloned.1.call-update) | async-done | bytes 6291472 | tf_op jit(solution)/shard_map/all_gather | solution.py:119
  355.6 17.0 %divide_select_fusion.1 = f32[3,256,8192]{2,1,0:T(8,128)} fusion(bf16[256,3,128]{0,2,1:T(8,128)(2,1)S(1)} %bitcast.96, bf16[8192,3,128]{0,2,1:T(8,128)(2,1)} %bitcast.107, f32[256]{0:T(256)S(1)} %convert_log_fusion.1, f32[3]{0:T(128)S(1)} %copy-done.12, pred[256,8192]{1,0:T(8,128)(4,1)} %fusion.15), kind=kOutput, calls=%fused_computation.3 | convolution fusion | flops 1654652928 | bytes 33752076 | tf_op jit(solution)/shard_map/qhd,khd->hqk/dot_general | solution.py:80
  372.6 16.3 %fusion.16 = f32[3,256,128]{1,2,0:T(8,128)} fusion(bf16[8192,3,128]{0,2,1:T(8,128)(2,1)} %bitcast.108, f32[3,256,8192]{2,1,0:T(8,128)} %divide_select_fusion.1, bf16[256,3,128]{0,2,1:T(8,128)(2,1)S(1)} %bitcast.100, bf16[8192,3,128]{0,2,1:T(8,128)(2,1)} %bitcast.82, pred[256,8192]{1,0:T(8,128)(4,1)} %fusion.15), kind=kOutput, calls=%fused_computation.25 | convolution fusion | flops 3252682752 | bytes 40435712 | tf_op jit(solution)/shard_map/hqk,khd->qhd/dot_general | solution.py:131
  388.9 2.9 fusion.26
  393.5 12.2 %fusion.2 = f32[3,256,128]{1,2,0:T(8,128)S(1)} fusion(bf16[8192,3,128]{0,2,1:T(8,128)(2,1)} %bitcast.83, f32[3,256,8192]{2,1,0:T(8,128)} %divide_select_fusion.1), kind=kOutput, calls=%fused_computation.6 | convolution fusion | flops 1616904192 | bytes 31850496 | tf_op jit(solution)/shard_map/hqk,khd->qhd/dot_general | solution.py:128
  406.2 2.1 convolution_convert_fusion.1
  408.4 102.1 %all-gather.14.cloned.1.call-done = bf16[8192,384]{0,1:T(8,128)(2,1)} async-done(((bf16[256,384]{0,1:T(8,128)(2,1)}), bf16[8192,384]{0,1:T(8,128)(2,1)}) %all-gather.14.cloned.1.call-update) | async-done | bytes 6291472 | tf_op jit(solution)/shard_map/all_gather | solution.py:139
  510.4 5.2 fusion.13
  515.6 14.0 %divide_select_fusion = f32[3,8192,256]{2,1,0:T(8,128)} fusion(bf16[8192,3,128]{0,2,1:T(8,128)(2,1)S(1)} %bitcast.89, bf16[256,3,128]{0,2,1:T(8,128)(2,1)S(1)} %bitcast.94, f32[8192]{0:T(1024)S(1)} %convert_log_fusion, f32[3]{0:T(128)S(1)} %copy-done.12, pred[8192,256]{1,0:T(8,128)(4,1)S(1)} %copy-done.13), kind=kOutput, calls=%fused_computation.1 | convolution fusion | flops 1654652928 | bytes 33783820 | tf_op jit(solution)/shard_map/qhd,khd->hqk/dot_general | solution.py:80
  529.6 146.4 %all-gather.12.cloned.1.call-done = bf16[8192,384]{1,0:T(8,128)(2,1)} async-done(((bf16[256,384]{1,0:T(8,128)(2,1)}), bf16[8192,384]{1,0:T(8,128)(2,1)}) %all-gather.12.cloned.1.call-update) | async-done | bytes 6291472 | tf_op jit(solution)/shard_map/all_gather | solution.py:140
  676.1 8.6 %copy.103 = bf16[8192,384]{0,1:T(8,128)(2,1)} copy(bf16[8192,384]{1,0:T(8,128)(2,1)} %all-gather.12.cloned.1.call-done) | data formatting | bytes 12582912 | tf_op jit(solution)/shard_map/all_gather | solution.py:140
  684.7 15.7 %fusion.34 = bf16[3,256,128]{1,2,0:T(8,128)(2,1)S(1)} fusion(bf16[8192,3,128]{0,2,1:T(8,128)(2,1)} %bitcast.85, f32[3,8192,256]{2,1,0:T(8,128)} %divide_select_fusion, bf16[8192,3,128]{0,2,1:T(8,128)(2,1)} %bitcast.78, bf16[256,3,128]{0,2,1:T(8,128)(2,1)S(1)} %bitcast.99, pred[8192,256]{1,0:T(8,128)(4,1)S(1)} %copy-done.13), kind=kOutput, calls=%fused_computation.49 | convolution fusion | flops 3252879360 | bytes 40239104 | tf_op jit(solution)/shard_map/hqk,qhd->khd/dot_general | solution.py:153
  701.2 12.0 %fusion.23 = bf16[3,128,256]{2,1,0:T(8,128)(2,1)S(1)} fusion(bf16[8192,3,128]{0,2,1:T(8,128)(2,1)} %bitcast.79, f32[3,8192,256]{2,1,0:T(8,128)} %divide_select_fusion), kind=kOutput, calls=%fused_computation.37 | convolution fusion | flops 1617002496 | bytes 31653888 | tf_op jit(solution)/shard_map/hqk,qhd->khd/dot_general | solution.py:156
  714.0 5.1 fusion.32
  719.2 7.6 %fusion.31 = bf16[3,2,8,128]{3,2,1,0:T(8,128)(2,1)S(1)} fusion(bf16[8192,3,128]{0,2,1:T(8,128)(2,1)} %bitcast.86, f32[3,8192,16]{1,2,0:T(8,128)} %fusion.13, bf16[8192,3,128]{0,2,1:T(8,128)(2,1)} %bitcast.81, pred[8192,16]{0,1:T(8,128)(4,1)S(1)} %broadcast_compare_fusion, bf16[16,384]{1,0:T(8,128)(2,1)S(1)} %copy-done.10), kind=kOutput, calls=%fused_computation.46 | convolution fusion | flops 203304960 | bytes 14311424 | tf_op jit(solution)/shard_map/hqk,qhd->khd/dot_general | solution.py:162
  (73 shorter events, 16.6 us)
Async XLA Ops:
  7.2 176.3 %copy-start = (bf16[384,3072]{1,0:T(8,128)(2,1)S(1)}, bf16[384,3072]{1,0:T(8,128)(2,1)}, u32[]{:S(2)}) copy-start(bf16[384,3072]{1,0:T(8,128)(2,1)} %param.17) | copy-start | bytes 7077892
  7.2 179.8 %copy-start.12 = (f32[3]{0:T(128)S(1)}, f32[3]{0:T(128)}, u32[]{:S(2)}) copy-start(f32[3]{0:T(128)} %param.16) | copy-start | bytes 40
  7.2 176.3 %all-gather.10.cloned.1.call-start = ((), (), s32[]{:S(2)}) async-start(), calls=%async_computation.4 | async-start | bytes 1966080 | tf_op jit(solution)/shard_map/all_gather | solution.py:95
  7.9 193.1 %all-gather.8.cloned.1.call-start = ((), (), s32[]{:S(2)}) async-start(), calls=%async_computation.2 | async-start | bytes 6488064 | tf_op jit(solution)/shard_map/all_gather | solution.py:120
  8.7 346.9 %all-gather.6.cloned.1.call-start = ((), (), s32[]{:S(2)}) async-start(), calls=%async_computation.1 | async-start | bytes 6488064 | tf_op jit(solution)/shard_map/all_gather | solution.py:119
  10.5 499.9 %all-gather.14.cloned.1.call-start = ((), (), s32[]{:S(2)}) async-start(), calls=%async_computation.6 | async-start | bytes 6488064 | tf_op jit(solution)/shard_map/all_gather | solution.py:139
  12.3 174.7 %copy-start.4 = (bf16[256,384]{0,1:T(8,128)(2,1)S(1)}, bf16[256,384]{0,1:T(8,128)(2,1)}, u32[]{:S(2)}) copy-start(bf16[256,384]{0,1:T(8,128)(2,1)} %copy.89) | copy-start | bytes 589828
  12.3 663.7 %all-gather.12.cloned.1.call-start = ((), (), s32[]{:S(2)}) async-start(), calls=%async_computation.5 | async-start | bytes 6488064 | tf_op jit(solution)/shard_map/all_gather | solution.py:140
  186.6 540.8 %reduce-scatter.2.cloned.1.call-start = ((), (), s32[]{:S(2)}) async-start(), calls=%async_computation.3 | async-start | bytes 1966080 | tf_op jit(solution)/shard_map/reduce_scatter | solution.py:172
  187.0 2.9 copy-start.9
  194.0 4.3 copy-start.5
  355.6 17.0 %copy-start.8 = (bf16[256,384]{0,1:T(8,128)(2,1)S(1)}, bf16[256,384]{0,1:T(8,128)(2,1)}, u32[]{:S(2)}) copy-start(bf16[256,384]{0,1:T(8,128)(2,1)} %copy.98) | copy-start | bytes 589828
  372.6 16.3 %copy-start.6 = (bf16[512,384]{0,1:T(8,128)(2,1)S(1)}, bf16[512,384]{0,1:T(8,128)(2,1)}, u32[]{:S(2)}) copy-start(bf16[512,384]{0,1:T(8,128)(2,1)} %copy.90) | copy-start | bytes 1179652
  393.5 12.2 %copy-start.2 = (f32[3,256,512]{2,1,0:T(8,128)S(1)}, f32[3,256,512]{2,1,0:T(8,128)}, u32[]{:S(2)}) copy-start(f32[3,256,512]{2,1,0:T(8,128)} %divide_select_fusion.2) | copy-start | bytes 4718596
  405.8 104.7 %copy-start.11 = (bf16[16,384]{1,0:T(8,128)(2,1)S(1)}, bf16[16,384]{1,0:T(8,128)(2,1)}, u32[]{:S(2)}) copy-start(bf16[16,384]{1,0:T(8,128)(2,1)} %param.14) | copy-start | bytes 36868
  408.4 107.3 %copy-start.3 = (bf16[256,384]{0,1:T(8,128)(2,1)S(1)}, bf16[256,384]{0,1:T(8,128)(2,1)}, u32[]{:S(2)}) copy-start(bf16[256,384]{0,1:T(8,128)(2,1)} %copy.94) | copy-start | bytes 589828
  408.4 107.3 %copy-start.13 = (pred[8192,256]{1,0:T(8,128)(4,1)S(1)}, pred[8192,256]{1,0:T(8,128)(4,1)}, u32[]{:S(2)}) copy-start(pred[8192,256]{1,0:T(8,128)(4,1)} %fusion.14) | copy-start | bytes 6291460
  510.4 5.2 slice-start
  510.4 5.2 slice-start.1
  529.6 155.1 %copy-start.7 = (bf16[256,384]{0,1:T(8,128)(2,1)S(1)}, bf16[256,384]{0,1:T(8,128)(2,1)}, u32[]{:S(2)}) copy-start(bf16[256,384]{0,1:T(8,128)(2,1)} %copy.104) | copy-start | bytes 589828
  713.2 5.9 copy-start.10
  714.0 13.4 %copy-start.1 = (bf16[384,3072]{1,0:T(8,128)(2,1)S(1)}, bf16[384,3072]{1,0:T(8,128)(2,1)}, u32[]{:S(2)}) copy-start(bf16[384,3072]{1,0:T(8,128)(2,1)} %param.17) | copy-start | bytes 7077892
Sparse Core Ops, SparseCore 0:
  9.7 26.1 all-gather.9
  37.5 163.4 all-gather.7
  203.2 152.2 all-gather.5
  357.6 152.8 all-gather.13
  511.9 164.0 all-gather.11
  679.1 35.4 reduce-scatter.1
where the time goes:
time: 735 us; the launch traced here: 734 us
  waiting for transfers between devices  398 us (54%)
  blocking collectives  164 us (22%)
  matrix products  125 us (17%)
  local copies, waits for them, and re-layouts  28.6 us (4%)
  between operations  14.3 us (2%)
    all_gather x1, waiting for transfers between devices, shards(): grad_piece = lax.all_gather(grad_attn, 'seq', axis=0, tiled=True)  146 us
    all_gather x1, waiting for transfers between devices, shards(): key_piece = lax.all_gather(keys, 'seq', axis=0, tiled=True)  146 us
    all_gather x1, waiting for transfers between devices, shards(): query_piece = lax.all_gather(queries, 'seq', axis=0, tiled=True)  102 us
    all_gather x1, blocking collectives, shards(): lax.all_gather(text_values, 'seq', axis=0, tiled=True)  85.3 us
    all_gather x1, blocking collectives, shards(): lax.all_gather(text_keys, 'seq', axis=0, tiled=True)  78.3 us
    dot_general x4, matrix products, sigmoid_weights(): jnp.einsum('qhd,khd->hqk', query_heads, key_heads, preferred_element_type...  39 us
    dot_general x1, matrix products, shards(): jnp.einsum('hqk,khd->qhd', grads_here, key_heads, preferred_element_type=...  16.3 us
    dot_general x1, matrix products, shards(): jnp.einsum('hqk,qhd->khd', grads_here, piece_queries, preferred_element_t...  15.7 us
  transfers between devices with their start and end apart: 6, of which 4 were waited for; matrix products, arithmetic and copies ran while one was open for 22% of the time, Pallas kernels for 0%

commit v1 on v0

v1 whole, which is shorter than its diff:
```python
import functools

import jax
import jax.numpy as jnp
from jax import lax
from jax.experimental import pallas as pl
from jax.experimental.pallas import tpu as pltpu
from jax.sharding import PartitionSpec as P

MESH = pl.DeviceIdType.MESH
BF = jnp.bfloat16
F32 = jnp.float32

NX, NZ, NY = 4, 4, 2
HS = 128
NH = 3
TR = 256
CR = 16
BR = TR + CR
HALF = TR // 2
CLIPS = 4
CAP = 128
TILE = 64
LAT = NY * NX * TR
ROWS = NY * NX * BR
MASKED = -32768.0
VMEM_LIMIT = 48 * 1024 * 1024


def place():
    seq = lax.axis_index("seq")
    head = lax.axis_index("head")
    y = seq // (NZ * NX)
    z = (seq // NX) % NZ
    x = seq % NX
    return seq, head, y, z, x


def peers(seq, head, y, z, x):
    def at(yy, zz, xx):
        return (yy * NZ + zz) * NX + xx

    other_head = (head + 2) % 4
    core_head = head + 1 - 2 * (head % 2)
    return {
        "pair": (at(1 - y, z, x), head),
        "back": (at(1 - y, z, x), other_head),
        "core": (seq, core_head),
        "right": (at(y, z, (x + 1) % NX), head),
        "left": (at(y, z, (x + NX - 1) % NX), head),
        "up": (at(y, (z + 1) % NZ, x), head),
        "down": (at(y, (z + NZ - 1) % NZ, x), head),
    }


def greet(peer):
    barrier = pltpu.get_barrier_semaphore()
    for device in peer.values():
        pl.semaphore_signal(barrier, inc=1, device_id=device, device_id_type=MESH)
    pl.semaphore_wait(barrier, len(peer))


def sender(peer, send_sem, recv_sem, sent):
    def send(n, src, dst, to):
        copy = pltpu.make_async_remote_copy(
            src_ref=src,
            dst_ref=dst,
            send_sem=send_sem.at[n],
            recv_sem=recv_sem.at[n],
            device_id=peer[to],
            device_id_type=MESH,
        )
        copy.start()
        sent.append(copy)

    def arrived(n, dst):
        pltpu.make_async_remote_copy(
            src_ref=dst,
            dst_ref=dst,
            send_sem=send_sem.at[n],
            recv_sem=recv_sem.at[n],
            device_id=peer["core"],
            device_id_type=MESH,
        ).wait_recv()

    return send, arrived


def dot_nt(a, b):
    return lax.dot_general(a, b, (((1,), (1,)), ((), ())), preferred_element_type=F32)


def dot_nn(a, b):
    return lax.dot_general(a, b, (((1,), (0,)), ((), ())), preferred_element_type=F32)


def dot_tn(a, b):
    return lax.dot_general(a, b, (((0,), (0,)), ((), ())), preferred_element_type=F32)


def gather_kernel(
    q_ref,
    k_ref,
    v_ref,
    tk_ref,
    tv_ref,
    go_ref,
    w_ref,
    qg_ref,
    kv_ref,
    st_own,
    st_pair,
    qz,
    q_pair,
    goall,
    relay,
    acc,
    send_sem,
    recv_sem,
    local_sem,
):
    seq, head, y, z, x = place()
    peer = peers(seq, head, y, z, x)
    zu, zd = (z + 1) % NZ, (z + NZ - 1) % NZ
    xr, xl = (x + 1) % NX, (x + NX - 1) % NX
    other_head = (head + 2) % 4
    core_head = head + 1 - 2 * (head % 2)
    first, second = pl.ds(0, HALF), pl.ds(HALF, HALF)
    sent = []
    send, arrived = sender(peer, send_sem, recv_sem, sent)
    cols = lambda h: slice(h * HS, (h + 1) * HS)
    by_y = lambda a, b: jnp.where(y == 0, a, b)

    greet(peer)

    send(0, go_ref.at[first], relay.at[0], "pair")
    send(1, go_ref.at[second], relay.at[1], "back")
    send(2, go_ref, goall.at[head], "core")

    for t, (ref, text) in enumerate(((k_ref, tk_ref), (v_ref, tv_ref))):
        st_own[t, 0, 0:TR] = by_y(ref[:, cols(0)], ref[:, cols(1)])
        st_own[t, 0, TR:BR] = by_y(text[:, cols(0)], text[:, cols(1)])
        st_own[t, 1, 0:TR] = ref[:, cols(2)]
        st_own[t, 1, TR:BR] = text[:, cols(2)]
        c = y * NX + x
        send(10 + 2 * t, st_own.at[t], kv_ref.at[t, c], "right")
        send(11 + 2 * t, st_own.at[t], kv_ref.at[t, c], "left")
        st_pair[t, 0, 0:TR] = by_y(ref[:, cols(1)], ref[:, cols(0)])
        st_pair[t, 0, TR:BR] = by_y(text[:, cols(1)], text[:, cols(0)])
        st_pair[t, 1, 0:TR] = ref[:, cols(2)]
        st_pair[t, 1, TR:BR] = text[:, cols(2)]
    qz[0, y] = by_y(q_ref[:, cols(0)], q_ref[:, cols(1)])
    qz[0, 2] = q_ref[:, cols(2)]
    q_pair[0] = by_y(q_ref[:, cols(1)], q_ref[:, cols(0)])
    own = []
    for t in range(2):
        copy = pltpu.make_async_copy(st_own.at[t], kv_ref.at[t, y * NX + x], local_sem.at[t])
        copy.start()
        own.append(copy)

    def z_send(t):
        base = 22 + 6 * t
        send(base + 0, qz.at[t, :, first], qg_ref.at[t, z, :, first], "up")
        send(base + 3, qz.at[t, :, second], qg_ref.at[t, z, :, second], "down")
        send(base + 1, qz.at[t, :, first], qg_ref.at[t, z, :, first], "down")
        send(base + 2, qz.at[t, :, second], qg_ref.at[t, z, :, second], "up")
        copy = pltpu.make_async_copy(qz.at[t], qg_ref.at[t, z], local_sem.at[2 + t])
        copy.start()
        own.append(copy)

    def z_forward(t):
        base = 22 + 6 * t
        arrived(base + 0, qg_ref.at[t, zd, :, first])
        send(base + 4, qg_ref.at[t, zd, :, first], qg_ref.at[t, zd, :, first], "up")
        arrived(base + 3, qg_ref.at[t, zu, :, second])
        send(base + 5, qg_ref.at[t, zu, :, second], qg_ref.at[t, zu, :, second], "down")

    def z_finish(t):
        base = 22 + 6 * t
        far = (z + 2) % NZ
        arrived(base + 1, qg_ref.at[t, zu, :, first])
        arrived(base + 2, qg_ref.at[t, zd, :, second])
        arrived(base + 4, qg_ref.at[t, far, :, first])
        arrived(base + 5, qg_ref.at[t, far, :, second])

    def x_forward(a, yy):
        base = 10 + 6 * a
        arrived(base + 0, kv_ref.at[0, yy * NX + xl])
        send(base + 4, kv_ref.at[0, yy * NX + xl], kv_ref.at[0, yy * NX + xl], "right")
        arrived(base + 3, kv_ref.at[1, yy * NX + xr])
        send(base + 5, kv_ref.at[1, yy * NX + xr], kv_ref.at[1, yy * NX + xr], "left")

    def x_finish(a, yy):
        base = 10 + 6 * a
        far = yy * NX + (x + 2) % NX
        arrived(base + 1, kv_ref.at[0, yy * NX + xr])
        arrived(base + 2, kv_ref.at[1, yy * NX + xl])
        arrived(base + 4, kv_ref.at[0, far])
        arrived(base + 5, kv_ref.at[1, far])

    def feature(n):
        return w_ref[:, pl.ds(pl.multiple_of(n * 768, 128), 768)]

    acc[...] = dot_nt(go_ref[...], feature(head))
    arrived(0, relay.at[0])
    send(3, relay.at[0], goall.at[head, first], "back")
    arrived(1, relay.at[1])
    send(4, relay.at[1], goall.at[other_head, second], "pair")
    send(6, q_pair.at[0], qz.at[0, y], "pair")
    for t in range(2):
        send(7 + t, st_pair.at[t], kv_ref.at[t, y * NX + x], "pair")
    arrived(2, goall.at[core_head])
    acc[...] += dot_nt(goall[core_head], feature(core_head))
    x_forward(0, y)
    arrived(3, goall.at[other_head, first])
    arrived(4, goall.at[other_head, second])
    send(5, goall.at[other_head], goall.at[other_head], "core")
    acc[...] += dot_nt(goall[other_head], feature(other_head))
    arrived(6, qz.at[0, 1 - y])
    z_send(0)
    last = core_head + 2 - 4 * (core_head // 2)
    arrived(5, goall.at[last])
    grad = (acc[...] + dot_nt(goall[last], feature(last))).astype(BF)
    q_pair[1] = by_y(grad[:, cols(1)], grad[:, cols(0)])
    send(9, q_pair.at[1], qz.at[1, y], "pair")
    qz[1, y] = by_y(grad[:, cols(0)], grad[:, cols(1)])
    qz[1, 2] = grad[:, cols(2)]
    for t in range(2):
        c = (1 - y) * NX + x
        arrived(7 + t, kv_ref.at[t, c])
        send(16 + 2 * t, kv_ref.at[t, c], kv_ref.at[t, c], "right")
        send(17 + 2 * t, kv_ref.at[t, c], kv_ref.at[t, c], "left")
    arrived(9, qz.at[1, 1 - y])
    z_send(1)
    z_forward(0)
    z_forward(1)
    x_forward(1, 1 - y)
    z_finish(0)
    z_finish(1)
    x_finish(0, y)
    x_finish(1, 1 - y)
    for copy in own:
        copy.wait()
    for copy in sent:
        copy.wait_send()


def attend_kernel(
    qg_ref,
    kv_ref,
    tile_ref,
    order_ref,
    len_ref,
    bias_ref,
    oq_ref,
    kvg_ref,
    kaug,
    vall,
    qaug,
    oacc,
    qacc,
    kacc,
    vacc,
):
    seq, head, y, z, x = place()
    factor = HS ** (-0.5)
    ends = [len_ref[0]]
    for c in range(1, CLIPS):
        ends.append(ends[-1] + len_ref[c])

    def clip_at(pos):
        total = 0
        for c in range(CLIPS - 1):
            total = total + jnp.where(pos >= ends[c], 1, 0)
        return total

    lane = lax.broadcasted_iota(jnp.int32, (1, HS), 1)
    tiles_here = (lane % 64) // 16 == z
    clip_lane = ((z + 1) % NZ) * 16
    bias_lane = clip_lane + CLIPS

    bias_ones = jnp.where((lane >= bias_lane) & (lane < bias_lane + 3), 1.0, 0.0)
    for c in range(NY * NX):
        first_pos = (c // NX) * (NZ * NX * TR) + z * (NX * TR) + (c % NX) * TR
        pos = first_pos + lax.broadcasted_iota(jnp.int32, (TR, HS), 0)
        hit = (tiles_here & (pos // TILE == lane)) | (clip_at(pos) == lane - clip_lane)
        aug = jnp.where(hit, 1.0, bias_ones).astype(BF)
        for s in range(2):
            kaug[s, c * TR : (c + 1) * TR, 0:HS] = kv_ref[0, c, s, 0:TR]
            kaug[s, c * TR : (c + 1) * TR, HS:] = aug
            vall[s, c * TR : (c + 1) * TR] = kv_ref[1, c, s, 0:TR]
            kaug[s, LAT + c * CR : LAT + (c + 1) * CR, 0:HS] = kv_ref[0, c, s, TR:BR]
            vall[s, LAT + c * CR : LAT + (c + 1) * CR] = kv_ref[1, c, s, TR:BR]
    text = lax.broadcasted_iota(jnp.int32, (NY * NX * CR, HS), 0)
    text_row = ((text // (NX * CR)) * NZ + z) * (NX * CR) + text % (NX * CR)
    aug = jnp.broadcast_to(bias_ones, text_row.shape)
    for c in range(CLIPS):
        listed = jnp.where(order_ref[c : c + 1, :] == text_row, 1.0, 0.0)
        found = jnp.max(listed, axis=1, keepdims=True)
        aug = jnp.where(lane == clip_lane + c, found, aug)
    for s in range(2):
        kaug[s, LAT:, HS:] = aug.astype(BF)

    kacc[...] = jnp.zeros_like(kacc)
    vacc[...] = jnp.zeros_like(vacc)

    log_len = [
        jnp.log(jnp.full((1, HS), len_ref[c] + CAP, jnp.int32).astype(F32)) for c in range(CLIPS)
    ]
    log2e = 1.4426950408889634

    def query_chunk(n, carry):
        zq = n // NH
        j = n % NH
        shared = j == 2
        slot = jnp.where(shared, 1, 0)
        yq = jnp.where(shared, y, j)
        own_head = jnp.where(shared, 2, y)
        start = ((yq * NZ + zq) * NX + x) * TR
        head_bias = bias_ref[own_head]
        pos = start + lax.broadcasted_iota(jnp.int32, (TR, HS), 0)
        clip = clip_at(pos)
        offset = jnp.broadcast_to(log_len[CLIPS - 1], (TR, HS))
        for c in range(CLIPS - 2, -1, -1):
            offset = jnp.where(pos < ends[c], log_len[c], offset)
        total = (head_bias - offset) * (HS**0.5)
        hi = total.astype(BF).astype(F32)
        mid = (total - hi).astype(BF).astype(F32)
        low = total - hi - mid
        in_bias = jnp.where(
            lane == bias_lane, hi, jnp.where(lane == bias_lane + 1, mid, low)
        )
        in_bias = jnp.where((lane >= bias_lane) & (lane < bias_lane + 3), in_bias, 0.0)
        in_clip = (lane >= clip_lane) & (lane < clip_lane + CLIPS) & (lane - clip_lane != clip)
        side = jnp.where(in_clip, MASKED, in_bias)
        for u in range(TR // TILE):
            tile = start // TILE + u
            off = (tile_ref[pl.ds(tile, 1), :] == 0) & (lane != tile) & tiles_here
            rows = slice(u * TILE, (u + 1) * TILE)
            qaug[rows, HS:] = jnp.where(off, MASKED, side[rows]).astype(BF)
        qaug[:, 0:HS] = qg_ref[0, zq, j]

        def block(first_row, count, fresh):
            rows = pl.ds(first_row, count)
            keys = kaug[slot, rows, :]
            queries = qaug[:, 0:HS]
            grads = qg_ref[1, zq, j]
            scores = dot_nt(qaug[...], keys)
            e = jnp.exp2(jnp.minimum(scores * (factor * log2e), 115.0))
            rest = pl.reciprocal(1.0 + e, approx=True)
            sig = e * rest
            weight = sig.astype(BF)
            product = dot_nt(grads, vall[slot, rows, :])
            slope = (product * (sig * rest)).astype(BF)
            o_part = dot_nn(weight, vall[slot, rows, :])
            q_part = dot_nn(slope, keys[:, 0:HS])
            if fresh:
                oacc[...] = o_part
                qacc[...] = q_part
            else:
                oacc[...] += o_part
                qacc[...] += q_part
            vacc[slot, rows, :] += dot_tn(weight, grads)
            kacc[slot, rows, :] += dot_tn(slope, queries)

        block(LAT, NY * NX * CR, True)
        q_low, q_high = clip_at(start), clip_at(start + TR - 1)
        width = 512
        for b in range(LAT // width):
            per_plane = NX * TR // width
            k_start = (b // per_plane) * (NZ * NX * TR) + z * (NX * TR) + (b % per_plane) * width
            k_low, k_high = clip_at(k_start), clip_at(k_start + width - 1)

            @pl.when((q_low <= k_high) & (k_low <= q_high))
            def _():
                block(b * width, width, False)

        oq_ref[0, zq, j] = oacc[...].astype(BF)
        oq_ref[1, zq, j] = qacc[...].astype(BF)
        return carry

    lax.fori_loop(0, NZ * NH, query_chunk, 0)
    for t, total in enumerate((kacc, vacc)):
        for c in range(NY * NX):
            for s in range(2):
                kvg_ref[t, c, s, 0:TR] = total[s, c * TR : (c + 1) * TR].astype(BF)
                kvg_ref[t, c, s, TR:BR] = total[s, LAT + c * CR : LAT + (c + 1) * CR].astype(BF)


def reduce_kernel(
    oq_ref,
    kvg_ref,
    w_ref,
    out_ref,
    gq_ref,
    gk_ref,
    gv_ref,
    gtk_ref,
    gtv_ref,
    z_in,
    z_sum,
    x_in,
    x_sum,
    yq_out,
    yq_in,
    yk_out,
    yk_in,
    keep_q,
    attn,
    part,
    core_in,
    pair_sum,
    relay,
    far_in,
    send_sem,
    recv_sem,
):
    seq, head, y, z, x = place()
    peer = peers(seq, head, y, z, x)
    zu, zd, zf = (z + 1) % NZ, (z + NZ - 1) % NZ, (z + 2) % NZ
    xr, xl, xf = (x + 1) % NX, (x + NX - 1) % NX, (x + 2) % NX
    other_head = (head + 2) % 4
    core_head = head + 1 - 2 * (head % 2)
    core_other = core_head + 2 - 4 * (core_head // 2)
    factor = HS ** (-0.5)
    first, second = pl.ds(0, HALF), pl.ds(HALF, HALF)
    sent = []
    send, arrived = sender(peer, send_sem, recv_sem, sent)
    by_y = lambda a, b: jnp.where(y == 0, a, b)
    cols = lambda h: slice(h * HS, (h + 1) * HS)
    wide = lambda a: a.astype(F32)

    greet(peer)

    def z_start(t):
        base = 6 * t
        send(base + 0, oq_ref.at[t, zf, :, first], z_in.at[t, 0], "up")
        send(base + 3, oq_ref.at[t, zf, :, second], z_in.at[t, 3], "down")
        send(base + 1, oq_ref.at[t, zd, :, first], z_in.at[t, 1], "down")
        send(base + 4, oq_ref.at[t, zu, :, second], z_in.at[t, 4], "up")

    def z_relay(t):
        base = 6 * t
        arrived(base + 0, z_in.at[t, 0])
        z_sum[t, 0] = (wide(z_in[t, 0]) + wide(oq_ref[t, zu, :, first])).astype(BF)
        send(base + 2, z_sum.at[t, 0], z_in.at[t, 2], "up")
        arrived(base + 3, z_in.at[t, 3])
        z_sum[t, 1] = (wide(z_in[t, 3]) + wide(oq_ref[t, zd, :, second])).astype(BF)
        send(base + 5, z_sum.at[t, 1], z_in.at[t, 5], "down")

    def z_total(t, scale):
        base = 6 * t
        for n in (1, 2, 4, 5):
            arrived(base + n, z_in.at[t, n])
        for h, rows, one, two in ((0, first, 1, 2), (1, second, 4, 5)):
            def total(j):
                value = wide(oq_ref[t, z, j, rows]) + wide(z_in[t, one, j]) + wide(z_in[t, two, j])
                return (value * scale).astype(BF) if scale != 1.0 else value.astype(BF)

            yq_out[t, rows] = total(1 - y)
            keep_q[t, 0, rows] = total(y)
            keep_q[t, 1, rows] = total(2)
        send(24 + t, yq_out.at[t], yq_in.at[t], "pair")

    def x_base(t, a):
        return 12 + 6 * t + 3 * a

    ring = (("right", "left"), ("left", "right"))
    ahead = ((xr, xl), (xl, xr))

    def x_start(t):
        for a in range(NY):
            send(x_base(t, a), kvg_ref.at[t, a * NX + xf], x_in.at[t, a, 0], ring[t][0])
        for a in range(NY):
            send(x_base(t, a) + 1, kvg_ref.at[t, a * NX + ahead[t][1]], x_in.at[t, a, 1], ring[t][1])

    def x_relay(t, a):
        arrived(x_base(t, a), x_in.at[t, a, 0])
        x_sum[t, a] = (wide(x_in[t, a, 0]) + wide(kvg_ref[t, a * NX + ahead[t][0]])).astype(BF)
        send(x_base(t, a) + 2, x_sum.at[t, a], x_in.at[t, a, 2], ring[t][0])

    def x_total(t, a):
        value = wide(kvg_ref[t, a * NX + x]) + wide(x_in[t, a, 1]) + wide(x_in[t, a, 2])
        return value * factor if t == 0 else value

    z_start(0)
    x_start(0)
    x_start(1)
    z_start(1)
    z_relay(0)
    for a in range(NY):
        for t in range(2):
            x_relay(t, a)
    z_total(0, 1.0)
    z_relay(1)
    arrived(24, yq_in.at[0])
    attn[:, cols(0)] = by_y(keep_q[0, 0], yq_in[0])
    attn[:, cols(1)] = by_y(yq_in[0], keep_q[0, 0])
    attn[:, cols(2)] = keep_q[0, 1]

    def project(n):
        return dot_nn(attn[...], w_ref[:, pl.ds(pl.multiple_of(n * 768, 128), 768)]).astype(BF)

    part[0] = project(core_other)
    send(28, part.at[0], core_in.at[0], "core")
    part[1] = project(core_head)
    send(29, part.at[1], core_in.at[1], "core")
    part[2] = project(other_head)
    arrived(28, core_in.at[0])
    pair_sum[...] = (wide(part[2]) + wide(core_in[0])).astype(BF)
    send(30, pair_sum.at[first], relay.at[0], "pair")
    send(31, pair_sum.at[second], relay.at[1], "back")
    part[3] = project(head)
    z_total(1, factor)
    for t in range(2):
        for a in range(NY):
            arrived(x_base(t, a) + 1, x_in.at[t, a, 1])
            arrived(x_base(t, a) + 2, x_in.at[t, a, 2])
        yk_out[t] = x_total(t, 1 - y).astype(BF)
        send(26 + t, yk_out.at[t], yk_in.at[t], "pair")
    arrived(30, relay.at[0])
    send(32, relay.at[0], far_in.at[first], "back")
    arrived(31, relay.at[1])
    send(33, relay.at[1], far_in.at[second], "pair")

    arrived(25, yq_in.at[1])
    gq_ref[:, cols(0)] = by_y(keep_q[1, 0], yq_in[1])
    gq_ref[:, cols(1)] = by_y(yq_in[1], keep_q[1, 0])
    gq_ref[:, cols(2)] = keep_q[1, 1]
    for t, (ref, text) in enumerate(((gk_ref, gtk_ref), (gv_ref, gtv_ref))):
        arrived(26 + t, yk_in.at[t])
        own = x_total(t, y)
        mine = own[0].astype(BF)
        other = yk_in[t, 0]
        both = (own[1] + wide(yk_in[t, 1])).astype(BF)
        for h, value in ((0, by_y(mine, other)), (1, by_y(other, mine)), (2, both)):
            ref[:, cols(h)] = value[0:TR]
            text[:, cols(h)] = value[TR:BR]
    arrived(29, core_in.at[1])
    arrived(32, far_in.at[first])
    arrived(33, far_in.at[second])
    out_ref[...] = (wide(part[3]) + wide(core_in[1]) + wide(far_in[...])).astype(BF)
    for copy in sent:
        copy.wait_send()


def shards(
    queries,
    keys,
    values,
    text_keys,
    text_values,
    head_bias,
    out_weight,
    grad_out,
    clip_lengths,
    tile_mask,
    caption_order,
):
    vmem = pl.BlockSpec(memory_space=pltpu.VMEM)
    smem = pl.BlockSpec(memory_space=pltpu.SMEM)
    anywhere = pl.BlockSpec(memory_space=pl.ANY)
    dma = pltpu.SemaphoreType.DMA
    qg_shape = (2, NZ, NH, TR, HS)
    kv_shape = (2, NY * NX, 2, BR, HS)
    out_cols = grad_out.shape[1]
    qg, kv = pl.pallas_call(
        gather_kernel,
        out_shape=(jax.ShapeDtypeStruct(qg_shape, BF), jax.ShapeDtypeStruct(kv_shape, BF)),
        in_specs=[vmem] * 7,
        out_specs=(anywhere, anywhere),
        scratch_shapes=[
            pltpu.VMEM((2, 2, BR, HS), BF),
            pltpu.VMEM((2, 2, BR, HS), BF),
            pltpu.VMEM((2, NH, TR, HS), BF),
            pltpu.VMEM((2, TR, HS), BF),
            pltpu.VMEM((4, TR, out_cols), BF),
            pltpu.VMEM((2, HALF, out_cols), BF),
            pltpu.VMEM((TR, NH * HS), F32),
            dma((34,)),
            dma((34,)),
            dma((4,)),
        ],
        compiler_params=pltpu.CompilerParams(
            collective_id=0, has_side_effects=True, vmem_limit_bytes=VMEM_LIMIT
        ),
    )(queries, keys, values, text_keys, text_values, grad_out, out_weight)

    oq, kvg = pl.pallas_call(
        attend_kernel,
        out_shape=(jax.ShapeDtypeStruct(qg_shape, BF), jax.ShapeDtypeStruct(kv_shape, BF)),
        in_specs=[vmem] * 4 + [smem] * 2,
        out_specs=(vmem, vmem),
        scratch_shapes=[
            pltpu.VMEM((2, ROWS, 2 * HS), BF),
            pltpu.VMEM((2, ROWS, HS), BF),
            pltpu.VMEM((TR, 2 * HS), BF),
            pltpu.VMEM((TR, HS), F32),
            pltpu.VMEM((TR, HS), F32),
            pltpu.VMEM((2, ROWS, HS), F32),
            pltpu.VMEM((2, ROWS, HS), F32),
        ],
        compiler_params=pltpu.CompilerParams(vmem_limit_bytes=VMEM_LIMIT),
    )(
        qg,
        kv,
        tile_mask,
        caption_order.reshape(CLIPS, CAP),
        clip_lengths,
        head_bias,
    )

    token_shape = jax.ShapeDtypeStruct((TR, NH * HS), BF)
    text_shape = jax.ShapeDtypeStruct((CR, NH * HS), BF)
    return pl.pallas_call(
        reduce_kernel,
        out_shape=(
            jax.ShapeDtypeStruct((TR, out_cols), BF),
            token_shape,
            token_shape,
            token_shape,
            text_shape,
            text_shape,
        ),
        in_specs=[vmem] * 3,
        out_specs=(vmem,) * 6,
        scratch_shapes=[
            pltpu.VMEM((2, 6, NH, HALF, HS), BF),
            pltpu.VMEM((2, 2, NH, HALF, HS), BF),
            pltpu.VMEM((2, NY, 3, 2, BR, HS), BF),
            pltpu.VMEM((2, NY, 2, BR, HS), BF),
            pltpu.VMEM((2, TR, HS), BF),
            pltpu.VMEM((2, TR, HS), BF),
            pltpu.VMEM((2, 2, BR, HS), BF),
            pltpu.VMEM((2, 2, BR, HS), BF),
            pltpu.VMEM((2, 2, TR, HS), BF),
            pltpu.VMEM((TR, NH * HS), BF),
            pltpu.VMEM((4, TR, out_cols), BF),
            pltpu.VMEM((2, TR, out_cols), BF),
            pltpu.VMEM((TR, out_cols), BF),
            pltpu.VMEM((2, HALF, out_cols), BF),
            pltpu.VMEM((TR, out_cols), BF),
            dma((34,)),
            dma((34,)),
        ],
        compiler_params=pltpu.CompilerParams(
            collective_id=1, has_side_effects=True, vmem_limit_bytes=VMEM_LIMIT
        ),
    )(oq, kvg, out_weight)


def solution(mesh):
    in_specs = (
        P("seq", "head"),
        P("seq", "head"),
        P("seq", "head"),
        P("seq", "head"),
        P("seq", "head"),
        P("head"),
        P("head", None),
        P("seq", "head"),
        P(),
        P(),
        P(),
    )
    out_specs = (P("seq", "head"),) * 6
    return jax.shard_map(shards, mesh=mesh, in_specs=in_specs, out_specs=out_specs, check_vma=False)
```

time: 735 us -> 117 us (0.16)
  waiting for transfers between devices: 398 us -> 0 us
  blocking collectives: 164 us -> 0 us
  matrix products: 125 us -> 0 us
  Pallas kernels: 0 us -> 105 us
  local copies, waits for them, and re-layouts: 28.6 us -> 10.5 us
  between operations: 14.3 us -> 0.71 us
    all_gather x5 -> x0, waiting for transfers between devices: 396 us -> none  [the longest x1 146 us: shards(): grad_piece = lax.all_gather(grad_attn, 'seq', axis=0, tiled=True)]
    all_gather x2 -> x0, blocking collectives: 164 us -> none  [the longest x1 85.3 us: shards(): lax.all_gather(text_values, 'seq', axis=0, tiled=True)]
    dot_general x16 -> x0, matrix products: 125 us -> none  [the longest x4 39 us: sigmoid_weights(): jnp.einsum('qhd,khd->hqk', query_heads, key_heads, preferred_element_type...]
    pallas_call x0 -> x3, Pallas kernels: none -> 105 us  [the longest x1 43.7 us: shards(): pl.pallas_call(reduce_kernel, out_shape=(jax.ShapeDtypeStruct((TR, out_co...]
    all_gather x4 -> x0, local copies, waits for them, and re-layouts: 18.4 us -> none  [the longest x1 8.62 us: shards(): value_piece = lax.all_gather(values, 'seq', axis=0, tiled=True)]
  transfers between devices with their start and end apart: 6 -> 0, of which waited for: 4 -> 0; matrix products, arithmetic and copies ran while one was open for 22% -> 0% of each run, Pallas kernels for 0% -> 0%
where the time goes in v1:
time: 117 us; the launch traced here: 116 us
  Pallas kernels  105 us (90%)
  local copies, waits for them, and re-layouts  10.5 us (9%)
    pallas_call x1, Pallas kernels, shards(): pl.pallas_call(reduce_kernel, out_shape=(jax.ShapeDtypeStruct((TR, out_co...  43.7 us
    pallas_call x1, Pallas kernels, shards(): pl.pallas_call(gather_kernel, out_shape=(jax.ShapeDtypeStruct(qg_shape, B...  38.6 us
    pallas_call x1, Pallas kernels, shards(): pl.pallas_call(attend_kernel, out_shape=(jax.ShapeDtypeStruct(qg_shape, B...  22.4 us
    unnamed x28, local copies, waits for them, and re-layouts  10.5 us

profile of v1, /device:TPU:0, one launch (start us, length us, event | category | flops | bytes accessed | tf_op | source)
XLA Modules:
  0.0 116.0 jit_solution(265929064054234794)
XLA Ops:
  0.6 0.0 copy-start.9
  0.6 0.0 copy-start.10
  0.7 0.0 copy-start.1
  0.7 1.0 copy-done.1
  1.7 0.9 copy-done.2
  2.6 0.9 copy-done.3
  3.5 0.9 copy-done.4
  4.4 0.7 copy-done.6
  5.2 0.7 copy-done.7
  5.9 38.6 %shard_map.154 = (bf16[2,4,3,256,128]{4,3,2,1,0:T(8,128)(2,1)S(1)}, bf16[2,8,2,272,128]{4,3,2,1,0:T(8,128)(2,1)S(1)}) custom-call(bf16[256,384]{1,0:T(8,128)(2,1)S(1)} %copy-done.2, bf16[256,384]{1,0:T(8,128)(2,1)S(1)} %copy-done.3, bf16[256,384]{1,0:T(8,128)(2,1)S(1)} %copy-done.4, bf16[16,384]{1,0:T(8,128)(2,1)S(1)} %copy-done.6, ...), custom_call_target="tpu_custom_call" | custom-call | tf_op jit(solution)/shard_map/pallas_call | solution.py:567
  44.5 0.0 copy-start
  44.5 1.4 %copy-done = bf16[2,8,2,272,128]{4,3,2,1,0:T(8,128)(2,1)} copy-done((bf16[2,8,2,272,128]{4,3,2,1,0:T(8,128)(2,1)}, bf16[2,8,2,272,128]{4,3,2,1,0:T(8,128)(2,1)S(1)}, u32[]{:S(2)}) %copy-start) | copy-done | bytes 2228248
  45.8 0.0 copy-done.9
  45.8 0.0 copy-done.10
  45.8 0.0 copy-done.5
  45.8 0.0 copy-done.8
  45.8 22.4 %shard_map.155 = (bf16[2,4,3,256,128]{4,3,2,1,0:T(8,128)(2,1)S(1)}, bf16[2,8,2,272,128]{4,3,2,1,0:T(8,128)(2,1)S(1)}) custom-call(bf16[2,4,3,256,128]{4,3,2,1,0:T(8,128)(2,1)S(1)} %get-tuple-element.10.qg_ref, bf16[2,8,2,272,128]{4,3,2,1,0:T(8,128)(2,1)} %copy-done, s32[128,128]{1,0:T(8,128)S(1)} %copy-done.5, s32[4,128]{1,0:T(4,128)S(1)} %bitcast.1, ...), custom_call_target="tpu_custom_call" | custom-call | tf_op jit(solution)/shard_map/pallas_call | solution.py:589
  68.3 43.7 %shard_map.156 = (bf16[256,768]{1,0:T(8,128)(2,1)S(1)}, bf16[256,384]{1,0:T(8,128)(2,1)S(1)}, bf16[256,384]{1,0:T(8,128)(2,1)S(1)}, bf16[256,384]{1,0:T(8,128)(2...) custom-call(bf16[2,4,3,256,128]{4,3,2,1,0:T(8,128)(2,1)S(1)} %get-tuple-element.12.oq_ref, ...), custom_call_target="tpu_custom_call" | custom-call | tf_op jit(solution)/shard_map/pallas_call | solution.py:615
  112.0 0.7 copy.23
  112.7 0.7 copy.24
  113.4 0.7 copy.25
  114.1 0.7 copy.26
  114.8 0.6 copy.27
  115.4 0.6 copy.28
  (7 shorter events, 0.0 us)
Async XLA Ops:
  0.6 45.2 %copy-start.9 = (s32[4]{0:T(128)S(1)}, s32[4]{0:T(128)}, u32[]{:S(2)}) copy-start(s32[4]{0:T(128)} %len_ref.1) | copy-start | bytes 52
  0.6 45.2 %copy-start.10 = (f32[3]{0:T(128)S(1)}, f32[3]{0:T(128)}, u32[]{:S(2)}) copy-start(f32[3]{0:T(128)} %bias_ref.1) | copy-start | bytes 40
  0.7 1.0 copy-start.1
  1.7 0.9 copy-start.2
  2.6 0.9 copy-start.3
  3.5 0.9 copy-start.4
  4.4 0.7 copy-start.6
  5.2 0.7 copy-start.7
  5.9 40.0 %copy-start.5 = (s32[128,128]{1,0:T(8,128)S(1)}, s32[128,128]{1,0:T(8,128)}, u32[]{:S(2)}) copy-start(s32[128,128]{1,0:T(8,128)} %tile_ref.1) | copy-start | bytes 196612
  5.9 40.0 %copy-start.8 = (s32[512]{0:T(512)S(1)}, s32[512]{0:T(512)}, u32[]{:S(2)}) copy-start(s32[512]{0:T(512)} %param.21) | copy-start | bytes 6148
  44.5 1.4 %copy-start = (bf16[2,8,2,272,128]{4,3,2,1,0:T(8,128)(2,1)}, bf16[2,8,2,272,128]{4,3,2,1,0:T(8,128)(2,1)S(1)}, u32[]{:S(2)}) copy-start(bf16[2,8,2,272,128]{4,3,2,1,0:T(8,128)(2,1)S(1)} %get-tuple-element.11.kv_ref) | copy-start | bytes 6684676

commit v2 on v1

--- a/solution.py
+++ b/solution.py
@@ -1,5 +1,3 @@
-import functools
-
 import jax
 import jax.numpy as jnp
 from jax import lax
@@ -24,7 +22,7 @@
 LAT = NY * NX * TR
 ROWS = NY * NX * BR
 MASKED = -32768.0
-VMEM_LIMIT = 48 * 1024 * 1024
+VMEM_LIMIT = 24 * 1024 * 1024
 
 
 def place():
@@ -94,11 +92,18 @@
     return lax.dot_general(a, b, (((1,), (0,)), ((), ())), preferred_element_type=F32)
 
 
-def dot_tn(a, b):
-    return lax.dot_general(a, b, (((0,), (0,)), ((), ())), preferred_element_type=F32)
-
-
 def gather_kernel(
+    q_hbm,
+    k_hbm,
+    v_hbm,
+    tk_hbm,
+    tv_hbm,
+    go_hbm,
+    w_hbm,
+    qg_hbm,
+    kv_hbm,
+    qg_ref,
+    kv_ref,
     q_ref,
     k_ref,
     v_ref,
@@ -106,11 +111,7 @@
     tv_ref,
     go_ref,
     w_ref,
-    qg_ref,
-    kv_ref,
-    st_own,
     st_pair,
-    qz,
     q_pair,
     goall,
     relay,
@@ -121,128 +122,178 @@
 ):
     seq, head, y, z, x = place()
     peer = peers(seq, head, y, z, x)
-    zu, zd = (z + 1) % NZ, (z + NZ - 1) % NZ
-    xr, xl = (x + 1) % NX, (x + NX - 1) % NX
+    zu, zd, zf = (z + 1) % NZ, (z + NZ - 1) % NZ, (z + 2) % NZ
+    xr, xl, xf = (x + 1) % NX, (x + NX - 1) % NX, (x + 2) % NX
     other_head = (head + 2) % 4
     core_head = head + 1 - 2 * (head % 2)
+    core_other = core_head + 2 - 4 * (core_head // 2)
     first, second = pl.ds(0, HALF), pl.ds(HALF, HALF)
     sent = []
     send, arrived = sender(peer, send_sem, recv_sem, sent)
     cols = lambda h: slice(h * HS, (h + 1) * HS)
     by_y = lambda a, b: jnp.where(y == 0, a, b)
 
+    load = []
+    for n, (src, dst) in enumerate(
+        (
+            (k_hbm, k_ref),
+            (tk_hbm, tk_ref),
+            (v_hbm, v_ref),
+            (tv_hbm, tv_ref),
+            (q_hbm, q_ref),
+            (go_hbm, go_ref),
+            (w_hbm, w_ref),
+        )
+    ):
+        copy = pltpu.make_async_copy(src, dst, local_sem.at[n])
+        copy.start()
+        load.append(copy)
+
     greet(peer)
 
-    send(0, go_ref.at[first], relay.at[0], "pair")
-    send(1, go_ref.at[second], relay.at[1], "back")
-    send(2, go_ref, goall.at[head], "core")
-
+    send(0, go_hbm.at[first], relay.at[0], "pair")
+    send(1, go_hbm.at[second], relay.at[1], "back")
+    send(2, go_hbm, goall.at[head], "core")
+
+    stores = []
+
+    def store(src, dst):
+        copy = pltpu.make_async_copy(src, dst, local_sem.at[7 + len(stores)])
+        copy.start()
+        stores.append(copy)
+
+    def x_send(a, t, yy):
+        c = yy * NX + x
+        send(10 + 6 * a + 2 * t, kv_ref.at[t, c], kv_ref.at[t, c], ("right", "left")[t])
+        send(11 + 6 * a + 2 * t, kv_ref.at[t, c], kv_ref.at[t, c], ("left", "right")[t])
+
+    def x_forward(a, yy):
+        base = 10 + 6 * a
+        left, right = yy * NX + xl, yy * NX + xr
+        arrived(base + 0, kv_ref.at[0, left])
+        send(base + 4, kv_ref.at[0, left], kv_ref.at[0, left], "right")
+        arrived(base + 2, kv_ref.at[1, right])
+        send(base + 5, kv_ref.at[1, right], kv_ref.at[1, right], "left")
+
+    def x_finish(a, yy):
+        base = 10 + 6 * a
+        arrived(base + 1, kv_ref.at[0, yy * NX + xr])
+        arrived(base + 3, kv_ref.at[1, yy * NX + xl])
+        arrived(base + 4, kv_ref.at[0, yy * NX + xf])
+        arrived(base + 5, kv_ref.at[1, yy * NX + xf])
+
+    def z_own(t):
+        base = 22 + 10 * t
+        send(base + 0, qg_ref.at[t, z, 2], qg_ref.at[t, z, 2], "up")
+        send(base + 1, qg_ref.at[t, z, y], qg_ref.at[t, z, y], "down")
+        send(base + 2, qg_ref.at[t, z, y], qg_ref.at[t, z, y], "up")
+        send(base + 3, qg_ref.at[t, z, 2], qg_ref.at[t, z, 2], "down")
+
+    def z_own_forward(t):
+        base = 22 + 10 * t
+        arrived(base + 0, qg_ref.at[t, zd, 2])
+        send(base + 4, qg_ref.at[t, zd, 2], qg_ref.at[t, zd, 2], "up")
+        arrived(base + 1, qg_ref.at[t, zu, y])
+        send(base + 5, qg_ref.at[t, zu, y], qg_ref.at[t, zu, y], "down")
+
+    def z_pair(t):
+        base = 22 + 10 * t
+        send(base + 6, qg_ref.at[t, z, 1 - y], qg_ref.at[t, z, 1 - y], "up")
+        send(base + 7, qg_ref.at[t, z, 1 - y], qg_ref.at[t, z, 1 - y], "down")
+
+    def z_pair_forward(t):
+        base = 22 + 10 * t
+        arrived(base + 6, qg_ref.at[t, zd, 1 - y])
+        src = qg_ref.at[t, zd, 1 - y, first]
+        send(base + 8, src, src, "up")
+        arrived(base + 7, qg_ref.at[t, zu, 1 - y])
+        src = qg_ref.at[t, zu, 1 - y, second]
+        send(base + 9, src, src, "down")
+
+    def z_finish(t):
+        base = 22 + 10 * t
+        arrived(base + 2, qg_ref.at[t, zd, y])
+        arrived(base + 3, qg_ref.at[t, zu, 2])
+        arrived(base + 4, qg_ref.at[t, zf, 2])
+        arrived(base + 5, qg_ref.at[t, zf, y])
+        arrived(base + 8, qg_ref.at[t, zf, 1 - y, first])
+        arrived(base + 9, qg_ref.at[t, zf, 1 - y, second])
+
+    def feature(n):
+        return w_ref[:, pl.ds(pl.multiple_of(n * 768, 128), 768)]
+
+    c = y * NX + x
     for t, (ref, text) in enumerate(((k_ref, tk_ref), (v_ref, tv_ref))):
-        st_own[t, 0, 0:TR] = by_y(ref[:, cols(0)], ref[:, cols(1)])
-        st_own[t, 0, TR:BR] = by_y(text[:, cols(0)], text[:, cols(1)])
-        st_own[t, 1, 0:TR] = ref[:, cols(2)]
-        st_own[t, 1, TR:BR] = text[:, cols(2)]
-        c = y * NX + x
-        send(10 + 2 * t, st_own.at[t], kv_ref.at[t, c], "right")
-        send(11 + 2 * t, st_own.at[t], kv_ref.at[t, c], "left")
+        load[2 * t].wait()
+        load[2 * t + 1].wait()
+        kv_ref[t, c, 0, 0:TR] = by_y(ref[:, cols(0)], ref[:, cols(1)])
+        kv_ref[t, c, 0, TR:BR] = by_y(text[:, cols(0)], text[:, cols(1)])
+        kv_ref[t, c, 1, 0:TR] = ref[:, cols(2)]
+        kv_ref[t, c, 1, TR:BR] = text[:, cols(2)]
+        x_send(0, t, y)
+    load[4].wait()
+    qg_ref[0, z, y] = by_y(q_ref[:, cols(0)], q_ref[:, cols(1)])
+    qg_ref[0, z, 2] = q_ref[:, cols(2)]
+    z_own(0)
+    q_pair[0] = by_y(q_ref[:, cols(1)], q_ref[:, cols(0)])
+    for t, (ref, text) in enumerate(((k_ref, tk_ref), (v_ref, tv_ref))):
         st_pair[t, 0, 0:TR] = by_y(ref[:, cols(1)], ref[:, cols(0)])
         st_pair[t, 0, TR:BR] = by_y(text[:, cols(1)], text[:, cols(0)])
         st_pair[t, 1, 0:TR] = ref[:, cols(2)]
         st_pair[t, 1, TR:BR] = text[:, cols(2)]
-    qz[0, y] = by_y(q_ref[:, cols(0)], q_ref[:, cols(1)])
-    qz[0, 2] = q_ref[:, cols(2)]
-    q_pair[0] = by_y(q_ref[:, cols(1)], q_ref[:, cols(0)])
-    own = []
-    for t in range(2):
-        copy = pltpu.make_async_copy(st_own.at[t], kv_ref.at[t, y * NX + x], local_sem.at[t])
-        copy.start()
-        own.append(copy)
-
-    def z_send(t):
-        base = 22 + 6 * t
-        send(base + 0, qz.at[t, :, first], qg_ref.at[t, z, :, first], "up")
-        send(base + 3, qz.at[t, :, second], qg_ref.at[t, z, :, second], "down")
-        send(base + 1, qz.at[t, :, first], qg_ref.at[t, z, :, first], "down")
-        send(base + 2, qz.at[t, :, second], qg_ref.at[t, z, :, second], "up")
-        copy = pltpu.make_async_copy(qz.at[t], qg_ref.at[t, z], local_sem.at[2 + t])
-        copy.start()
-        own.append(copy)
-
-    def z_forward(t):
-        base = 22 + 6 * t
-        arrived(base + 0, qg_ref.at[t, zd, :, first])
-        send(base + 4, qg_ref.at[t, zd, :, first], qg_ref.at[t, zd, :, first], "up")
-        arrived(base + 3, qg_ref.at[t, zu, :, second])
-        send(base + 5, qg_ref.at[t, zu, :, second], qg_ref.at[t, zu, :, second], "down")
-
-    def z_finish(t):
-        base = 22 + 6 * t
-        far = (z + 2) % NZ
-        arrived(base + 1, qg_ref.at[t, zu, :, first])
-        arrived(base + 2, qg_ref.at[t, zd, :, second])
-        arrived(base + 4, qg_ref.at[t, far, :, first])
-        arrived(base + 5, qg_ref.at[t, far, :, second])
-
-    def x_forward(a, yy):
-        base = 10 + 6 * a
-        arrived(base + 0, kv_ref.at[0, yy * NX + xl])
-        send(base + 4, kv_ref.at[0, yy * NX + xl], kv_ref.at[0, yy * NX + xl], "right")
-        arrived(base + 3, kv_ref.at[1, yy * NX + xr])
-        send(base + 5, kv_ref.at[1, yy * NX + xr], kv_ref.at[1, yy * NX + xr], "left")
-
-    def x_finish(a, yy):
-        base = 10 + 6 * a
-        far = yy * NX + (x + 2) % NX
-        arrived(base + 1, kv_ref.at[0, yy * NX + xr])
-        arrived(base + 2, kv_ref.at[1, yy * NX + xl])
-        arrived(base + 4, kv_ref.at[0, far])
-        arrived(base + 5, kv_ref.at[1, far])
-
-    def feature(n):
-        return w_ref[:, pl.ds(pl.multiple_of(n * 768, 128), 768)]
-
+    load[5].wait()
+    load[6].wait()
     acc[...] = dot_nt(go_ref[...], feature(head))
+
     arrived(0, relay.at[0])
     send(3, relay.at[0], goall.at[head, first], "back")
     arrived(1, relay.at[1])
     send(4, relay.at[1], goall.at[other_head, second], "pair")
-    send(6, q_pair.at[0], qz.at[0, y], "pair")
-    for t in range(2):
-        send(7 + t, st_pair.at[t], kv_ref.at[t, y * NX + x], "pair")
+    send(6, q_pair.at[0], qg_ref.at[0, z, y], "pair")
+    z_own_forward(0)
+    x_forward(0, y)
     arrived(2, goall.at[core_head])
     acc[...] += dot_nt(goall[core_head], feature(core_head))
-    x_forward(0, y)
     arrived(3, goall.at[other_head, first])
     arrived(4, goall.at[other_head, second])
     send(5, goall.at[other_head], goall.at[other_head], "core")
+    for t in range(2):
+        send(7 + t, st_pair.at[t], kv_ref.at[t, c], "pair")
     acc[...] += dot_nt(goall[other_head], feature(other_head))
-    arrived(6, qz.at[0, 1 - y])
-    z_send(0)
-    last = core_head + 2 - 4 * (core_head // 2)
-    arrived(5, goall.at[last])
-    grad = (acc[...] + dot_nt(goall[last], feature(last))).astype(BF)
+    arrived(6, qg_ref.at[0, z, 1 - y])
+    z_pair(0)
+    arrived(5, goall.at[core_other])
+    grad = (acc[...] + dot_nt(goall[core_other], feature(core_other))).astype(BF)
     q_pair[1] = by_y(grad[:, cols(1)], grad[:, cols(0)])
-    send(9, q_pair.at[1], qz.at[1, y], "pair")
-    qz[1, y] = by_y(grad[:, cols(0)], grad[:, cols(1)])
-    qz[1, 2] = grad[:, cols(2)]
-    for t in range(2):
-        c = (1 - y) * NX + x
-        arrived(7 + t, kv_ref.at[t, c])
-        send(16 + 2 * t, kv_ref.at[t, c], kv_ref.at[t, c], "right")
-        send(17 + 2 * t, kv_ref.at[t, c], kv_ref.at[t, c], "left")
-    arrived(9, qz.at[1, 1 - y])
-    z_send(1)
-    z_forward(0)
-    z_forward(1)
+    send(9, q_pair.at[1], qg_ref.at[1, z, y], "pair")
+    qg_ref[1, z, y] = by_y(grad[:, cols(0)], grad[:, cols(1)])
+    qg_ref[1, z, 2] = grad[:, cols(2)]
+    z_own(1)
+    z_pair_forward(0)
+    arrived(9, qg_ref.at[1, z, 1 - y])
+    z_pair(1)
+    for t in range(2):
+        arrived(7 + t, kv_ref.at[t, (1 - y) * NX + x])
+        x_send(1, t, 1 - y)
+    z_own_forward(1)
+    z_pair_forward(1)
+    x_finish(0, y)
+    plane = pl.ds(y * NX, NX)
+    for t in range(2):
+        store(kv_ref.at[t, plane], kv_hbm.at[t, plane])
     x_forward(1, 1 - y)
     z_finish(0)
+    store(qg_ref.at[0], qg_hbm.at[0])
     z_finish(1)
-    x_finish(0, y)
+    store(qg_ref.at[1], qg_hbm.at[1])
     x_finish(1, 1 - y)
-    for copy in own:
-        copy.wait()
+    plane = pl.ds((1 - y) * NX, NX)
+    for t in range(2):
+        store(kv_ref.at[t, plane], kv_hbm.at[t, plane])
     for copy in sent:
         copy.wait_send()
+    for copy in stores:
+        copy.wait()
 
 
 def attend_kernel(
@@ -261,6 +312,8 @@
     qacc,
     kacc,
     vacc,
+    queries_t,
+    grads_t,
 ):
     seq, head, y, z, x = place()
     factor = HS ** (-0.5)
@@ -338,12 +391,15 @@
             off = (tile_ref[pl.ds(tile, 1), :] == 0) & (lane != tile) & tiles_here
             rows = slice(u * TILE, (u + 1) * TILE)
             qaug[rows, HS:] = jnp.where(off, MASKED, side[rows]).astype(BF)
-        qaug[:, 0:HS] = qg_ref[0, zq, j]
+        queries = qg_ref[0, zq, j]
+        grads = qg_ref[1, zq, j]
+        qaug[:, 0:HS] = queries
+        queries_t[...] = queries.T
+        grads_t[...] = grads.T
 
         def block(first_row, count, fresh):
             rows = pl.ds(first_row, count)
             keys = kaug[slot, rows, :]
-            queries = qaug[:, 0:HS]
             grads = qg_ref[1, zq, j]
             scores = dot_nt(qaug[...], keys)
             e = jnp.exp2(jnp.minimum(scores * (factor * log2e), 115.0))
@@ -360,8 +416,8 @@
             else:
                 oacc[...] += o_part
                 qacc[...] += q_part
-            vacc[slot, rows, :] += dot_tn(weight, grads)
-            kacc[slot, rows, :] += dot_tn(slope, queries)
+            vacc[slot, :, rows] += dot_nn(grads_t[...], weight)
+            kacc[slot, :, rows] += dot_nn(queries_t[...], slope)
 
         block(LAT, NY * NX * CR, True)
         q_low, q_high = clip_at(start), clip_at(start + TR - 1)
@@ -383,14 +439,17 @@
     for t, total in enumerate((kacc, vacc)):
         for c in range(NY * NX):
             for s in range(2):
-                kvg_ref[t, c, s, 0:TR] = total[s, c * TR : (c + 1) * TR].astype(BF)
-                kvg_ref[t, c, s, TR:BR] = total[s, LAT + c * CR : LAT + (c + 1) * CR].astype(BF)
+                kvg_ref[t, c, s, 0:TR] = total[s, :, c * TR : (c + 1) * TR].astype(BF).T
+        for s in range(2):
+            text_rows = total[s, :, LAT:].astype(BF).T
+            for c in range(NY * NX):
+                kvg_ref[t, c, s, TR:BR] = text_rows[c * CR : (c + 1) * CR]
 
 
 def reduce_kernel(
     oq_ref,
     kvg_ref,
-    w_ref,
+    w_hbm,
     out_ref,
     gq_ref,
     gk_ref,
@@ -412,8 +471,10 @@
     pair_sum,
     relay,
     far_in,
+    w_ref,
     send_sem,
     recv_sem,
+    load_sem,
 ):
     seq, head, y, z, x = place()
     peer = peers(seq, head, y, z, x)
@@ -429,6 +490,8 @@
     by_y = lambda a, b: jnp.where(y == 0, a, b)
     cols = lambda h: slice(h * HS, (h + 1) * HS)
     wide = lambda a: a.astype(F32)
+    load = pltpu.make_async_copy(w_hbm, w_ref, load_sem.at[0])
+    load.start()
 
     greet(peer)
 
@@ -468,11 +531,11 @@
     ring = (("right", "left"), ("left", "right"))
     ahead = ((xr, xl), (xl, xr))
 
-    def x_start(t):
-        for a in range(NY):
-            send(x_base(t, a), kvg_ref.at[t, a * NX + xf], x_in.at[t, a, 0], ring[t][0])
-        for a in range(NY):
-            send(x_base(t, a) + 1, kvg_ref.at[t, a * NX + ahead[t][1]], x_in.at[t, a, 1], ring[t][1])
+    def x_far(t, a):
+        send(x_base(t, a), kvg_ref.at[t, a * NX + xf], x_in.at[t, a, 0], ring[t][0])
+
+    def x_near(t, a):
+        send(x_base(t, a) + 1, kvg_ref.at[t, a * NX + ahead[t][1]], x_in.at[t, a, 1], ring[t][1])
 
     def x_relay(t, a):
         arrived(x_base(t, a), x_in.at[t, a, 0])
@@ -484,19 +547,21 @@
         return value * factor if t == 0 else value
 
     z_start(0)
-    x_start(0)
-    x_start(1)
+    for t in range(2):
+        x_far(t, 1 - y)
+    z_relay(0)
+    for t in range(2):
+        x_relay(t, 1 - y)
+        x_near(t, 1 - y)
+    z_total(0, 1.0)
     z_start(1)
-    z_relay(0)
-    for a in range(NY):
-        for t in range(2):
-            x_relay(t, a)
-    z_total(0, 1.0)
-    z_relay(1)
+    for t in range(2):
+        x_far(t, y)
     arrived(24, yq_in.at[0])
     attn[:, cols(0)] = by_y(keep_q[0, 0], yq_in[0])
     attn[:, cols(1)] = by_y(yq_in[0], keep_q[0, 0])
     attn[:, cols(2)] = keep_q[0, 1]
+    load.wait()
 
     def project(n):
         return dot_nn(attn[...], w_ref[:, pl.ds(pl.multiple_of(n * 768, 128), 768)]).astype(BF)
@@ -510,18 +575,24 @@
     pair_sum[...] = (wide(part[2]) + wide(core_in[0])).astype(BF)
     send(30, pair_sum.at[first], relay.at[0], "pair")
     send(31, pair_sum.at[second], relay.at[1], "back")
-    part[3] = project(head)
-    z_total(1, factor)
-    for t in range(2):
-        for a in range(NY):
-            arrived(x_base(t, a) + 1, x_in.at[t, a, 1])
-            arrived(x_base(t, a) + 2, x_in.at[t, a, 2])
+    z_relay(1)
+    for t in range(2):
+        arrived(x_base(t, 1 - y) + 1, x_in.at[t, 1 - y, 1])
+        arrived(x_base(t, 1 - y) + 2, x_in.at[t, 1 - y, 2])
         yk_out[t] = x_total(t, 1 - y).astype(BF)
         send(26 + t, yk_out.at[t], yk_in.at[t], "pair")
+    for t in range(2):
+        x_relay(t, y)
+        x_near(t, y)
+    part[3] = project(head)
     arrived(30, relay.at[0])
     send(32, relay.at[0], far_in.at[first], "back")
     arrived(31, relay.at[1])
     send(33, relay.at[1], far_in.at[second], "pair")
+    z_total(1, factor)
+    for t in range(2):
+        arrived(x_base(t, y) + 1, x_in.at[t, y, 1])
+        arrived(x_base(t, y) + 2, x_in.at[t, y, 2])
 
     arrived(25, yq_in.at[1])
     gq_ref[:, cols(0)] = by_y(keep_q[1, 0], yq_in[1])
@@ -544,6 +615,18 @@
         copy.wait_send()
 
 
+def store_kernel(*refs):
+    count = len(refs) // 2
+    sems = refs[-1]
+    copies = [
+        pltpu.make_async_copy(refs[n], refs[count + n], sems.at[n]) for n in range(count)
+    ]
+    for copy in copies:
+        copy.start()
+    for copy in copies:
+        copy.wait()
+
+
 def shards(
     queries,
     keys,
@@ -559,7 +642,7 @@
 ):
     vmem = pl.BlockSpec(memory_space=pltpu.VMEM)
     smem = pl.BlockSpec(memory_space=pltpu.SMEM)
-    anywhere = pl.BlockSpec(memory_space=pl.ANY)
+    hbm = pl.BlockSpec(memory_space=pltpu.HBM)
     dma = pltpu.SemaphoreType.DMA
     qg_shape = (2, NZ, NH, TR, HS)
     kv_shape = (2, NY * NX, 2, BR, HS)
@@ -567,22 +650,29 @@
     qg, kv = pl.pallas_call(
         gather_kernel,
         out_shape=(jax.ShapeDtypeStruct(qg_shape, BF), jax.ShapeDtypeStruct(kv_shape, BF)),
-        in_specs=[vmem] * 7,
-        out_specs=(anywhere, anywhere),
+        in_specs=[hbm] * 7,
+        out_specs=(hbm, hbm),
         scratch_shapes=[
+            pltpu.VMEM(qg_shape, BF),
+            pltpu.VMEM(kv_shape, BF),
+            pltpu.VMEM((TR, NH * HS), BF),
+            pltpu.VMEM((TR, NH * HS), BF),
+            pltpu.VMEM((TR, NH * HS), BF),
+            pltpu.VMEM((CR, NH * HS), BF),
+            pltpu.VMEM((CR, NH * HS), BF),
+            pltpu.VMEM((TR, out_cols), BF),
+            pltpu.VMEM(out_weight.shape, BF),
             pltpu.VMEM((2, 2, BR, HS), BF),
-            pltpu.VMEM((2, 2, BR, HS), BF),
-            pltpu.VMEM((2, NH, TR, HS), BF),
             pltpu.VMEM((2, TR, HS), BF),
             pltpu.VMEM((4, TR, out_cols), BF),
             pltpu.VMEM((2, HALF, out_cols), BF),
             pltpu.VMEM((TR, NH * HS), F32),
-            dma((34,)),
-            dma((34,)),
-            dma((4,)),
+            dma((42,)),
+            dma((42,)),
+            dma((13,)),
         ],
         compiler_params=pltpu.CompilerParams(
-            collective_id=0, has_side_effects=True, vmem_limit_bytes=VMEM_LIMIT
+            collective_id=0, has_side_effects=True, vmem_limit_bytes=56 * 1024 * 1024
         ),
     )(queries, keys, values, text_keys, text_values, grad_out, out_weight)
 
@@ -597,8 +687,10 @@
             pltpu.VMEM((TR, 2 * HS), BF),
             pltpu.VMEM((TR, HS), F32),
             pltpu.VMEM((TR, HS), F32),
-            pltpu.VMEM((2, ROWS, HS), F32),
-            pltpu.VMEM((2, ROWS, HS), F32),
+            pltpu.VMEM((2, HS, ROWS), F32),
+            pltpu.VMEM((2, HS, ROWS), F32),
+            pltpu.VMEM((HS, TR), BF),
+            pltpu.VMEM((HS, TR), BF),
         ],
         compiler_params=pltpu.CompilerParams(vmem_limit_bytes=VMEM_LIMIT),
     )(
@@ -612,17 +704,18 @@
 
     token_shape = jax.ShapeDtypeStruct((TR, NH * HS), BF)
     text_shape = jax.ShapeDtypeStruct((CR, NH * HS), BF)
-    return pl.pallas_call(
+    result = (
+        jax.ShapeDtypeStruct((TR, out_cols), BF),
+        token_shape,
+        token_shape,
+        token_shape,
+        text_shape,
+        text_shape,
+    )
+    held = pl.pallas_call(
         reduce_kernel,
-        out_shape=(
-            jax.ShapeDtypeStruct((TR, out_cols), BF),
-            token_shape,
-            token_shape,
-            token_shape,
-            text_shape,
-            text_shape,
-        ),
-        in_specs=[vmem] * 3,
+        out_shape=result,
+        in_specs=[vmem, vmem, hbm],
         out_specs=(vmem,) * 6,
         scratch_shapes=[
             pltpu.VMEM((2, 6, NH, HALF, HS), BF),
@@ -640,13 +733,22 @@
             pltpu.VMEM((TR, out_cols), BF),
             pltpu.VMEM((2, HALF, out_cols), BF),
             pltpu.VMEM((TR, out_cols), BF),
+            pltpu.VMEM(out_weight.shape, BF),
             dma((34,)),
             dma((34,)),
+            dma((1,)),
         ],
         compiler_params=pltpu.CompilerParams(
             collective_id=1, has_side_effects=True, vmem_limit_bytes=VMEM_LIMIT
         ),
     )(oq, kvg, out_weight)
+    return pl.pallas_call(
+        store_kernel,
+        out_shape=result,
+        in_specs=[vmem] * len(result),
+        out_specs=(hbm,) * len(result),
+        scratch_shapes=[dma((len(result),))],
+    )(*held)
 
 
 def solution(mesh):

time: 117 us -> 113 us (0.966)
  local copies, waits for them, and re-layouts: 10.5 us -> 7.16 us
  Pallas kernels: 105 us -> 103 us
    pallas_call x1 -> x2, Pallas kernels: 43.7 us -> 38.8 us  [the longest x1 36.6 us: shards(): pl.pallas_call(reduce_kernel, out_shape=result, in_specs=[vmem, vmem, hbm...]
    unnamed x28 -> x26, local copies, waits for them, and re-layouts: 10.5 us -> 7.16 us
    pallas_call x1, Pallas kernels: 22.4 us -> 25.4 us  [shards(): pl.pallas_call(attend_kernel, out_shape=(jax.ShapeDtypeStruct(qg_shape, B...]
where the time goes in v2:
time: 113 us; the launch traced here: 111 us
  Pallas kernels  103 us (91%)
  local copies, waits for them, and re-layouts  7.16 us (6%)
    pallas_call x1, Pallas kernels, shards(): pl.pallas_call(gather_kernel, out_shape=(jax.ShapeDtypeStruct(qg_shape, B...  38.8 us
    pallas_call x1, Pallas kernels, shards(): pl.pallas_call(reduce_kernel, out_shape=result, in_specs=[vmem, vmem, hbm...  36.6 us
    pallas_call x1, Pallas kernels, shards(): pl.pallas_call(attend_kernel, out_shape=(jax.ShapeDtypeStruct(qg_shape, B...  25.4 us
    unnamed x26, local copies, waits for them, and re-layouts  7.16 us

profile of v2, /device:TPU:0, one launch (start us, length us, event | category | flops | bytes accessed | tf_op | source)
XLA Modules:
  0.0 110.9 jit_solution(12395997148480787623)
XLA Ops:
  0.6 0.0 copy-start.10
  0.6 0.0 copy-start.7
  0.7 0.0 copy-start.11
  0.7 0.0 copy-start.12
  0.7 38.8 %shard_map.154 = (bf16[2,4,3,256,128]{4,3,2,1,0:T(8,128)(2,1)}, bf16[2,8,2,272,128]{4,3,2,1,0:T(8,128)(2,1)}) custom-call(bf16[256,384]{1,0:T(8,128)(2,1)} %q_hbm.1, bf16[256,384]{1,0:T(8,128)(2,1)} %k_hbm.1, bf16[256,384]{1,0:T(8,128)(2,1)} %v_hbm.1, bf16[16,384]{1,0:T(8,128)(2,1)} %tk_hbm.1, bf16[16,384]{1,0:T(8,128)(2,1)} %tv_hbm.1, ...), custom_call_target="tpu_custom_call" | custom-call | tf_op jit(solution)/shard_map/pallas_call | solution.py:650
  39.5 0.0 copy-start
  39.5 0.0 copy-done.10
  39.5 0.0 copy-done.7
  39.6 0.0 copy-done.11
  39.6 0.0 copy-done.12
  39.6 0.0 copy-start.1
  39.6 1.8 %copy-done.1 = bf16[2,8,2,272,128]{4,3,2,1,0:T(8,128)(2,1)S(1)} copy-done((bf16[2,8,2,272,128]{4,3,2,1,0:T(8,128)(2,1)S(1)}, bf16[2,8,2,272,128]{4,3,2,1,0:T(8,128)(2,1)}, u32[]{:S(2)}) %copy-start.1) | copy-done | bytes 2228248
  41.4 1.4 %copy-done.2 = bf16[2,4,3,256,128]{4,3,2,1,0:T(8,128)(2,1)S(1)} copy-done((bf16[2,4,3,256,128]{4,3,2,1,0:T(8,128)(2,1)S(1)}, bf16[2,4,3,256,128]{4,3,2,1,0:T(8,128)(2,1)}, u32[]{:S(2)}) %copy-start.2) | copy-done | bytes 1572888
  42.8 25.4 %shard_map.155 = (bf16[2,4,3,256,128]{4,3,2,1,0:T(8,128)(2,1)S(1)}, bf16[2,8,2,272,128]{4,3,2,1,0:T(8,128)(2,1)S(1)}) custom-call(bf16[2,4,3,256,128]{4,3,2,1,0:T(8,128)(2,1)S(1)} %copy-done.2, bf16[2,8,2,272,128]{4,3,2,1,0:T(8,128)(2,1)S(1)} %copy-done.1, s32[128,128]{1,0:T(8,128)S(1)} %copy-done.7, s32[4,128]{1,0:T(4,128)S(1)} %bitcast.1, ...), custom_call_target="tpu_custom_call" | custom-call | tf_op jit(solution)/shard_map/pallas_call | solution.py:679
  68.2 0.0 copy-done
  68.2 36.6 %shard_map.156 = (bf16[256,768]{1,0:T(8,128)(2,1)S(1)}, bf16[256,384]{1,0:T(8,128)(2,1)S(1)}, bf16[256,384]{1,0:T(8,128)(2,1)S(1)}, bf16[256,384]{1,0:T(8,128)(2...) custom-call(bf16[2,4,3,256,128]{4,3,2,1,0:T(8,128)(2,1)S(1)} %get-tuple-element.18.oq_ref, ...), custom_call_target="tpu_custom_call" | custom-call | tf_op jit(solution)/shard_map/pallas_call | solution.py:715
  104.7 0.0 copy-start.3
  104.7 0.7 copy-done.3
  105.5 0.7 copy-done.4
  106.1 0.7 copy-done.5
  106.8 0.7 copy-done.6
  107.5 0.6 copy-done.8
  108.1 0.6 copy-done.9
  108.7 2.2 %shard_map.157 = (bf16[256,768]{1,0:T(8,128)(2,1)}, bf16[256,384]{1,0:T(8,128)(2,1)}, bf16[256,384]{1,0:T(8,128)(2,1)}, bf16[256,384]{1,0:T(8,128)(2,1)}, bf16[1...) custom-call(bf16[256,768]{1,0:T(8,128)(2,1)} %copy-done.3, bf16[256,384]{1,0:T(8,128)(2,1)} %copy-done.4, ...), custom_call_target="tpu_custom_call" | custom-call | tf_op jit(solution)/shard_map/pallas_call | solution.py:745
  (6 shorter events, 0.0 us)
Async XLA Ops:
  0.6 38.9 %copy-start.10 = (s32[512]{0:T(512)S(1)}, s32[512]{0:T(512)}, u32[]{:S(2)}) copy-start(s32[512]{0:T(512)} %param.21) | copy-start | bytes 6148
  0.6 38.9 %copy-start.7 = (s32[128,128]{1,0:T(8,128)S(1)}, s32[128,128]{1,0:T(8,128)}, u32[]{:S(2)}) copy-start(s32[128,128]{1,0:T(8,128)} %tile_ref.1) | copy-start | bytes 196612
  0.7 38.9 %copy-start.11 = (s32[4]{0:T(128)S(1)}, s32[4]{0:T(128)}, u32[]{:S(2)}) copy-start(s32[4]{0:T(128)} %len_ref.1) | copy-start | bytes 52
  0.7 38.9 %copy-start.12 = (f32[3]{0:T(128)S(1)}, f32[3]{0:T(128)}, u32[]{:S(2)}) copy-start(f32[3]{0:T(128)} %bias_ref.1) | copy-start | bytes 40
  39.5 28.6 %copy-start = (bf16[384,3072]{1,0:T(8,128)(2,1)S(1)}, bf16[384,3072]{1,0:T(8,128)(2,1)}, u32[]{:S(2)}) copy-start(bf16[384,3072]{1,0:T(8,128)(2,1)} %w_hbm.3) | copy-start | bytes 7077892
  39.6 1.8 %copy-start.1 = (bf16[2,8,2,272,128]{4,3,2,1,0:T(8,128)(2,1)S(1)}, bf16[2,8,2,272,128]{4,3,2,1,0:T(8,128)(2,1)}, u32[]{:S(2)}) copy-start(bf16[2,8,2,272,128]{4,3,2,1,0:T(8,128)(2,1)} %get-tuple-element.17.kv_ref) | copy-start | bytes 6684676
  41.4 1.4 %copy-start.2 = (bf16[2,4,3,256,128]{4,3,2,1,0:T(8,128)(2,1)S(1)}, bf16[2,4,3,256,128]{4,3,2,1,0:T(8,128)(2,1)}, u32[]{:S(2)}) copy-start(bf16[2,4,3,256,128]{4,3,2,1,0:T(8,128)(2,1)} %get-tuple-element.16.qg_ref) | copy-start | bytes 4718596
  104.7 0.7 copy-start.3
  105.5 0.7 copy-start.4
  106.1 0.7 copy-start.5
  106.8 0.7 copy-start.6
  107.5 0.6 copy-start.8
  108.1 0.6 copy-start.9

commit v3 on v2

v3 whole, which is shorter than its diff:
```python
import jax
import jax.numpy as jnp
from jax import lax
from jax.experimental import pallas as pl
from jax.experimental.pallas import tpu as pltpu
from jax.sharding import PartitionSpec as P

MESH = pl.DeviceIdType.MESH
BF = jnp.bfloat16
F32 = jnp.float32

NX, NZ, NY = 4, 4, 2
HS = 128
NH = 3
TR = 256
CR = 16
BR = TR + CR
HALF = TR // 2
CLIPS = 4
CAP = 128
TILE = 64
LAT = NY * NX * TR
ROWS = NY * NX * BR
MASKED = -32768.0
BLOCKS = NH * NZ
VMEM_LIMIT = 58 * 1024 * 1024


def place():
    seq = lax.axis_index("seq")
    head = lax.axis_index("head")
    y = seq // (NZ * NX)
    z = (seq // NX) % NZ
    x = seq % NX
    return seq, head, y, z, x


def peers(seq, head, y, z, x):
    def at(yy, zz, xx):
        return (yy * NZ + zz) * NX + xx

    other_head = (head + 2) % 4
    core_head = head + 1 - 2 * (head % 2)
    return {
        "pair": (at(1 - y, z, x), head),
        "back": (at(1 - y, z, x), other_head),
        "core": (seq, core_head),
        "right": (at(y, z, (x + 1) % NX), head),
        "left": (at(y, z, (x + NX - 1) % NX), head),
        "up": (at(y, (z + 1) % NZ, x), head),
        "down": (at(y, (z + NZ - 1) % NZ, x), head),
    }


def greet(peer):
    barrier = pltpu.get_barrier_semaphore()
    for device in peer.values():
        pl.semaphore_signal(barrier, inc=1, device_id=device, device_id_type=MESH)
    pl.semaphore_wait(barrier, len(peer))


def sender(peer, send_sem, recv_sem, sent):
    def send(n, src, dst, to):
        copy = pltpu.make_async_remote_copy(
            src_ref=src,
            dst_ref=dst,
            send_sem=send_sem.at[n],
            recv_sem=recv_sem.at[n],
            device_id=peer[to],
            device_id_type=MESH,
        )
        copy.start()
        sent.append(copy)

    def arrived(n, dst):
        pltpu.make_async_remote_copy(
            src_ref=dst,
            dst_ref=dst,
            send_sem=send_sem.at[n],
            recv_sem=recv_sem.at[n],
            device_id=peer["core"],
            device_id_type=MESH,
        ).wait_recv()

    return send, arrived


def dot_nt(a, b):
    return lax.dot_general(a, b, (((1,), (1,)), ((), ())), preferred_element_type=F32)


def dot_nn(a, b):
    return lax.dot_general(a, b, (((1,), (0,)), ((), ())), preferred_element_type=F32)


def fused_kernel(
    q_hbm,
    k_hbm,
    v_hbm,
    tk_hbm,
    tv_hbm,
    go_hbm,
    w_hbm,
    tile_hbm,
    order_hbm,
    len_ref,
    bias_ref,
    out_hbm,
    gq_hbm,
    gk_hbm,
    gv_hbm,
    gtk_hbm,
    gtv_hbm,
    q_ref,
    k_ref,
    v_ref,
    tk_ref,
    tv_ref,
    go_ref,
    w_ref,
    tile_ref,
    order_ref,
    out_ref,
    gq_ref,
    gk_ref,
    gv_ref,
    gtk_ref,
    gtv_ref,
    qg_ref,
    kv_ref,
    st_pair,
    q_pair,
    goall,
    go_relay,
    acc,
    kaug,
    qaug,
    weights,
    slopes,
    vtext,
    queries_t,
    grads_t,
    oacc,
    qacc,
    oq_ref,
    kvg_ref,
    z_in,
    z_sum,
    x_in,
    x_sum,
    yq_out,
    yq_in,
    yk_out,
    yk_in,
    keep_q,
    attn,
    part,
    core_in,
    pair_sum,
    out_relay,
    far_in,
    g_send,
    g_recv,
    r_send,
    r_recv,
    local_sem,
    store_sem,
):
    seq, head, y, z, x = place()
    peer = peers(seq, head, y, z, x)
    zu, zd, zf = (z + 1) % NZ, (z + NZ - 1) % NZ, (z + 2) % NZ
    xr, xl, xf = (x + 1) % NX, (x + NX - 1) % NX, (x + 2) % NX
    other_head = (head + 2) % 4
    core_head = head + 1 - 2 * (head % 2)
    core_other = core_head + 2 - 4 * (core_head // 2)
    first, second = pl.ds(0, HALF), pl.ds(HALF, HALF)
    sent = []
    send, arrived = sender(peer, g_send, g_recv, sent)
    rsend, rarrived = sender(peer, r_send, r_recv, sent)
    cols = lambda h: slice(h * HS, (h + 1) * HS)
    by_y = lambda a, b: jnp.where(y == 0, a, b)
    wide = lambda a: a.astype(F32)
    factor = HS ** (-0.5)
    log2e = 1.4426950408889634

    load = []
    for n, (src, dst) in enumerate(
        (
            (k_hbm, k_ref),
            (tk_hbm, tk_ref),
            (v_hbm, v_ref),
            (tv_hbm, tv_ref),
            (q_hbm, q_ref),
            (go_hbm, go_ref),
            (w_hbm, w_ref),
            (tile_hbm, tile_ref),
            (order_hbm, order_ref),
        )
    ):
        copy = pltpu.make_async_copy(src, dst, local_sem.at[n])
        copy.start()
        load.append(copy)

    greet(peer)


    def x_send(a, t, yy):
        c = yy * NX + x
        send(10 + 6 * a + 2 * t, kv_ref.at[t, c], kv_ref.at[t, c], ("right", "left")[t])
        send(11 + 6 * a + 2 * t, kv_ref.at[t, c], kv_ref.at[t, c], ("left", "right")[t])

    def x_forward(a, yy):
        base = 10 + 6 * a
        left, right = yy * NX + xl, yy * NX + xr
        arrived(base + 0, kv_ref.at[0, left])
        send(base + 4, kv_ref.at[0, left], kv_ref.at[0, left], "right")
        arrived(base + 2, kv_ref.at[1, right])
        send(base + 5, kv_ref.at[1, right], kv_ref.at[1, right], "left")

    def x_finish(a, yy):
        base = 10 + 6 * a
        arrived(base + 1, kv_ref.at[0, yy * NX + xr])
        arrived(base + 3, kv_ref.at[1, yy * NX + xl])
        arrived(base + 4, kv_ref.at[0, yy * NX + xf])
        arrived(base + 5, kv_ref.at[1, yy * NX + xf])

    def z_own(t):
        base = 22 + 10 * t
        send(base + 0, qg_ref.at[t, z, 2], qg_ref.at[t, z, 2], "up")
        send(base + 1, qg_ref.at[t, z, y], qg_ref.at[t, z, y], "down")
        send(base + 2, qg_ref.at[t, z, y], qg_ref.at[t, z, y], "up")
        send(base + 3, qg_ref.at[t, z, 2], qg_ref.at[t, z, 2], "down")

    def z_own_forward(t):
        base = 22 + 10 * t
        arrived(base + 0, qg_ref.at[t, zd, 2])
        send(base + 4, qg_ref.at[t, zd, 2], qg_ref.at[t, zd, 2], "up")
        arrived(base + 1, qg_ref.at[t, zu, y])
        send(base + 5, qg_ref.at[t, zu, y], qg_ref.at[t, zu, y], "down")

    def z_pair(t):
        base = 22 + 10 * t
        send(base + 6, qg_ref.at[t, z, 1 - y], qg_ref.at[t, z, 1 - y], "up")
        send(base + 7, qg_ref.at[t, z, 1 - y], qg_ref.at[t, z, 1 - y], "down")

    def z_pair_forward(t):
        base = 22 + 10 * t
        arrived(base + 6, qg_ref.at[t, zd, 1 - y])
        src = qg_ref.at[t, zd, 1 - y, first]
        send(base + 8, src, src, "up")
        arrived(base + 7, qg_ref.at[t, zu, 1 - y])
        src = qg_ref.at[t, zu, 1 - y, second]
        send(base + 9, src, src, "down")

    def z_own_finish(t):
        base = 22 + 10 * t
        arrived(base + 2, qg_ref.at[t, zd, y])
        arrived(base + 3, qg_ref.at[t, zu, 2])
        arrived(base + 4, qg_ref.at[t, zf, 2])
        arrived(base + 5, qg_ref.at[t, zf, y])

    def z_pair_finish(t):
        base = 22 + 10 * t
        arrived(base + 8, qg_ref.at[t, zf, 1 - y, first])
        arrived(base + 9, qg_ref.at[t, zf, 1 - y, second])

    def feature(n):
        return w_ref[:, pl.ds(pl.multiple_of(n * 768, 128), 768)]

    ends = [len_ref[0]]
    for c in range(1, CLIPS):
        ends.append(ends[-1] + len_ref[c])

    def clip_at(pos):
        total = 0
        for c in range(CLIPS - 1):
            total = total + jnp.where(pos >= ends[c], 1, 0)
        return total

    lane = lax.broadcasted_iota(jnp.int32, (1, HS), 1)
    tiles_here = (lane % 64) // 16 == z
    clip_lane = ((z + 1) % NZ) * 16
    bias_lane = clip_lane + CLIPS
    bias_ones = jnp.where((lane >= bias_lane) & (lane < bias_lane + 3), 1.0, 0.0)

    def kv_index(n):
        return ((y + n % 2) % NY) * NX + (x + n // 2) % NX

    def key_side():
        for n in range(NY * NX):
            pos = kv_index(n) // NX * (NZ * NX * TR) + z * (NX * TR) + kv_index(n) % NX * TR
            pos = pos + lax.broadcasted_iota(jnp.int32, (TR, HS), 0)
            hit = (tiles_here & (pos // TILE == lane)) | (clip_at(pos) == lane - clip_lane)
            aug = jnp.where(hit, 1.0, bias_ones).astype(BF)
            for s in range(2):
                kaug[s, n * TR : (n + 1) * TR, HS:] = aug
        row = lax.broadcasted_iota(jnp.int32, (NY * NX * CR, HS), 0)
        n = row // CR
        plane = ((y + n % 2) % NY) * NZ + z
        text_row = (plane * NX + (x + n // 2) % NX) * CR + row % CR
        aug = jnp.broadcast_to(bias_ones, text_row.shape)
        for c in range(CLIPS):
            listed = jnp.where(order_ref[c : c + 1, :] == text_row, 1.0, 0.0)
            found = jnp.max(listed, axis=1, keepdims=True)
            aug = jnp.where(lane == clip_lane + c, found, aug)
        for s in range(2):
            kaug[s, LAT:, HS:] = aug.astype(BF)

    log_len = [
        jnp.log(jnp.full((1, HS), len_ref[c] + CAP, jnp.int32).astype(F32)) for c in range(CLIPS)
    ]

    def query_side(n, carry):
        yq = jnp.where(n // NZ == 1, 1 - y, y)
        start = ((yq * NZ + n % NZ) * NX + x) * TR
        head_bias = bias_ref[jnp.where(n // NZ == 2, 2, y)]
        pos = start + lax.broadcasted_iota(jnp.int32, (TR, HS), 0)
        clip = clip_at(pos)
        offset = jnp.broadcast_to(log_len[CLIPS - 1], (TR, HS))
        for c in range(CLIPS - 2, -1, -1):
            offset = jnp.where(pos < ends[c], log_len[c], offset)
        total = (head_bias - offset) * (HS**0.5)
        hi = total.astype(BF).astype(F32)
        mid = (total - hi).astype(BF).astype(F32)
        low = total - hi - mid
        in_bias = jnp.where(lane == bias_lane, hi, jnp.where(lane == bias_lane + 1, mid, low))
        in_bias = jnp.where((lane >= bias_lane) & (lane < bias_lane + 3), in_bias, 0.0)
        in_clip = (lane >= clip_lane) & (lane < clip_lane + CLIPS) & (lane - clip_lane != clip)
        side = jnp.where(in_clip, MASKED, in_bias)
        for u in range(TR // TILE):
            tile = start // TILE + u
            off = (tile_ref[pl.ds(tile, 1), :] == 0) & (lane != tile) & tiles_here
            rows = slice(u * TILE, (u + 1) * TILE)
            qaug[n, rows, HS:] = jnp.where(off, MASKED, side[rows]).astype(BF)
        return carry

    def block_j(n):
        return jnp.where(n // NZ == 2, 2, jnp.where(n // NZ == 1, 1 - y, y))

    def take_queries(n):
        value = qg_ref[0, n % NZ, n // NZ if n // NZ == 2 else (y + n // NZ) % NY]
        qaug[n, :, 0:HS] = value
        queries_t[:, n * TR : (n + 1) * TR] = value.T

    def take_keys(r):
        for n in range(r, NY * NX, 2):
            for s in range(2):
                kaug[s, n * TR : (n + 1) * TR, 0:HS] = kv_ref[0, kv_index(n), s, 0:TR]
                kaug[s, LAT + n * CR : LAT + (n + 1) * CR, 0:HS] = kv_ref[0, kv_index(n), s, TR:BR]
                vtext[s, n * CR : (n + 1) * CR] = kv_ref[1, kv_index(n), s, TR:BR]

    def weigh(n, slot, first_row, count):
        scores = dot_nt(qaug[n], kaug[slot, first_row : first_row + count, :])
        e = jnp.exp2(jnp.minimum(scores * (factor * log2e), 115.0))
        rest = pl.reciprocal(1.0 + e, approx=True)
        sig = e * rest
        weight = sig.astype(BF)
        rows = pl.ds(pl.multiple_of(n * TR, TR), TR)
        weights[rows, first_row : first_row + count] = weight
        slopes[rows, first_row : first_row + count] = (sig * rest).astype(BF)
        return weight

    def forward(n, r, slot, text):
        total = None
        for d in range(NX):
            c = 2 * d + r
            weight = weigh(n, slot, c * TR, TR)
            share = dot_nn(weight, kv_ref[1, kv_index(c), slot, 0:TR])
            total = share if total is None else total + share
        if text:
            total = total + dot_nn(weigh(n, slot, LAT, NY * NX * CR), vtext[slot])
        if r == 0:
            oacc[n] = total
        else:
            oq_ref[0, n % NZ, block_j(n)] = (oacc[n] + total).astype(BF)

    def forward_blocks(low, high, r, text):
        def body(n, carry):
            forward(n, r, n // (2 * NZ), text)
            return carry

        lax.fori_loop(low, high, body, 0)

    def slope_blocks(first_row, count):
        def body(n, carry):
            slot = n // (2 * NZ)
            rows = pl.ds(pl.multiple_of(n * TR, TR), TR)
            slope = wide(slopes[rows, first_row : first_row + count])
            grads = qg_ref[1, n % NZ, block_j(n)]
            if first_row == LAT:
                vals = vtext[slot]
            else:
                c = first_row // TR
                vals = jnp.concatenate(
                    [kv_ref[1, kv_index(c + r), slot, 0:TR] for r in range(2)], axis=0
                )
            product = dot_nt(grads, vals)
            slope = (product * slope).astype(BF)
            slopes[rows, first_row : first_row + count] = slope
            share = dot_nn(slope, kaug[slot, first_row : first_row + count, 0:HS])
            if first_row == LAT:
                qacc[n] = share
            else:
                qacc[n] += share
            return carry

        lax.fori_loop(0, BLOCKS, body, 0)

    def key_grads(first_row, count):
        for s, (low, high) in enumerate(((0, 2 * NZ * TR), (2 * NZ * TR, BLOCKS * TR))):
            for t in range(2):
                left = (queries_t, grads_t)[t][:, low:high]
                right = (slopes, weights)[t][low:high, first_row : first_row + count]
                total = dot_nn(left, right).astype(BF)
                if first_row == LAT:
                    text_rows = total.T
                    for n in range(NY * NX):
                        kvg_ref[t, kv_index(n), s, TR:BR] = text_rows[n * CR : (n + 1) * CR]
                else:
                    for r in range(2):
                        n = first_row // TR + r
                        kvg_ref[t, kv_index(n), s, 0:TR] = total[:, r * TR : (r + 1) * TR].T


    def z_start(t):
        base = 6 * t
        rsend(base + 0, oq_ref.at[t, zf, :, first], z_in.at[t, 0], "up")
        rsend(base + 3, oq_ref.at[t, zf, :, second], z_in.at[t, 3], "down")
        rsend(base + 1, oq_ref.at[t, zd, :, first], z_in.at[t, 1], "down")
        rsend(base + 4, oq_ref.at[t, zu, :, second], z_in.at[t, 4], "up")

    def z_relay(t):
        base = 6 * t
        rarrived(base + 0, z_in.at[t, 0])
        z_sum[t, 0] = (wide(z_in[t, 0]) + wide(oq_ref[t, zu, :, first])).astype(BF)
        rsend(base + 2, z_sum.at[t, 0], z_in.at[t, 2], "up")
        rarrived(base + 3, z_in.at[t, 3])
        z_sum[t, 1] = (wide(z_in[t, 3]) + wide(oq_ref[t, zd, :, second])).astype(BF)
        rsend(base + 5, z_sum.at[t, 1], z_in.at[t, 5], "down")

    def z_total(t, scale):
        base = 6 * t
        for n in (1, 2, 4, 5):
            rarrived(base + n, z_in.at[t, n])
        for rows, one, two in ((first, 1, 2), (second, 4, 5)):

            def total(j):
                value = wide(oq_ref[t, z, j, rows]) + wide(z_in[t, one, j]) + wide(z_in[t, two, j])
                return (value * scale).astype(BF) if scale != 1.0 else value.astype(BF)

            yq_out[t, rows] = total(1 - y)
            keep_q[t, 0, rows] = total(y)
            keep_q[t, 1, rows] = total(2)
        rsend(24 + t, yq_out.at[t], yq_in.at[t], "pair")

    def x_base(t, a):
        return 12 + 6 * t + 3 * a

    ring = (("right", "left"), ("left", "right"))
    ahead = ((xr, xl), (xl, xr))
    plane = (y, 1 - y)

    def x_far(t, a):
        src = kvg_ref.at[t, plane[a] * NX + xf]
        rsend(x_base(t, a), src, x_in.at[t, a, 0], ring[t][0])

    def x_near(t, a):
        src = kvg_ref.at[t, plane[a] * NX + ahead[t][1]]
        rsend(x_base(t, a) + 1, src, x_in.at[t, a, 1], ring[t][1])

    def x_relay(t, a):
        rarrived(x_base(t, a), x_in.at[t, a, 0])
        mine = wide(kvg_ref[t, plane[a] * NX + ahead[t][0]])
        x_sum[t, a] = (wide(x_in[t, a, 0]) + mine).astype(BF)
        rsend(x_base(t, a) + 2, x_sum.at[t, a], x_in.at[t, a, 2], ring[t][0])

    def x_total(t, a):
        rarrived(x_base(t, a) + 1, x_in.at[t, a, 1])
        rarrived(x_base(t, a) + 2, x_in.at[t, a, 2])
        value = wide(kvg_ref[t, plane[a] * NX + x]) + wide(x_in[t, a, 1]) + wide(x_in[t, a, 2])
        return value * factor if t == 0 else value

    def project(n):
        return dot_nn(attn[...], feature(n)).astype(BF)

    send(0, go_hbm.at[first], go_relay.at[0], "pair")
    send(1, go_hbm.at[second], go_relay.at[1], "back")
    send(2, go_hbm, goall.at[head], "core")
    c = y * NX + x
    for t, (ref, text) in enumerate(((k_ref, tk_ref), (v_ref, tv_ref))):
        load[2 * t].wait()
        load[2 * t + 1].wait()
        kv_ref[t, c, 0, 0:TR] = by_y(ref[:, cols(0)], ref[:, cols(1)])
        kv_ref[t, c, 0, TR:BR] = by_y(text[:, cols(0)], text[:, cols(1)])
        kv_ref[t, c, 1, 0:TR] = ref[:, cols(2)]
        kv_ref[t, c, 1, TR:BR] = text[:, cols(2)]
        x_send(0, t, y)
        st_pair[t, 0, 0:TR] = by_y(ref[:, cols(1)], ref[:, cols(0)])
        st_pair[t, 0, TR:BR] = by_y(text[:, cols(1)], text[:, cols(0)])
        st_pair[t, 1, 0:TR] = ref[:, cols(2)]
        st_pair[t, 1, TR:BR] = text[:, cols(2)]
        send(7 + t, st_pair.at[t], kv_ref.at[t, c], "pair")
    load[4].wait()
    qg_ref[0, z, y] = by_y(q_ref[:, cols(0)], q_ref[:, cols(1)])
    qg_ref[0, z, 2] = q_ref[:, cols(2)]
    q_pair[0] = by_y(q_ref[:, cols(1)], q_ref[:, cols(0)])
    send(6, q_pair.at[0], qg_ref.at[0, z, y], "pair")
    z_own(0)
    load[5].wait()
    load[6].wait()
    acc[...] = dot_nt(go_ref[...], feature(head))
    load[7].wait()
    load[8].wait()
    key_side()
    lax.fori_loop(0, BLOCKS, query_side, 0)

    arrived(1, go_relay.at[1])
    send(4, go_relay.at[1], goall.at[other_head, second], "pair")
    z_own_forward(0)
    arrived(6, qg_ref.at[0, z, 1 - y])
    z_pair(0)
    arrived(0, go_relay.at[0])
    send(3, go_relay.at[0], goall.at[head, first], "back")
    x_forward(0, y)
    arrived(2, goall.at[core_head])
    acc[...] += dot_nt(goall[core_head], feature(core_head))
    z_own_finish(0)
    for n in (0, 1, 2, 3, 8, 9, 10, 11):
        take_queries(n)
    z_pair_forward(0)
    for t in range(2):
        arrived(7 + t, kv_ref.at[t, (1 - y) * NX + x])
        x_send(1, t, 1 - y)
    x_finish(0, y)
    take_keys(0)
    forward_blocks(0, NZ, 0, False)
    arrived(3, goall.at[other_head, first])
    arrived(4, goall.at[other_head, second])
    send(5, goall.at[other_head], goall.at[other_head], "core")
    acc[...] += dot_nt(goall[other_head], feature(other_head))
    forward_blocks(2 * NZ, 3 * NZ, 0, False)
    arrived(5, goall.at[core_other])
    grad = (acc[...] + dot_nt(goall[core_other], feature(core_other))).astype(BF)
    q_pair[1] = by_y(grad[:, cols(1)], grad[:, cols(0)])
    send(9, q_pair.at[1], qg_ref.at[1, z, y], "pair")
    qg_ref[1, z, y] = by_y(grad[:, cols(0)], grad[:, cols(1)])
    qg_ref[1, z, 2] = grad[:, cols(2)]
    z_own(1)
    x_forward(1, 1 - y)
    z_pair_finish(0)
    for n in range(NZ, 2 * NZ):
        take_queries(n)
    forward_blocks(NZ, 2 * NZ, 0, False)
    arrived(9, qg_ref.at[1, z, 1 - y])
    z_pair(1)
    z_own_forward(1)
    x_finish(1, 1 - y)
    take_keys(1)
    forward_blocks(0, NZ, 1, True)
    z_pair_forward(1)
    forward_blocks(NZ, 3 * NZ, 1, True)
    z_start(0)

    z_own_finish(1)
    z_pair_finish(1)
    for n in range(BLOCKS):
        j = 2 if n // NZ == 2 else (y + n // NZ) % NY
        grads_t[:, n * TR : (n + 1) * TR] = qg_ref[1, n % NZ, j].T
    slope_blocks(LAT, NY * NX * CR)
    key_grads(LAT, NY * NX * CR)
    pair_rows = 2 * TR

    slope_blocks(2 * pair_rows, pair_rows)
    z_relay(0)
    key_grads(2 * pair_rows, pair_rows)
    for a in (1, 0):
        for t in range(2):
            x_far(t, a)

    slope_blocks(1 * pair_rows, pair_rows)
    z_total(0, 1.0)
    key_grads(1 * pair_rows, pair_rows)
    for a in (1, 0):
        x_near(1, a)
        x_relay(0, a)

    rarrived(24, yq_in.at[0])
    attn[:, cols(0)] = by_y(keep_q[0, 0], yq_in[0])
    attn[:, cols(1)] = by_y(yq_in[0], keep_q[0, 0])
    attn[:, cols(2)] = keep_q[0, 1]
    part[0] = project(core_other)
    rsend(28, part.at[0], core_in.at[0], "core")
    part[1] = project(core_head)
    rsend(29, part.at[1], core_in.at[1], "core")
    part[2] = project(other_head)
    slope_blocks(3 * pair_rows, pair_rows)
    rarrived(28, core_in.at[0])
    pair_sum[...] = (wide(part[2]) + wide(core_in[0])).astype(BF)
    rsend(30, pair_sum.at[first], out_relay.at[0], "pair")
    rsend(31, pair_sum.at[second], out_relay.at[1], "back")
    key_grads(3 * pair_rows, pair_rows)
    for a in (1, 0):
        x_near(0, a)
        x_relay(1, a)

    slope_blocks(0, pair_rows)
    for n in range(BLOCKS):
        j = 2 if n // NZ == 2 else (y + n // NZ) % NY
        oq_ref[1, n % NZ, j] = qacc[n].astype(BF)
    z_start(1)
    key_grads(0, pair_rows)
    part[3] = project(head)
    rarrived(31, out_relay.at[1])
    rsend(33, out_relay.at[1], far_in.at[second], "pair")
    rarrived(30, out_relay.at[0])
    rsend(32, out_relay.at[0], far_in.at[first], "back")
    z_relay(1)
    for t in range(2):
        yk_out[t] = x_total(t, 1).astype(BF)
        rsend(26 + t, yk_out.at[t], yk_in.at[t], "pair")
    z_total(1, factor)

    stores = []

    def store(src, dst):
        copy = pltpu.make_async_copy(src, dst, store_sem.at[len(stores)])
        copy.start()
        stores.append(copy)

    results = ((gk_ref, gtk_ref, gk_hbm, gtk_hbm), (gv_ref, gtv_ref, gv_hbm, gtv_hbm))
    rarrived(29, core_in.at[1])
    rarrived(32, far_in.at[first])
    rarrived(33, far_in.at[second])
    out_ref[...] = (wide(part[3]) + wide(core_in[1]) + wide(far_in[...])).astype(BF)
    store(out_ref, out_hbm)
    for t, (ref, text, to, text_to) in enumerate(results):
        own = x_total(t, 0)
        rarrived(26 + t, yk_in.at[t])
        mine = own[0].astype(BF)
        other = yk_in[t, 0]
        both = (own[1] + wide(yk_in[t, 1])).astype(BF)
        for h, value in ((0, by_y(mine, other)), (1, by_y(other, mine)), (2, both)):
            ref[:, cols(h)] = value[0:TR]
            text[:, cols(h)] = value[TR:BR]
        store(ref, to)
        store(text, text_to)
    rarrived(25, yq_in.at[1])
    gq_ref[:, cols(0)] = by_y(keep_q[1, 0], yq_in[1])
    gq_ref[:, cols(1)] = by_y(yq_in[1], keep_q[1, 0])
    gq_ref[:, cols(2)] = keep_q[1, 1]
    store(gq_ref, gq_hbm)
    for copy in sent:
        copy.wait_send()
    for copy in stores:
        copy.wait()


def store_kernel(*refs):
    count = len(refs) // 2
    sems = refs[-1]
    copies = [
        pltpu.make_async_copy(refs[n], refs[count + n], sems.at[n]) for n in range(count)
    ]
    for copy in copies:
        copy.start()
    for copy in copies:
        copy.wait()


def shards(
    queries,
    keys,
    values,
    text_keys,
    text_values,
    head_bias,
    out_weight,
    grad_out,
    clip_lengths,
    tile_mask,
    caption_order,
):
    smem = pl.BlockSpec(memory_space=pltpu.SMEM)
    hbm = pl.BlockSpec(memory_space=pltpu.HBM)
    dma = pltpu.SemaphoreType.DMA
    qg_shape = (2, NZ, NH, TR, HS)
    kv_shape = (2, NY * NX, 2, BR, HS)
    out_cols = grad_out.shape[1]
    order = caption_order.reshape(CLIPS, CAP)
    token = pltpu.VMEM((TR, NH * HS), BF)
    text = pltpu.VMEM((CR, NH * HS), BF)
    wide_out = pltpu.VMEM((TR, out_cols), BF)
    halves = pltpu.VMEM((2, HALF, out_cols), BF)
    token_shape = jax.ShapeDtypeStruct((TR, NH * HS), BF)
    text_shape = jax.ShapeDtypeStruct((CR, NH * HS), BF)
    result = (
        jax.ShapeDtypeStruct((TR, out_cols), BF),
        token_shape,
        token_shape,
        token_shape,
        text_shape,
        text_shape,
    )
    held = pl.pallas_call(
        fused_kernel,
        out_shape=result,
        in_specs=[hbm] * 9 + [smem] * 2,
        out_specs=(hbm,) * len(result),
        scratch_shapes=[
            token,
            token,
            token,
            text,
            text,
            wide_out,
            pltpu.VMEM(out_weight.shape, BF),
            pltpu.VMEM(tile_mask.shape, jnp.int32),
            pltpu.VMEM(order.shape, jnp.int32),
            wide_out,
            token,
            token,
            token,
            text,
            text,
            pltpu.VMEM(qg_shape, BF),
            pltpu.VMEM(kv_shape, BF),
            pltpu.VMEM((2, 2, BR, HS), BF),
            pltpu.VMEM((2, TR, HS), BF),
            pltpu.VMEM((4, TR, out_cols), BF),
            halves,
            pltpu.VMEM((TR, NH * HS), F32),
            pltpu.VMEM((2, ROWS, 2 * HS), BF),
            pltpu.VMEM((BLOCKS, TR, 2 * HS), BF),
            pltpu.VMEM((BLOCKS * TR, ROWS), BF),
            pltpu.VMEM((BLOCKS * TR, ROWS), BF),
            pltpu.VMEM((2, NY * NX * CR, HS), BF),
            pltpu.VMEM((HS, BLOCKS * TR), BF),
            pltpu.VMEM((HS, BLOCKS * TR), BF),
            pltpu.VMEM((BLOCKS, TR, HS), F32),
            pltpu.VMEM((BLOCKS, TR, HS), F32),
            pltpu.VMEM(qg_shape, BF),
            pltpu.VMEM(kv_shape, BF),
            pltpu.VMEM((2, 6, NH, HALF, HS), BF),
            pltpu.VMEM((2, 2, NH, HALF, HS), BF),
            pltpu.VMEM((2, NY, 3, 2, BR, HS), BF),
            pltpu.VMEM((2, NY, 2, BR, HS), BF),
            pltpu.VMEM((2, TR, HS), BF),
            pltpu.VMEM((2, TR, HS), BF),
            pltpu.VMEM((2, 2, BR, HS), BF),
            pltpu.VMEM((2, 2, BR, HS), BF),
            pltpu.VMEM((2, 2, TR, HS), BF),
            token,
            pltpu.VMEM((4, TR, out_cols), BF),
            pltpu.VMEM((2, TR, out_cols), BF),
            wide_out,
            halves,
            wide_out,
            dma((42,)),
            dma((42,)),
            dma((34,)),
            dma((34,)),
            dma((9,)),
            dma((len(result),)),
        ],
        compiler_params=pltpu.CompilerParams(
            collective_id=0, has_side_effects=True, vmem_limit_bytes=VMEM_LIMIT
        ),
    )(
        queries,
        keys,
        values,
        text_keys,
        text_values,
        grad_out,
        out_weight,
        tile_mask,
        order,
        clip_lengths,
        head_bias,
    )
    return pl.pallas_call(
        store_kernel,
        out_shape=result,
        in_specs=[hbm] * len(result),
        out_specs=(hbm,) * len(result),
        scratch_shapes=[dma((len(result),))],
        compiler_params=pltpu.CompilerParams(vmem_limit_bytes=VMEM_LIMIT),
    )(*held)


def solution(mesh):
    in_specs = (
        P("seq", "head"),
        P("seq", "head"),
        P("seq", "head"),
        P("seq", "head"),
        P("seq", "head"),
        P("head"),
        P("head", None),
        P("seq", "head"),
        P(),
        P(),
        P(),
    )
    out_specs = (P("seq", "head"),) * 6
    return jax.shard_map(shards, mesh=mesh, in_specs=in_specs, out_specs=out_specs, check_vma=False)
```

time: 113 us -> 126 us (1.12); the launches traced: 111 us -> 125 us
  Pallas kernels: 103 us -> 125 us
  local copies, waits for them, and re-layouts: 7.16 us -> 0 us
    pallas_call x4 -> x2, Pallas kernels: 103 us -> 125 us  [the longest x1 93 us: shards(): pl.pallas_call(fused_kernel, out_shape=result, in_specs=[hbm] * 9 + [smem...]
    unnamed x26 -> x0, local copies, waits for them, and re-layouts: 7.16 us -> none
where the time goes in v3:
time: 126 us; the launch traced here: 125 us
  Pallas kernels  125 us (99%)
    pallas_call x1, Pallas kernels, shards(): pl.pallas_call(fused_kernel, out_shape=result, in_specs=[hbm] * 9 + [smem...  93 us
    pallas_call x1, Pallas kernels, shards(): pl.pallas_call(store_kernel, out_shape=result, in_specs=[hbm] * len(resul...  31.7 us

profile of v3, /device:TPU:0, one launch (start us, length us, event | category | flops | bytes accessed | tf_op | source)
XLA Modules:
  0.0 125.5 jit_solution(2827510425933245900)
XLA Ops:
  0.6 93.0 %shard_map.154 = (bf16[256,768]{1,0:T(8,128)(2,1)}, bf16[256,384]{1,0:T(8,128)(2,1)}, bf16[256,384]{1,0:T(8,128)(2,1)}, bf16[256,384]{1,0:T(8,128)(2,1)}, bf16[1...) custom-call(bf16[256,384]{1,0:T(8,128)(2,1)} %q_hbm.1, bf16[256,384]{1,0:T(8,128)(2,1)} %k_hbm.1, bf16[256,384]{1,0:T(8,128)(2,1)} %v_hbm.1, ...), custom_call_target="tpu_custom_call" | custom-call | tf_op jit(solution)/shard_map/pallas_call | solution.py:704
  93.6 31.7 %shard_map.155 = (bf16[256,768]{1,0:T(8,128)(2,1)}, bf16[256,384]{1,0:T(8,128)(2,1)}, bf16[256,384]{1,0:T(8,128)(2,1)}, bf16[256,384]{1,0:T(8,128)(2,1)}, bf16[1...) custom-call(bf16[256,768]{1,0:T(8,128)(2,1)} %get-tuple-element.12.refs_0_, bf16[256,384]{1,0:T(8,128)(2,1)} %get-tuple-element.13.refs_1_, ...), custom_call_target="tpu_custom_call" | custom-call | tf_op jit(solution)/shard_map/pallas_call | solution.py:781

commit v4 on v3

--- a/solution.py
+++ b/solution.py
@@ -217,10 +217,13 @@
         arrived(base + 2, kv_ref.at[1, right])
         send(base + 5, kv_ref.at[1, right], kv_ref.at[1, right], "left")
 
-    def x_finish(a, yy):
+    def x_near_finish(a, yy):
         base = 10 + 6 * a
         arrived(base + 1, kv_ref.at[0, yy * NX + xr])
         arrived(base + 3, kv_ref.at[1, yy * NX + xl])
+
+    def x_far_finish(a, yy):
+        base = 10 + 6 * a
         arrived(base + 4, kv_ref.at[0, yy * NX + xf])
         arrived(base + 5, kv_ref.at[1, yy * NX + xf])
 
@@ -342,12 +345,11 @@
         qaug[n, :, 0:HS] = value
         queries_t[:, n * TR : (n + 1) * TR] = value.T
 
-    def take_keys(r):
-        for n in range(r, NY * NX, 2):
-            for s in range(2):
-                kaug[s, n * TR : (n + 1) * TR, 0:HS] = kv_ref[0, kv_index(n), s, 0:TR]
-                kaug[s, LAT + n * CR : LAT + (n + 1) * CR, 0:HS] = kv_ref[0, kv_index(n), s, TR:BR]
-                vtext[s, n * CR : (n + 1) * CR] = kv_ref[1, kv_index(n), s, TR:BR]
+    def take_key(n):
+        for s in range(2):
+            kaug[s, n * TR : (n + 1) * TR, 0:HS] = kv_ref[0, kv_index(n), s, 0:TR]
+            kaug[s, LAT + n * CR : LAT + (n + 1) * CR, 0:HS] = kv_ref[0, kv_index(n), s, TR:BR]
+            vtext[s, n * CR : (n + 1) * CR] = kv_ref[1, kv_index(n), s, TR:BR]
 
     def weigh(n, slot, first_row, count):
         scores = dot_nt(qaug[n], kaug[slot, first_row : first_row + count, :])
@@ -360,30 +362,35 @@
         slopes[rows, first_row : first_row + count] = (sig * rest).astype(BF)
         return weight
 
-    def forward(n, r, slot, text):
-        total = None
-        for d in range(NX):
-            c = 2 * d + r
-            weight = weigh(n, slot, c * TR, TR)
-            share = dot_nn(weight, kv_ref[1, kv_index(c), slot, 0:TR])
-            total = share if total is None else total + share
-        if text:
-            total = total + dot_nn(weigh(n, slot, LAT, NY * NX * CR), vtext[slot])
-        if r == 0:
-            oacc[n] = total
-        else:
-            oq_ref[0, n % NZ, block_j(n)] = (oacc[n] + total).astype(BF)
-
-    def forward_blocks(low, high, r, text):
-        def body(n, carry):
-            forward(n, r, n // (2 * NZ), text)
+    def per_plane(body):
+        def step(zq, carry):
+            for g in range(NH):
+                body(g * NZ + zq, g // 2)
             return carry
 
-        lax.fori_loop(low, high, body, 0)
+        lax.fori_loop(0, NZ, step, 0)
+
+    def forward(c, fresh=False):
+        take_key(c)
+
+        def body(n, slot):
+            share = dot_nn(weigh(n, slot, c * TR, TR), kv_ref[1, kv_index(c), slot, 0:TR])
+            if fresh:
+                oacc[n] = share
+            else:
+                oacc[n] += share
+
+        per_plane(body)
+
+    def forward_text():
+        def body(n, slot):
+            share = dot_nn(weigh(n, slot, LAT, NY * NX * CR), vtext[slot])
+            oq_ref[0, n % NZ, block_j(n)] = (oacc[n] + share).astype(BF)
+
+        per_plane(body)
 
     def slope_blocks(first_row, count):
-        def body(n, carry):
-            slot = n // (2 * NZ)
+        def body(n, slot):
             rows = pl.ds(pl.multiple_of(n * TR, TR), TR)
             slope = wide(slopes[rows, first_row : first_row + count])
             grads = qg_ref[1, n % NZ, block_j(n)]
@@ -402,9 +409,8 @@
                 qacc[n] = share
             else:
                 qacc[n] += share
-            return carry
-
-        lax.fori_loop(0, BLOCKS, body, 0)
+
+        per_plane(body)
 
     def key_grads(first_row, count):
         for s, (low, high) in enumerate(((0, 2 * NZ * TR), (2 * NZ * TR, BLOCKS * TR))):
@@ -483,62 +489,68 @@
     def project(n):
         return dot_nn(attn[...], feature(n)).astype(BF)
 
-    send(0, go_hbm.at[first], go_relay.at[0], "pair")
     send(1, go_hbm.at[second], go_relay.at[1], "back")
-    send(2, go_hbm, goall.at[head], "core")
+    load[4].wait()
+    q_pair[0] = by_y(q_ref[:, cols(1)], q_ref[:, cols(0)])
+    send(6, q_pair.at[0], qg_ref.at[0, z, y], "pair")
+    qg_ref[0, z, y] = by_y(q_ref[:, cols(0)], q_ref[:, cols(1)])
+    qg_ref[0, z, 2] = q_ref[:, cols(2)]
+    z_own(0)
     c = y * NX + x
     for t, (ref, text) in enumerate(((k_ref, tk_ref), (v_ref, tv_ref))):
         load[2 * t].wait()
         load[2 * t + 1].wait()
+        st_pair[t, 0, 0:TR] = by_y(ref[:, cols(1)], ref[:, cols(0)])
+        st_pair[t, 0, TR:BR] = by_y(text[:, cols(1)], text[:, cols(0)])
+        st_pair[t, 1, 0:TR] = ref[:, cols(2)]
+        st_pair[t, 1, TR:BR] = text[:, cols(2)]
+        send(7 + t, st_pair.at[t], kv_ref.at[t, c], "pair")
         kv_ref[t, c, 0, 0:TR] = by_y(ref[:, cols(0)], ref[:, cols(1)])
         kv_ref[t, c, 0, TR:BR] = by_y(text[:, cols(0)], text[:, cols(1)])
         kv_ref[t, c, 1, 0:TR] = ref[:, cols(2)]
         kv_ref[t, c, 1, TR:BR] = text[:, cols(2)]
         x_send(0, t, y)
-        st_pair[t, 0, 0:TR] = by_y(ref[:, cols(1)], ref[:, cols(0)])
-        st_pair[t, 0, TR:BR] = by_y(text[:, cols(1)], text[:, cols(0)])
-        st_pair[t, 1, 0:TR] = ref[:, cols(2)]
-        st_pair[t, 1, TR:BR] = text[:, cols(2)]
-        send(7 + t, st_pair.at[t], kv_ref.at[t, c], "pair")
-    load[4].wait()
-    qg_ref[0, z, y] = by_y(q_ref[:, cols(0)], q_ref[:, cols(1)])
-    qg_ref[0, z, 2] = q_ref[:, cols(2)]
-    q_pair[0] = by_y(q_ref[:, cols(1)], q_ref[:, cols(0)])
-    send(6, q_pair.at[0], qg_ref.at[0, z, y], "pair")
-    z_own(0)
-    load[5].wait()
-    load[6].wait()
-    acc[...] = dot_nt(go_ref[...], feature(head))
+    send(2, go_hbm, goall.at[head], "core")
     load[7].wait()
     load[8].wait()
     key_side()
     lax.fori_loop(0, BLOCKS, query_side, 0)
-
-    arrived(1, go_relay.at[1])
-    send(4, go_relay.at[1], goall.at[other_head, second], "pair")
     z_own_forward(0)
     arrived(6, qg_ref.at[0, z, 1 - y])
     z_pair(0)
-    arrived(0, go_relay.at[0])
-    send(3, go_relay.at[0], goall.at[head, first], "back")
+    load[5].wait()
+    load[6].wait()
+    acc[...] = dot_nt(go_ref[...], feature(head))
     x_forward(0, y)
-    arrived(2, goall.at[core_head])
-    acc[...] += dot_nt(goall[core_head], feature(core_head))
-    z_own_finish(0)
-    for n in (0, 1, 2, 3, 8, 9, 10, 11):
-        take_queries(n)
     z_pair_forward(0)
     for t in range(2):
         arrived(7 + t, kv_ref.at[t, (1 - y) * NX + x])
         x_send(1, t, 1 - y)
-    x_finish(0, y)
-    take_keys(0)
-    forward_blocks(0, NZ, 0, False)
+    send(0, go_hbm.at[first], go_relay.at[0], "pair")
+    z_own_finish(0)
+    z_pair_finish(0)
+    for n in range(BLOCKS):
+        take_queries(n)
+    forward(0, True)
+    arrived(2, goall.at[core_head])
+    acc[...] += dot_nt(goall[core_head], feature(core_head))
+    forward(1)
+    arrived(0, go_relay.at[0])
+    send(3, go_relay.at[0], goall.at[head, first], "back")
+    arrived(1, go_relay.at[1])
+    send(4, go_relay.at[1], goall.at[other_head, second], "pair")
+    x_near_finish(0, y)
+    x_far_finish(0, y)
+    forward(2)
+    forward(6)
+    x_forward(1, 1 - y)
+    forward(4)
     arrived(3, goall.at[other_head, first])
     arrived(4, goall.at[other_head, second])
     send(5, goall.at[other_head], goall.at[other_head], "core")
     acc[...] += dot_nt(goall[other_head], feature(other_head))
-    forward_blocks(2 * NZ, 3 * NZ, 0, False)
+    x_near_finish(1, 1 - y)
+    forward(3)
     arrived(5, goall.at[core_other])
     grad = (acc[...] + dot_nt(goall[core_other], feature(core_other))).astype(BF)
     q_pair[1] = by_y(grad[:, cols(1)], grad[:, cols(0)])
@@ -546,24 +558,21 @@
     qg_ref[1, z, y] = by_y(grad[:, cols(0)], grad[:, cols(1)])
     qg_ref[1, z, 2] = grad[:, cols(2)]
     z_own(1)
-    x_forward(1, 1 - y)
-    z_pair_finish(0)
-    for n in range(NZ, 2 * NZ):
-        take_queries(n)
-    forward_blocks(NZ, 2 * NZ, 0, False)
+    forward(7)
+    x_far_finish(1, 1 - y)
+    forward(5)
     arrived(9, qg_ref.at[1, z, 1 - y])
     z_pair(1)
     z_own_forward(1)
-    x_finish(1, 1 - y)
-    take_keys(1)
-    forward_blocks(0, NZ, 1, True)
+    forward_text()
+    z_start(0)
     z_pair_forward(1)
-    forward_blocks(NZ, 3 * NZ, 1, True)
-    z_start(0)
 
     z_own_finish(1)
-    z_pair_finish(1)
-    for n in range(BLOCKS):
+    for n in (0, 1, 2, 3, 8, 9, 10, 11, 4, 5, 6, 7):
+        if n == NZ:
+            z_relay(0)
+            z_pair_finish(1)
         j = 2 if n // NZ == 2 else (y + n // NZ) % NY
         grads_t[:, n * TR : (n + 1) * TR] = qg_ref[1, n % NZ, j].T
     slope_blocks(LAT, NY * NX * CR)
@@ -571,37 +580,41 @@
     pair_rows = 2 * TR
 
     slope_blocks(2 * pair_rows, pair_rows)
-    z_relay(0)
+    z_total(0, 1.0)
     key_grads(2 * pair_rows, pair_rows)
     for a in (1, 0):
         for t in range(2):
             x_far(t, a)
-
-    slope_blocks(1 * pair_rows, pair_rows)
-    z_total(0, 1.0)
-    key_grads(1 * pair_rows, pair_rows)
-    for a in (1, 0):
-        x_near(1, a)
-        x_relay(0, a)
-
     rarrived(24, yq_in.at[0])
     attn[:, cols(0)] = by_y(keep_q[0, 0], yq_in[0])
     attn[:, cols(1)] = by_y(yq_in[0], keep_q[0, 0])
     attn[:, cols(2)] = keep_q[0, 1]
     part[0] = project(core_other)
     rsend(28, part.at[0], core_in.at[0], "core")
+    part[2] = project(other_head)
     part[1] = project(core_head)
-    rsend(29, part.at[1], core_in.at[1], "core")
-    part[2] = project(other_head)
-    slope_blocks(3 * pair_rows, pair_rows)
     rarrived(28, core_in.at[0])
     pair_sum[...] = (wide(part[2]) + wide(core_in[0])).astype(BF)
     rsend(30, pair_sum.at[first], out_relay.at[0], "pair")
     rsend(31, pair_sum.at[second], out_relay.at[1], "back")
+    rsend(29, part.at[1], core_in.at[1], "core")
+
+    slope_blocks(1 * pair_rows, pair_rows)
+    key_grads(1 * pair_rows, pair_rows)
+    for a in (1, 0):
+        x_near(1, a)
+        x_relay(0, a)
+    part[3] = project(head)
+
+    slope_blocks(3 * pair_rows, pair_rows)
     key_grads(3 * pair_rows, pair_rows)
     for a in (1, 0):
         x_near(0, a)
         x_relay(1, a)
+    rarrived(30, out_relay.at[0])
+    rsend(32, out_relay.at[0], far_in.at[first], "back")
+    rarrived(31, out_relay.at[1])
+    rsend(33, out_relay.at[1], far_in.at[second], "pair")
 
     slope_blocks(0, pair_rows)
     for n in range(BLOCKS):
@@ -609,11 +622,6 @@
         oq_ref[1, n % NZ, j] = qacc[n].astype(BF)
     z_start(1)
     key_grads(0, pair_rows)
-    part[3] = project(head)
-    rarrived(31, out_relay.at[1])
-    rsend(33, out_relay.at[1], far_in.at[second], "pair")
-    rarrived(30, out_relay.at[0])
-    rsend(32, out_relay.at[0], far_in.at[first], "back")
     z_relay(1)
     for t in range(2):
         yk_out[t] = x_total(t, 1).astype(BF)
@@ -656,14 +664,21 @@
 
 
 def store_kernel(*refs):
-    count = len(refs) // 2
-    sems = refs[-1]
-    copies = [
-        pltpu.make_async_copy(refs[n], refs[count + n], sems.at[n]) for n in range(count)
+    count = (len(refs) - 2) // 3
+    held, result, buffers = refs[:count], refs[count : 2 * count], refs[2 * count : 3 * count]
+    load_sem, store_sem = refs[-2:]
+    loads = [
+        pltpu.make_async_copy(held[n], buffers[n], load_sem.at[n]) for n in range(count)
     ]
-    for copy in copies:
+    stores = [
+        pltpu.make_async_copy(buffers[n], result[n], store_sem.at[n]) for n in range(count)
+    ]
+    for copy in loads:
         copy.start()
-    for copy in copies:
+    for load, copy in zip(loads, stores):
+        load.wait()
+        copy.start()
+    for copy in stores:
         copy.wait()
 
 
@@ -783,7 +798,8 @@
         out_shape=result,
         in_specs=[hbm] * len(result),
         out_specs=(hbm,) * len(result),
-        scratch_shapes=[dma((len(result),))],
+        scratch_shapes=[pltpu.VMEM(array.shape, array.dtype) for array in result]
+        + [dma((len(result),)), dma((len(result),))],
         compiler_params=pltpu.CompilerParams(vmem_limit_bytes=VMEM_LIMIT),
     )(*held)
 

time: 126 us -> 95 us (0.75)
  Pallas kernels: 125 us -> 93 us
    pallas_call x1, Pallas kernels: 31.7 us -> 2.04 us  [shards(): pl.pallas_call(store_kernel, out_shape=result, in_specs=[hbm] * len(resul...]
    pallas_call x1, Pallas kernels: 93 us -> 91 us  [shards(): pl.pallas_call(fused_kernel, out_shape=result, in_specs=[hbm] * 9 + [smem...]
where the time goes in v4:
time: 95 us; the launch traced here: 93.8 us
  Pallas kernels  93 us (98%)
    pallas_call x1, Pallas kernels, shards(): pl.pallas_call(fused_kernel, out_shape=result, in_specs=[hbm] * 9 + [smem...  91 us
    pallas_call x1, Pallas kernels, shards(): pl.pallas_call(store_kernel, out_shape=result, in_specs=[hbm] * len(resul...  2.04 us

profile of v4, /device:TPU:0, one launch (start us, length us, event | category | flops | bytes accessed | tf_op | source)
XLA Modules:
  0.0 93.8 jit_solution(5348208161958309940)
XLA Ops:
  0.6 91.0 %shard_map.154 = (bf16[256,768]{1,0:T(8,128)(2,1)}, bf16[256,384]{1,0:T(8,128)(2,1)}, bf16[256,384]{1,0:T(8,128)(2,1)}, bf16[256,384]{1,0:T(8,128)(2,1)}, bf16[1...) custom-call(bf16[256,384]{1,0:T(8,128)(2,1)} %q_hbm.1, bf16[256,384]{1,0:T(8,128)(2,1)} %k_hbm.1, bf16[256,384]{1,0:T(8,128)(2,1)} %v_hbm.1, ...), custom_call_target="tpu_custom_call" | custom-call | tf_op jit(solution)/shard_map/pallas_call | solution.py:719
  91.6 2.0 %shard_map.155 = (bf16[256,768]{1,0:T(8,128)(2,1)}, bf16[256,384]{1,0:T(8,128)(2,1)}, bf16[256,384]{1,0:T(8,128)(2,1)}, bf16[256,384]{1,0:T(8,128)(2,1)}, bf16[1...) custom-call(bf16[256,768]{1,0:T(8,128)(2,1)} %get-tuple-element.12.refs_0_, bf16[256,384]{1,0:T(8,128)(2,1)} %get-tuple-element.13.refs_1_, ...), custom_call_target="tpu_custom_call" | custom-call | tf_op jit(solution)/shard_map/pallas_call | solution.py:796

commit v5 on v4

--- a/solution.py
+++ b/solution.py
@@ -181,7 +181,6 @@
     by_y = lambda a, b: jnp.where(y == 0, a, b)
     wide = lambda a: a.astype(F32)
     factor = HS ** (-0.5)
-    log2e = 1.4426950408889634
 
     load = []
     for n, (src, dst) in enumerate(
@@ -353,13 +352,12 @@
 
     def weigh(n, slot, first_row, count):
         scores = dot_nt(qaug[n], kaug[slot, first_row : first_row + count, :])
-        e = jnp.exp2(jnp.minimum(scores * (factor * log2e), 115.0))
-        rest = pl.reciprocal(1.0 + e, approx=True)
-        sig = e * rest
-        weight = sig.astype(BF)
+        half = jnp.tanh(scores * (0.5 * factor))
+        twice = 1.0 + half
+        weight = twice.astype(BF)
         rows = pl.ds(pl.multiple_of(n * TR, TR), TR)
         weights[rows, first_row : first_row + count] = weight
-        slopes[rows, first_row : first_row + count] = (sig * rest).astype(BF)
+        slopes[rows, first_row : first_row + count] = (twice * (1.0 - half)).astype(BF)
         return weight
 
     def per_plane(body):
@@ -385,7 +383,7 @@
     def forward_text():
         def body(n, slot):
             share = dot_nn(weigh(n, slot, LAT, NY * NX * CR), vtext[slot])
-            oq_ref[0, n % NZ, block_j(n)] = (oacc[n] + share).astype(BF)
+            oq_ref[0, n % NZ, block_j(n)] = ((oacc[n] + share) * 0.5).astype(BF)
 
         per_plane(body)
 
@@ -417,7 +415,7 @@
             for t in range(2):
                 left = (queries_t, grads_t)[t][:, low:high]
                 right = (slopes, weights)[t][low:high, first_row : first_row + count]
-                total = dot_nn(left, right).astype(BF)
+                total = (dot_nn(left, right) * (0.25, 0.5)[t]).astype(BF)
                 if first_row == LAT:
                     text_rows = total.T
                     for n in range(NY * NX):
@@ -619,7 +617,7 @@
     slope_blocks(0, pair_rows)
     for n in range(BLOCKS):
         j = 2 if n // NZ == 2 else (y + n // NZ) % NY
-        oq_ref[1, n % NZ, j] = qacc[n].astype(BF)
+        oq_ref[1, n % NZ, j] = (qacc[n] * 0.25).astype(BF)
     z_start(1)
     key_grads(0, pair_rows)
     z_relay(1)

time: 95 us -> 94 us (0.989)
  Pallas kernels: 93 us -> 92 us
    pallas_call x1, Pallas kernels: 91 us -> 90 us  [shards(): pl.pallas_call(fused_kernel, out_shape=result, in_specs=[hbm] * 9 + [smem...]
where the time goes in v5:
time: 94 us; the launch traced here: 92.8 us
  Pallas kernels  92 us (98%)
    pallas_call x1, Pallas kernels, shards(): pl.pallas_call(fused_kernel, out_shape=result, in_specs=[hbm] * 9 + [smem...  90 us
    pallas_call x1, Pallas kernels, shards(): pl.pallas_call(store_kernel, out_shape=result, in_specs=[hbm] * len(resul...  2.04 us

profile of v5, /device:TPU:0, one launch (start us, length us, event | category | flops | bytes accessed | tf_op | source)
XLA Modules:
  0.0 92.8 jit_solution(11144168331566998624)
XLA Ops:
  0.6 90.0 %shard_map.154 = (bf16[256,768]{1,0:T(8,128)(2,1)}, bf16[256,384]{1,0:T(8,128)(2,1)}, bf16[256,384]{1,0:T(8,128)(2,1)}, bf16[256,384]{1,0:T(8,128)(2,1)}, bf16[1...) custom-call(bf16[256,384]{1,0:T(8,128)(2,1)} %q_hbm.1, bf16[256,384]{1,0:T(8,128)(2,1)} %k_hbm.1, bf16[256,384]{1,0:T(8,128)(2,1)} %v_hbm.1, ...), custom_call_target="tpu_custom_call" | custom-call | tf_op jit(solution)/shard_map/pallas_call | solution.py:717
  90.6 2.0 %shard_map.155 = (bf16[256,768]{1,0:T(8,128)(2,1)}, bf16[256,384]{1,0:T(8,128)(2,1)}, bf16[256,384]{1,0:T(8,128)(2,1)}, bf16[256,384]{1,0:T(8,128)(2,1)}, bf16[1...) custom-call(bf16[256,768]{1,0:T(8,128)(2,1)} %get-tuple-element.12.refs_0_, bf16[256,384]{1,0:T(8,128)(2,1)} %get-tuple-element.13.refs_1_, ...), custom_call_target="tpu_custom_call" | custom-call | tf_op jit(solution)/shard_map/pallas_call | solution.py:794

commit v6 on v5

--- a/solution.py
+++ b/solution.py
@@ -23,6 +23,8 @@
 ROWS = NY * NX * BR
 MASKED = -32768.0
 BLOCKS = NH * NZ
+SIDE = NX * TR
+TEXT = NY * NX * CR
 VMEM_LIMIT = 58 * 1024 * 1024
 
 
@@ -134,10 +136,16 @@
     go_relay,
     acc,
     kaug,
+    kaug_own,
+    ktext,
+    vals_own,
+    vtext,
     qaug,
+    gsel,
     weights,
     slopes,
-    vtext,
+    weights_own,
+    slopes_own,
     queries_t,
     grads_t,
     oacc,
@@ -269,9 +277,13 @@
     def feature(n):
         return w_ref[:, pl.ds(pl.multiple_of(n * 768, 128), 768)]
 
+    half_rows = NZ * NX * TR
     ends = [len_ref[0]]
     for c in range(1, CLIPS):
         ends.append(ends[-1] + len_ref[c])
+    long_start = 0
+    for c in range(1, CLIPS):
+        long_start = jnp.where(len_ref[c] == half_rows, ends[c - 1], long_start)
 
     def clip_at(pos):
         total = 0
@@ -279,6 +291,19 @@
             total = total + jnp.where(pos >= ends[c], 1, 0)
         return total
 
+    row_index = lax.broadcasted_iota(jnp.int32, (TR, HS), 0)
+
+    def chunk_rows(zz, xx):
+        return (zz * NX + xx) * TR + row_index
+
+    def own_is_long(zz, xx):
+        t = chunk_rows(zz, xx)
+        return jnp.where(y == 0, t - long_start, long_start - 1 - t) >= 0
+
+    def by_side(mask, mine, other):
+        mine, other = wide(mine), wide(other)
+        return jnp.where(mask, mine, other).astype(BF), jnp.where(mask, other, mine).astype(BF)
+
     lane = lax.broadcasted_iota(jnp.int32, (1, HS), 1)
     tiles_here = (lane % 64) // 16 == z
     clip_lane = ((z + 1) % NZ) * 16
@@ -288,15 +313,22 @@
     def kv_index(n):
         return ((y + n % 2) % NY) * NX + (x + n // 2) % NX
 
+    def key_columns(pos):
+        hit = (tiles_here & ((pos >> 6) == lane)) | (clip_at(pos) == lane - clip_lane)
+        return jnp.where(hit, 1.0, bias_ones).astype(BF)
+
     def key_side():
-        for n in range(NY * NX):
-            pos = kv_index(n) // NX * (NZ * NX * TR) + z * (NX * TR) + kv_index(n) % NX * TR
-            pos = pos + lax.broadcasted_iota(jnp.int32, (TR, HS), 0)
-            hit = (tiles_here & (pos // TILE == lane)) | (clip_at(pos) == lane - clip_lane)
-            aug = jnp.where(hit, 1.0, bias_ones).astype(BF)
-            for s in range(2):
-                kaug[s, n * TR : (n + 1) * TR, HS:] = aug
-        row = lax.broadcasted_iota(jnp.int32, (NY * NX * CR, HS), 0)
+        for d in range(NX):
+            t = chunk_rows(z, (x + d) % NX)
+            low = key_columns(t)
+            high = key_columns(t + half_rows)
+            for r in range(2):
+                n = 2 * d + r
+                plane_zero = (y + r) % NY == 0
+                kaug[n * TR : (n + 1) * TR, HS:] = jnp.where(plane_zero, low, high)
+            for side, value in enumerate(by_side(t >= long_start, low, high)):
+                kaug_own[side, d * TR : (d + 1) * TR, HS:] = value
+        row = lax.broadcasted_iota(jnp.int32, (TEXT, HS), 0)
         n = row // CR
         plane = ((y + n % 2) % NY) * NZ + z
         text_row = (plane * NX + (x + n // 2) % NX) * CR + row % CR
@@ -306,17 +338,19 @@
             found = jnp.max(listed, axis=1, keepdims=True)
             aug = jnp.where(lane == clip_lane + c, found, aug)
         for s in range(2):
-            kaug[s, LAT:, HS:] = aug.astype(BF)
+            ktext[s, :, HS:] = aug.astype(BF)
 
     log_len = [
         jnp.log(jnp.full((1, HS), len_ref[c] + CAP, jnp.int32).astype(F32)) for c in range(CLIPS)
     ]
 
     def query_side(n, carry):
-        yq = jnp.where(n // NZ == 1, 1 - y, y)
-        start = ((yq * NZ + n % NZ) * NX + x) * TR
-        head_bias = bias_ref[jnp.where(n // NZ == 2, 2, y)]
-        pos = start + lax.broadcasted_iota(jnp.int32, (TR, HS), 0)
+        g, zq = n // NZ, n % NZ
+        t = chunk_rows(zq, x)
+        in_high = jnp.where(g == 0, long_start - 1 - t, t - long_start)
+        in_high = jnp.where(g == 2, 2 * y - 1, in_high) >= 0
+        pos = t + jnp.where(in_high, half_rows, 0)
+        head_bias = bias_ref[jnp.where(g == 2, 2, y)]
         clip = clip_at(pos)
         offset = jnp.broadcast_to(log_len[CLIPS - 1], (TR, HS))
         for c in range(CLIPS - 2, -1, -1):
@@ -330,108 +364,221 @@
         in_clip = (lane >= clip_lane) & (lane < clip_lane + CLIPS) & (lane - clip_lane != clip)
         side = jnp.where(in_clip, MASKED, in_bias)
         for u in range(TR // TILE):
-            tile = start // TILE + u
-            off = (tile_ref[pl.ds(tile, 1), :] == 0) & (lane != tile) & tiles_here
             rows = slice(u * TILE, (u + 1) * TILE)
-            qaug[n, rows, HS:] = jnp.where(off, MASKED, side[rows]).astype(BF)
+            tile = (zq * NX + x) * (TR // TILE) + u
+            off = []
+            for p in range(NY):
+                at = tile + p * (half_rows // TILE)
+                mask_row = tile_ref[pl.ds(at, 1), :]
+                off.append(jnp.where((mask_row == 0) & (lane != at) & tiles_here, 1.0, 0.0))
+            masked = jnp.where(in_high[rows], off[1], off[0]) > 0.5
+            qaug[n, rows, HS:] = jnp.where(masked, MASKED, side[rows]).astype(BF)
         return carry
 
-    def block_j(n):
-        return jnp.where(n // NZ == 2, 2, jnp.where(n // NZ == 1, 1 - y, y))
-
-    def take_queries(n):
-        value = qg_ref[0, n % NZ, n // NZ if n // NZ == 2 else (y + n // NZ) % NY]
+    def keep_query(n, value):
         qaug[n, :, 0:HS] = value
         queries_t[:, n * TR : (n + 1) * TR] = value.T
 
+    def keep_grad(n, value):
+        gsel[n] = value
+        grads_t[:, n * TR : (n + 1) * TR] = value.T
+
+    def take_own(t, keep):
+        for zq in range(NZ):
+            mask = own_is_long(zq, x)
+            sides = by_side(mask, qg_ref[t, zq, y], qg_ref[t, zq, 1 - y])
+            for g in range(2):
+                keep(g * NZ + zq, sides[g])
+
+    def take_shared(t, keep):
+        for zq in range(NZ):
+            keep(2 * NZ + zq, qg_ref[t, zq, 2])
+
     def take_key(n):
+        kaug[n * TR : (n + 1) * TR, 0:HS] = kv_ref[0, kv_index(n), 1, 0:TR]
         for s in range(2):
-            kaug[s, n * TR : (n + 1) * TR, 0:HS] = kv_ref[0, kv_index(n), s, 0:TR]
-            kaug[s, LAT + n * CR : LAT + (n + 1) * CR, 0:HS] = kv_ref[0, kv_index(n), s, TR:BR]
+            ktext[s, n * CR : (n + 1) * CR, 0:HS] = kv_ref[0, kv_index(n), s, TR:BR]
             vtext[s, n * CR : (n + 1) * CR] = kv_ref[1, kv_index(n), s, TR:BR]
 
-    def weigh(n, slot, first_row, count):
-        scores = dot_nt(qaug[n], kaug[slot, first_row : first_row + count, :])
+    def take_key_own(d):
+        mask = own_is_long(z, (x + d) % NX)
+        mine, other = kv_index(2 * d), kv_index(2 * d + 1)
+        rows = slice(d * TR, (d + 1) * TR)
+        for side, value in enumerate(by_side(mask, kv_ref[0, mine, 0, 0:TR], kv_ref[0, other, 0, 0:TR])):
+            kaug_own[side, rows, 0:HS] = value
+        for side, value in enumerate(by_side(mask, kv_ref[1, mine, 0, 0:TR], kv_ref[1, other, 0, 0:TR])):
+            vals_own[side, rows, :] = value
+
+    def weigh(n, keys, weight_ref, slope_ref, rows, columns):
+        scores = dot_nt(qaug[n], keys)
         half = jnp.tanh(scores * (0.5 * factor))
         twice = 1.0 + half
         weight = twice.astype(BF)
-        rows = pl.ds(pl.multiple_of(n * TR, TR), TR)
-        weights[rows, first_row : first_row + count] = weight
-        slopes[rows, first_row : first_row + count] = (twice * (1.0 - half)).astype(BF)
+        weight_ref[rows, columns] = weight
+        slope_ref[rows, columns] = (twice * (1.0 - half)).astype(BF)
         return weight
 
-    def per_plane(body):
+    def block_rows(n):
+        return pl.ds(pl.multiple_of(n * TR, TR), TR)
+
+    def forward(n, fresh=False):
+        take_key(n)
+        columns = slice(n * TR, (n + 1) * TR)
+
+        def step(half, carry):
+            for u in range(2):
+                zq = 2 * half + u
+                block = 2 * NZ + zq
+                weight = weigh(block, kaug[columns, :], weights, slopes, block_rows(zq), columns)
+                share = dot_nn(weight, kv_ref[1, kv_index(n), 1, 0:TR])
+                if fresh:
+                    oacc[block] = share
+                else:
+                    oacc[block] += share
+            return carry
+
+        lax.fori_loop(0, NZ // 2, step, 0)
+
+    def forward_own(d, fresh=False):
+        take_key_own(d)
+        columns = slice(d * TR, (d + 1) * TR)
+
         def step(zq, carry):
-            for g in range(NH):
-                body(g * NZ + zq, g // 2)
+            for g in range(2):
+                block = g * NZ + zq
+                keys = kaug_own[g, columns, :]
+                weight = weigh(block, keys, weights_own, slopes_own, block_rows(block), columns)
+                share = dot_nn(weight, vals_own[g, columns, :])
+                if fresh:
+                    oacc[block] = share
+                else:
+                    oacc[block] += share
             return carry
 
         lax.fori_loop(0, NZ, step, 0)
 
-    def forward(c, fresh=False):
-        take_key(c)
-
-        def body(n, slot):
-            share = dot_nn(weigh(n, slot, c * TR, TR), kv_ref[1, kv_index(c), slot, 0:TR])
-            if fresh:
-                oacc[n] = share
+    own_text = slice(SIDE, SIDE + TEXT)
+    shared_text = slice(LAT, LAT + TEXT)
+
+    def forward_text(zq):
+        totals = []
+        for g in range(NH):
+            block = g * NZ + zq
+            if g == 2:
+                weight = weigh(block, ktext[1], weights, slopes, block_rows(zq), shared_text)
             else:
-                oacc[n] += share
-
-        per_plane(body)
-
-    def forward_text():
-        def body(n, slot):
-            share = dot_nn(weigh(n, slot, LAT, NY * NX * CR), vtext[slot])
-            oq_ref[0, n % NZ, block_j(n)] = ((oacc[n] + share) * 0.5).astype(BF)
-
-        per_plane(body)
-
-    def slope_blocks(first_row, count):
-        def body(n, slot):
-            rows = pl.ds(pl.multiple_of(n * TR, TR), TR)
-            slope = wide(slopes[rows, first_row : first_row + count])
-            grads = qg_ref[1, n % NZ, block_j(n)]
-            if first_row == LAT:
-                vals = vtext[slot]
+                weight = weigh(block, ktext[0], weights_own, slopes_own, block_rows(block), own_text)
+            totals.append((oacc[block] + dot_nn(weight, vtext[g // 2])) * 0.5)
+        mine, other = by_side(own_is_long(zq, x), totals[0], totals[1])
+        oq_ref[0, zq, y] = mine
+        oq_ref[0, zq, 1 - y] = other
+        oq_ref[0, zq, 2] = totals[2].astype(BF)
+
+    def slope_step(block, slope_ref, rows, columns, vals, keys, fresh):
+        slope = (dot_nt(gsel[block], vals) * wide(slope_ref[rows, columns])).astype(BF)
+        slope_ref[rows, columns] = slope
+        share = dot_nn(slope, keys)
+        if fresh:
+            qacc[block] = share
+        else:
+            qacc[block] += share
+
+    def slope_shared(d):
+        columns = slice(d * 2 * TR, (d + 1) * 2 * TR)
+
+        def step(zq, carry):
+            vals = jnp.concatenate(
+                [kv_ref[1, kv_index(2 * d + r), 1, 0:TR] for r in range(2)], axis=0
+            )
+            keys = kaug[columns, 0:HS]
+            slope_step(2 * NZ + zq, slopes, block_rows(zq), columns, vals, keys, False)
+            return carry
+
+        lax.fori_loop(0, NZ, step, 0)
+
+    def slope_shared_text():
+        def step(zq, carry):
+            rows = block_rows(zq)
+            slope_step(2 * NZ + zq, slopes, rows, shared_text, vtext[1], ktext[1, :, 0:HS], True)
+            return carry
+
+        lax.fori_loop(0, NZ, step, 0)
+
+    def slope_own_row(d, zq):
+        columns = slice(d * TR, (d + 1) * TR)
+        for g in range(2):
+            block = g * NZ + zq
+            vals, keys = vals_own[g, columns, :], kaug_own[g, columns, 0:HS]
+            slope_step(block, slopes_own, block_rows(block), columns, vals, keys, False)
+
+    def slope_own(d):
+        def step(half, carry):
+            for u in range(2):
+                slope_own_row(d, 2 * half + u)
+            return carry
+
+        lax.fori_loop(0, NZ // 2, step, 0)
+
+    def slope_own_text():
+        def step(half, carry):
+            for u in range(2):
+                for g in range(2):
+                    block = g * NZ + 2 * half + u
+                    rows = block_rows(block)
+                    slope_step(block, slopes_own, rows, own_text, vtext[0], ktext[0, :, 0:HS], True)
+            return carry
+
+        lax.fori_loop(0, NZ // 2, step, 0)
+
+    def finish_dq(zq):
+        mine, other = by_side(own_is_long(zq, x), qacc[zq] * 0.25, qacc[NZ + zq] * 0.25)
+        oq_ref[1, zq, y] = mine
+        oq_ref[1, zq, 1 - y] = other
+        oq_ref[1, zq, 2] = (qacc[2 * NZ + zq] * 0.25).astype(BF)
+
+    left_of = (queries_t, grads_t)
+    scale_of = (0.25, 0.5)
+
+    def key_grads_shared(d):
+        for t in range(2):
+            right = (slopes, weights)[t][:, d * 2 * TR : (d + 1) * 2 * TR]
+            total = (dot_nn(left_of[t][:, 2 * NZ * TR :], right) * scale_of[t]).astype(BF)
+            for r in range(2):
+                kvg_ref[t, kv_index(2 * d + r), 1, 0:TR] = total[:, r * TR : (r + 1) * TR].T
+
+    def key_grads_own(d):
+        mask = own_is_long(z, (x + d) % NX)
+        for t in range(2):
+            sides = []
+            for g in range(2):
+                rows = slice(g * SIDE, (g + 1) * SIDE)
+                right = (slopes_own, weights_own)[t][rows, d * TR : (d + 1) * TR]
+                total = dot_nn(left_of[t][:, rows], right) * scale_of[t]
+                sides.append(total.astype(BF).T)
+            mine, other = by_side(mask, sides[0], sides[1])
+            kvg_ref[t, kv_index(2 * d), 0, 0:TR] = mine
+            kvg_ref[t, kv_index(2 * d + 1), 0, 0:TR] = other
+
+    def key_grads_text(s):
+        for t in range(2):
+            if s == 0:
+                left = left_of[t][:, 0 : 2 * NZ * TR]
+                right = (slopes_own, weights_own)[t][:, own_text]
             else:
-                c = first_row // TR
-                vals = jnp.concatenate(
-                    [kv_ref[1, kv_index(c + r), slot, 0:TR] for r in range(2)], axis=0
-                )
-            product = dot_nt(grads, vals)
-            slope = (product * slope).astype(BF)
-            slopes[rows, first_row : first_row + count] = slope
-            share = dot_nn(slope, kaug[slot, first_row : first_row + count, 0:HS])
-            if first_row == LAT:
-                qacc[n] = share
-            else:
-                qacc[n] += share
-
-        per_plane(body)
-
-    def key_grads(first_row, count):
-        for s, (low, high) in enumerate(((0, 2 * NZ * TR), (2 * NZ * TR, BLOCKS * TR))):
-            for t in range(2):
-                left = (queries_t, grads_t)[t][:, low:high]
-                right = (slopes, weights)[t][low:high, first_row : first_row + count]
-                total = (dot_nn(left, right) * (0.25, 0.5)[t]).astype(BF)
-                if first_row == LAT:
-                    text_rows = total.T
-                    for n in range(NY * NX):
-                        kvg_ref[t, kv_index(n), s, TR:BR] = text_rows[n * CR : (n + 1) * CR]
-                else:
-                    for r in range(2):
-                        n = first_row // TR + r
-                        kvg_ref[t, kv_index(n), s, 0:TR] = total[:, r * TR : (r + 1) * TR].T
-
-
-    def z_start(t):
-        base = 6 * t
-        rsend(base + 0, oq_ref.at[t, zf, :, first], z_in.at[t, 0], "up")
-        rsend(base + 3, oq_ref.at[t, zf, :, second], z_in.at[t, 3], "down")
-        rsend(base + 1, oq_ref.at[t, zd, :, first], z_in.at[t, 1], "down")
-        rsend(base + 4, oq_ref.at[t, zu, :, second], z_in.at[t, 4], "up")
+                left = left_of[t][:, 2 * NZ * TR :]
+                right = (slopes, weights)[t][:, shared_text]
+            text_rows = (dot_nn(left, right) * scale_of[t]).astype(BF).T
+            for n in range(NY * NX):
+                kvg_ref[t, kv_index(n), s, TR:BR] = text_rows[n * CR : (n + 1) * CR]
+
+
+    def z_far(t):
+        rsend(6 * t + 0, oq_ref.at[t, zf, :, first], z_in.at[t, 0], "up")
+        rsend(6 * t + 3, oq_ref.at[t, zf, :, second], z_in.at[t, 3], "down")
+
+    def z_near(t):
+        rsend(6 * t + 1, oq_ref.at[t, zd, :, first], z_in.at[t, 1], "down")
+        rsend(6 * t + 4, oq_ref.at[t, zu, :, second], z_in.at[t, 4], "up")
 
     def z_relay(t):
         base = 6 * t
@@ -527,12 +674,13 @@
     send(0, go_hbm.at[first], go_relay.at[0], "pair")
     z_own_finish(0)
     z_pair_finish(0)
-    for n in range(BLOCKS):
-        take_queries(n)
+    take_shared(0, keep_query)
+    take_own(0, keep_query)
     forward(0, True)
     arrived(2, goall.at[core_head])
     acc[...] += dot_nt(goall[core_head], feature(core_head))
     forward(1)
+    forward_own(0, True)
     arrived(0, go_relay.at[0])
     send(3, go_relay.at[0], goall.at[head, first], "back")
     arrived(1, go_relay.at[1])
@@ -549,6 +697,7 @@
     acc[...] += dot_nt(goall[other_head], feature(other_head))
     x_near_finish(1, 1 - y)
     forward(3)
+    forward_own(1)
     arrived(5, goall.at[core_other])
     grad = (acc[...] + dot_nt(goall[core_other], feature(core_other))).astype(BF)
     q_pair[1] = by_y(grad[:, cols(1)], grad[:, cols(0)])
@@ -557,32 +706,42 @@
     qg_ref[1, z, 2] = grad[:, cols(2)]
     z_own(1)
     forward(7)
-    x_far_finish(1, 1 - y)
-    forward(5)
+    forward_own(3)
     arrived(9, qg_ref.at[1, z, 1 - y])
     z_pair(1)
     z_own_forward(1)
-    forward_text()
-    z_start(0)
+    x_far_finish(1, 1 - y)
+    forward(5)
+    forward_own(2)
+    forward_text(zf)
+    z_far(0)
+    forward_text(zu)
+    forward_text(zd)
+    z_near(0)
+    forward_text(z)
     z_pair_forward(1)
 
     z_own_finish(1)
-    for n in (0, 1, 2, 3, 8, 9, 10, 11, 4, 5, 6, 7):
-        if n == NZ:
-            z_relay(0)
-            z_pair_finish(1)
-        j = 2 if n // NZ == 2 else (y + n // NZ) % NY
-        grads_t[:, n * TR : (n + 1) * TR] = qg_ref[1, n % NZ, j].T
-    slope_blocks(LAT, NY * NX * CR)
-    key_grads(LAT, NY * NX * CR)
-    pair_rows = 2 * TR
-
-    slope_blocks(2 * pair_rows, pair_rows)
-    z_total(0, 1.0)
-    key_grads(2 * pair_rows, pair_rows)
+    take_shared(1, keep_grad)
+    slope_shared_text()
+    z_relay(0)
+    for d in (2, 1):
+        slope_shared(d)
+    z_pair_finish(1)
+    take_own(1, keep_grad)
+    slope_own_text()
+    for s in range(2):
+        key_grads_text(s)
+    slope_own(2)
+    key_grads_own(2)
+    key_grads_shared(2)
     for a in (1, 0):
         for t in range(2):
             x_far(t, a)
+    z_total(0, 1.0)
+    for d in (3, 0):
+        slope_shared(d)
+    slope_own(1)
     rarrived(24, yq_in.at[0])
     attn[:, cols(0)] = by_y(keep_q[0, 0], yq_in[0])
     attn[:, cols(1)] = by_y(yq_in[0], keep_q[0, 0])
@@ -590,37 +749,39 @@
     part[0] = project(core_other)
     rsend(28, part.at[0], core_in.at[0], "core")
     part[2] = project(other_head)
-    part[1] = project(core_head)
+    key_grads_own(1)
+    key_grads_shared(1)
     rarrived(28, core_in.at[0])
     pair_sum[...] = (wide(part[2]) + wide(core_in[0])).astype(BF)
     rsend(30, pair_sum.at[first], out_relay.at[0], "pair")
     rsend(31, pair_sum.at[second], out_relay.at[1], "back")
-    rsend(29, part.at[1], core_in.at[1], "core")
-
-    slope_blocks(1 * pair_rows, pair_rows)
-    key_grads(1 * pair_rows, pair_rows)
     for a in (1, 0):
         x_near(1, a)
         x_relay(0, a)
-    part[3] = project(head)
-
-    slope_blocks(3 * pair_rows, pair_rows)
-    key_grads(3 * pair_rows, pair_rows)
+    part[1] = project(core_head)
+    rsend(29, part.at[1], core_in.at[1], "core")
+
+    slope_own(3)
+    key_grads_own(3)
+    key_grads_shared(3)
     for a in (1, 0):
         x_near(0, a)
         x_relay(1, a)
+    part[3] = project(head)
+    for zq in (zf, zu, zd, z):
+        slope_own_row(0, zq)
+        finish_dq(zq)
+        if zq is zf:
+            z_far(1)
+        elif zq is zd:
+            z_near(1)
     rarrived(30, out_relay.at[0])
     rsend(32, out_relay.at[0], far_in.at[first], "back")
     rarrived(31, out_relay.at[1])
     rsend(33, out_relay.at[1], far_in.at[second], "pair")
-
-    slope_blocks(0, pair_rows)
-    for n in range(BLOCKS):
-        j = 2 if n // NZ == 2 else (y + n // NZ) % NY
-        oq_ref[1, n % NZ, j] = (qacc[n] * 0.25).astype(BF)
-    z_start(1)
-    key_grads(0, pair_rows)
     z_relay(1)
+    key_grads_own(0)
+    key_grads_shared(0)
     for t in range(2):
         yk_out[t] = x_total(t, 1).astype(BF)
         rsend(26 + t, yk_out.at[t], yk_in.at[t], "pair")
@@ -742,11 +903,17 @@
             pltpu.VMEM((4, TR, out_cols), BF),
             halves,
             pltpu.VMEM((TR, NH * HS), F32),
-            pltpu.VMEM((2, ROWS, 2 * HS), BF),
+            pltpu.VMEM((LAT, 2 * HS), BF),
+            pltpu.VMEM((2, SIDE, 2 * HS), BF),
+            pltpu.VMEM((2, TEXT, 2 * HS), BF),
+            pltpu.VMEM((2, SIDE, HS), BF),
+            pltpu.VMEM((2, TEXT, HS), BF),
             pltpu.VMEM((BLOCKS, TR, 2 * HS), BF),
-            pltpu.VMEM((BLOCKS * TR, ROWS), BF),
-            pltpu.VMEM((BLOCKS * TR, ROWS), BF),
-            pltpu.VMEM((2, NY * NX * CR, HS), BF),
+            pltpu.VMEM((BLOCKS, TR, HS), BF),
+            pltpu.VMEM((NZ * TR, LAT + TEXT), BF),
+            pltpu.VMEM((NZ * TR, LAT + TEXT), BF),
+            pltpu.VMEM((2 * NZ * TR, SIDE + TEXT), BF),
+            pltpu.VMEM((2 * NZ * TR, SIDE + TEXT), BF),
             pltpu.VMEM((HS, BLOCKS * TR), BF),
             pltpu.VMEM((HS, BLOCKS * TR), BF),
             pltpu.VMEM((BLOCKS, TR, HS), F32),

time: 94 us -> 86.3 us (0.918)
  Pallas kernels: 92 us -> 84.8 us
    pallas_call x1, Pallas kernels: 90 us -> 82.8 us  [shards(): pl.pallas_call(fused_kernel, out_shape=result, in_specs=[hbm] * 9 + [smem...]
where the time goes in v6:
time: 86.3 us; the launch traced here: 85.6 us
  Pallas kernels  84.8 us (98%)
    pallas_call x1, Pallas kernels, shards(): pl.pallas_call(fused_kernel, out_shape=result, in_specs=[hbm] * 9 + [smem...  82.8 us
    pallas_call x1, Pallas kernels, shards(): pl.pallas_call(store_kernel, out_shape=result, in_specs=[hbm] * len(resul...  2.04 us

profile of v6, /device:TPU:0, one launch (start us, length us, event | category | flops | bytes accessed | tf_op | source)
XLA Modules:
  0.0 85.6 jit_solution(10245804131253219172)
XLA Ops:
  0.6 82.8 %shard_map.154 = (bf16[256,768]{1,0:T(8,128)(2,1)}, bf16[256,384]{1,0:T(8,128)(2,1)}, bf16[256,384]{1,0:T(8,128)(2,1)}, bf16[256,384]{1,0:T(8,128)(2,1)}, bf16[1...) custom-call(bf16[256,384]{1,0:T(8,128)(2,1)} %q_hbm.1, bf16[256,384]{1,0:T(8,128)(2,1)} %k_hbm.1, bf16[256,384]{1,0:T(8,128)(2,1)} %v_hbm.1, ...), custom_call_target="tpu_custom_call" | custom-call | tf_op jit(solution)/shard_map/pallas_call | solution.py:878
  83.4 2.0 %shard_map.155 = (bf16[256,768]{1,0:T(8,128)(2,1)}, bf16[256,384]{1,0:T(8,128)(2,1)}, bf16[256,384]{1,0:T(8,128)(2,1)}, bf16[256,384]{1,0:T(8,128)(2,1)}, bf16[1...) custom-call(bf16[256,768]{1,0:T(8,128)(2,1)} %get-tuple-element.12.refs_0_, bf16[256,384]{1,0:T(8,128)(2,1)} %get-tuple-element.13.refs_1_, ...), custom_call_target="tpu_custom_call" | custom-call | tf_op jit(solution)/shard_map/pallas_call | solution.py:961

commit v7 on v6

--- a/solution.py
+++ b/solution.py
@@ -139,7 +139,7 @@
     kaug_own,
     ktext,
     vals_own,
-    vtext,
+    vals,
     qaug,
     gsel,
     weights,
@@ -216,23 +216,17 @@
         send(10 + 6 * a + 2 * t, kv_ref.at[t, c], kv_ref.at[t, c], ("right", "left")[t])
         send(11 + 6 * a + 2 * t, kv_ref.at[t, c], kv_ref.at[t, c], ("left", "right")[t])
 
-    def x_forward(a, yy):
+    def x_forward(a, t, yy):
         base = 10 + 6 * a
-        left, right = yy * NX + xl, yy * NX + xr
-        arrived(base + 0, kv_ref.at[0, left])
-        send(base + 4, kv_ref.at[0, left], kv_ref.at[0, left], "right")
-        arrived(base + 2, kv_ref.at[1, right])
-        send(base + 5, kv_ref.at[1, right], kv_ref.at[1, right], "left")
-
-    def x_near_finish(a, yy):
-        base = 10 + 6 * a
-        arrived(base + 1, kv_ref.at[0, yy * NX + xr])
-        arrived(base + 3, kv_ref.at[1, yy * NX + xl])
-
-    def x_far_finish(a, yy):
-        base = 10 + 6 * a
-        arrived(base + 4, kv_ref.at[0, yy * NX + xf])
-        arrived(base + 5, kv_ref.at[1, yy * NX + xf])
+        source = yy * NX + (xl, xr)[t]
+        arrived(base + 2 * t, kv_ref.at[t, source])
+        send(base + 4 + t, kv_ref.at[t, source], kv_ref.at[t, source], ("right", "left")[t])
+
+    def x_near_finish(a, t, yy):
+        arrived(10 + 6 * a + 1 + 2 * t, kv_ref.at[t, yy * NX + (xr, xl)[t]])
+
+    def x_far_finish(a, t, yy):
+        arrived(10 + 6 * a + 4 + t, kv_ref.at[t, yy * NX + xf])
 
     def z_own(t):
         base = 22 + 10 * t
@@ -398,16 +392,20 @@
         kaug[n * TR : (n + 1) * TR, 0:HS] = kv_ref[0, kv_index(n), 1, 0:TR]
         for s in range(2):
             ktext[s, n * CR : (n + 1) * CR, 0:HS] = kv_ref[0, kv_index(n), s, TR:BR]
-            vtext[s, n * CR : (n + 1) * CR] = kv_ref[1, kv_index(n), s, TR:BR]
-
-    def take_key_own(d):
+
+    def take_value(n):
+        vals[n * TR : (n + 1) * TR] = kv_ref[1, kv_index(n), 1, 0:TR]
+        vals[LAT + n * CR : LAT + (n + 1) * CR] = kv_ref[1, kv_index(n), 1, TR:BR]
+        for g in range(2):
+            rows = slice(SIDE + n * CR, SIDE + (n + 1) * CR)
+            vals_own[g, rows] = kv_ref[1, kv_index(n), 0, TR:BR]
+
+    def take_sides(t, d, ref, lanes):
         mask = own_is_long(z, (x + d) % NX)
         mine, other = kv_index(2 * d), kv_index(2 * d + 1)
-        rows = slice(d * TR, (d + 1) * TR)
-        for side, value in enumerate(by_side(mask, kv_ref[0, mine, 0, 0:TR], kv_ref[0, other, 0, 0:TR])):
-            kaug_own[side, rows, 0:HS] = value
-        for side, value in enumerate(by_side(mask, kv_ref[1, mine, 0, 0:TR], kv_ref[1, other, 0, 0:TR])):
-            vals_own[side, rows, :] = value
+        sides = by_side(mask, kv_ref[t, mine, 0, 0:TR], kv_ref[t, other, 0, 0:TR])
+        for side, value in enumerate(sides):
+            ref[side, d * TR : (d + 1) * TR, lanes] = value
 
     def weigh(n, keys, weight_ref, slope_ref, rows, columns):
         scores = dot_nt(qaug[n], keys)
@@ -421,38 +419,28 @@
     def block_rows(n):
         return pl.ds(pl.multiple_of(n * TR, TR), TR)
 
-    def forward(n, fresh=False):
+    def score(n):
         take_key(n)
         columns = slice(n * TR, (n + 1) * TR)
 
         def step(half, carry):
             for u in range(2):
                 zq = 2 * half + u
-                block = 2 * NZ + zq
-                weight = weigh(block, kaug[columns, :], weights, slopes, block_rows(zq), columns)
-                share = dot_nn(weight, kv_ref[1, kv_index(n), 1, 0:TR])
-                if fresh:
-                    oacc[block] = share
-                else:
-                    oacc[block] += share
+                rows = block_rows(zq)
+                weigh(2 * NZ + zq, kaug[columns, :], weights, slopes, rows, columns)
             return carry
 
         lax.fori_loop(0, NZ // 2, step, 0)
 
-    def forward_own(d, fresh=False):
-        take_key_own(d)
+    def score_own(d):
+        take_sides(0, d, kaug_own, slice(0, HS))
         columns = slice(d * TR, (d + 1) * TR)
 
         def step(zq, carry):
             for g in range(2):
                 block = g * NZ + zq
                 keys = kaug_own[g, columns, :]
-                weight = weigh(block, keys, weights_own, slopes_own, block_rows(block), columns)
-                share = dot_nn(weight, vals_own[g, columns, :])
-                if fresh:
-                    oacc[block] = share
-                else:
-                    oacc[block] += share
+                weigh(block, keys, weights_own, slopes_own, block_rows(block), columns)
             return carry
 
         lax.fori_loop(0, NZ, step, 0)
@@ -460,22 +448,50 @@
     own_text = slice(SIDE, SIDE + TEXT)
     shared_text = slice(LAT, LAT + TEXT)
 
-    def forward_text(zq):
+    def score_text():
+        def step(zq, carry):
+            for g in range(NH):
+                block = g * NZ + zq
+                if g == 2:
+                    weigh(block, ktext[1], weights, slopes, block_rows(zq), shared_text)
+                else:
+                    weigh(block, ktext[0], weights_own, slopes_own, block_rows(block), own_text)
+            return carry
+
+        lax.fori_loop(0, NZ, step, 0)
+
+    def mix(block, low, high):
+        g, zq = block
+        if g == 2:
+            columns = slice(low * 2 * TR, high * 2 * TR)
+            return dot_nn(weights[block_rows(zq), columns], vals[columns, :])
+        columns = slice(low * TR, high * TR)
+        return dot_nn(weights_own[block_rows(g * NZ + zq), columns], vals_own[g, columns, :])
+
+    def mix_near():
+        def step(zq, carry):
+            for g in range(NH):
+                oacc[g * NZ + zq] = mix((g, zq), 0, 2) + mix((g, zq), 3, 4)
+            return carry
+
+        lax.fori_loop(0, NZ, step, 0)
+
+    def mix_far(zq):
         totals = []
         for g in range(NH):
-            block = g * NZ + zq
             if g == 2:
-                weight = weigh(block, ktext[1], weights, slopes, block_rows(zq), shared_text)
+                text = dot_nn(weights[block_rows(zq), shared_text], vals[LAT:, :])
             else:
-                weight = weigh(block, ktext[0], weights_own, slopes_own, block_rows(block), own_text)
-            totals.append((oacc[block] + dot_nn(weight, vtext[g // 2])) * 0.5)
+                rows = block_rows(g * NZ + zq)
+                text = dot_nn(weights_own[rows, own_text], vals_own[g, SIDE:, :])
+            totals.append((oacc[g * NZ + zq] + mix((g, zq), 2, 3) + text) * 0.5)
         mine, other = by_side(own_is_long(zq, x), totals[0], totals[1])
         oq_ref[0, zq, y] = mine
         oq_ref[0, zq, 1 - y] = other
         oq_ref[0, zq, 2] = totals[2].astype(BF)
 
-    def slope_step(block, slope_ref, rows, columns, vals, keys, fresh):
-        slope = (dot_nt(gsel[block], vals) * wide(slope_ref[rows, columns])).astype(BF)
+    def slope_step(block, slope_ref, rows, columns, values, keys, fresh):
+        slope = (dot_nt(gsel[block], values) * wide(slope_ref[rows, columns])).astype(BF)
         slope_ref[rows, columns] = slope
         share = dot_nn(slope, keys)
         if fresh:
@@ -483,33 +499,36 @@
         else:
             qacc[block] += share
 
-    def slope_shared(d):
-        columns = slice(d * 2 * TR, (d + 1) * 2 * TR)
-
-        def step(zq, carry):
-            vals = jnp.concatenate(
-                [kv_ref[1, kv_index(2 * d + r), 1, 0:TR] for r in range(2)], axis=0
-            )
-            keys = kaug[columns, 0:HS]
-            slope_step(2 * NZ + zq, slopes, block_rows(zq), columns, vals, keys, False)
+    def slope_shared(n, fresh=False):
+        columns = slice(n * TR, (n + 1) * TR)
+
+        def step(half, carry):
+            for u in range(2):
+                zq = 2 * half + u
+                keys = kaug[columns, 0:HS]
+                rows = block_rows(zq)
+                slope_step(2 * NZ + zq, slopes, rows, columns, vals[columns, :], keys, fresh)
             return carry
 
-        lax.fori_loop(0, NZ, step, 0)
+        lax.fori_loop(0, NZ // 2, step, 0)
 
     def slope_shared_text():
-        def step(zq, carry):
-            rows = block_rows(zq)
-            slope_step(2 * NZ + zq, slopes, rows, shared_text, vtext[1], ktext[1, :, 0:HS], True)
+        def step(half, carry):
+            for u in range(2):
+                zq = 2 * half + u
+                keys = ktext[1, :, 0:HS]
+                rows = block_rows(zq)
+                slope_step(2 * NZ + zq, slopes, rows, shared_text, vals[LAT:, :], keys, False)
             return carry
 
-        lax.fori_loop(0, NZ, step, 0)
+        lax.fori_loop(0, NZ // 2, step, 0)
 
     def slope_own_row(d, zq):
         columns = slice(d * TR, (d + 1) * TR)
         for g in range(2):
             block = g * NZ + zq
-            vals, keys = vals_own[g, columns, :], kaug_own[g, columns, 0:HS]
-            slope_step(block, slopes_own, block_rows(block), columns, vals, keys, False)
+            side_vals, keys = vals_own[g, columns, :], kaug_own[g, columns, 0:HS]
+            slope_step(block, slopes_own, block_rows(block), columns, side_vals, keys, False)
 
     def slope_own(d):
         def step(half, carry):
@@ -525,7 +544,8 @@
                 for g in range(2):
                     block = g * NZ + 2 * half + u
                     rows = block_rows(block)
-                    slope_step(block, slopes_own, rows, own_text, vtext[0], ktext[0, :, 0:HS], True)
+                    keys = ktext[0, :, 0:HS]
+                    slope_step(block, slopes_own, rows, own_text, vals_own[g, SIDE:, :], keys, True)
             return carry
 
         lax.fori_loop(0, NZ // 2, step, 0)
@@ -642,6 +662,7 @@
     qg_ref[0, z, 2] = q_ref[:, cols(2)]
     z_own(0)
     c = y * NX + x
+    pair_y = 1 - y
     for t, (ref, text) in enumerate(((k_ref, tk_ref), (v_ref, tv_ref))):
         load[2 * t].wait()
         load[2 * t + 1].wait()
@@ -649,7 +670,9 @@
         st_pair[t, 0, TR:BR] = by_y(text[:, cols(1)], text[:, cols(0)])
         st_pair[t, 1, 0:TR] = ref[:, cols(2)]
         st_pair[t, 1, TR:BR] = text[:, cols(2)]
-        send(7 + t, st_pair.at[t], kv_ref.at[t, c], "pair")
+        if t == 0:
+            send(7, st_pair.at[0], kv_ref.at[0, c], "pair")
+            send(0, go_hbm.at[first], go_relay.at[0], "pair")
         kv_ref[t, c, 0, 0:TR] = by_y(ref[:, cols(0)], ref[:, cols(1)])
         kv_ref[t, c, 0, TR:BR] = by_y(text[:, cols(0)], text[:, cols(1)])
         kv_ref[t, c, 1, 0:TR] = ref[:, cols(2)]
@@ -660,44 +683,44 @@
     load[8].wait()
     key_side()
     lax.fori_loop(0, BLOCKS, query_side, 0)
+    arrived(1, go_relay.at[1])
+    send(4, go_relay.at[1], goall.at[other_head, second], "pair")
     z_own_forward(0)
     arrived(6, qg_ref.at[0, z, 1 - y])
     z_pair(0)
+    arrived(7, kv_ref.at[0, pair_y * NX + x])
+    x_send(1, 0, pair_y)
     load[5].wait()
     load[6].wait()
     acc[...] = dot_nt(go_ref[...], feature(head))
-    x_forward(0, y)
+    x_forward(0, 0, y)
+    x_forward(0, 1, y)
     z_pair_forward(0)
-    for t in range(2):
-        arrived(7 + t, kv_ref.at[t, (1 - y) * NX + x])
-        x_send(1, t, 1 - y)
-    send(0, go_hbm.at[first], go_relay.at[0], "pair")
     z_own_finish(0)
+    take_shared(0, keep_query)
+    score(0)
+    score(1)
     z_pair_finish(0)
-    take_shared(0, keep_query)
     take_own(0, keep_query)
-    forward(0, True)
+    arrived(0, go_relay.at[0])
+    send(3, go_relay.at[0], goall.at[head, first], "back")
+    send(8, st_pair.at[1], kv_ref.at[1, c], "pair")
+    x_forward(1, 0, pair_y)
+    score_own(0)
     arrived(2, goall.at[core_head])
     acc[...] += dot_nt(goall[core_head], feature(core_head))
-    forward(1)
-    forward_own(0, True)
-    arrived(0, go_relay.at[0])
-    send(3, go_relay.at[0], goall.at[head, first], "back")
-    arrived(1, go_relay.at[1])
-    send(4, go_relay.at[1], goall.at[other_head, second], "pair")
-    x_near_finish(0, y)
-    x_far_finish(0, y)
-    forward(2)
-    forward(6)
-    x_forward(1, 1 - y)
-    forward(4)
+    x_near_finish(0, 0, y)
+    x_far_finish(0, 0, y)
+    score(2)
+    score(6)
+    score(4)
     arrived(3, goall.at[other_head, first])
     arrived(4, goall.at[other_head, second])
     send(5, goall.at[other_head], goall.at[other_head], "core")
     acc[...] += dot_nt(goall[other_head], feature(other_head))
-    x_near_finish(1, 1 - y)
-    forward(3)
-    forward_own(1)
+    x_near_finish(1, 0, pair_y)
+    score(3)
+    score_own(1)
     arrived(5, goall.at[core_other])
     grad = (acc[...] + dot_nt(goall[core_other], feature(core_other))).astype(BF)
     q_pair[1] = by_y(grad[:, cols(1)], grad[:, cols(0)])
@@ -705,43 +728,64 @@
     qg_ref[1, z, y] = by_y(grad[:, cols(0)], grad[:, cols(1)])
     qg_ref[1, z, 2] = grad[:, cols(2)]
     z_own(1)
-    forward(7)
-    forward_own(3)
+    arrived(8, kv_ref.at[1, pair_y * NX + x])
+    x_send(1, 1, pair_y)
+    score(7)
+    score_own(3)
     arrived(9, qg_ref.at[1, z, 1 - y])
     z_pair(1)
     z_own_forward(1)
-    x_far_finish(1, 1 - y)
-    forward(5)
-    forward_own(2)
-    forward_text(zf)
-    z_far(0)
-    forward_text(zu)
-    forward_text(zd)
-    z_near(0)
-    forward_text(z)
+    x_far_finish(1, 0, pair_y)
+    score(5)
+    score_own(2)
+    x_forward(1, 1, pair_y)
     z_pair_forward(1)
+    score_text()
+    x_near_finish(0, 1, y)
+    x_far_finish(0, 1, y)
+    for n in (0, 2, 6, 4, 1):
+        take_value(n)
+    take_sides(1, 0, vals_own, slice(0, HS))
 
     z_own_finish(1)
     take_shared(1, keep_grad)
-    slope_shared_text()
-    z_relay(0)
-    for d in (2, 1):
-        slope_shared(d)
+    slope_shared(0, True)
+    for n in (2, 6, 4):
+        slope_shared(n)
+    x_near_finish(1, 1, pair_y)
+    for n in (3, 7):
+        take_value(n)
+    for d in (1, 3):
+        take_sides(1, d, vals_own, slice(0, HS))
+    mix_near()
+    x_far_finish(1, 1, pair_y)
+    take_value(5)
+    take_sides(1, 2, vals_own, slice(0, HS))
+    mix_far(zf)
+    z_far(0)
+    mix_far(zu)
+    mix_far(zd)
+    z_near(0)
+    mix_far(z)
     z_pair_finish(1)
     take_own(1, keep_grad)
+    slope_shared_text()
     slope_own_text()
+    z_relay(0)
     for s in range(2):
         key_grads_text(s)
+    slope_shared(5)
     slope_own(2)
     key_grads_own(2)
     key_grads_shared(2)
     for a in (1, 0):
         for t in range(2):
             x_far(t, a)
+    slope_shared(3)
+    slope_own(1)
     z_total(0, 1.0)
-    for d in (3, 0):
-        slope_shared(d)
-    slope_own(1)
+    slope_shared(7)
+    slope_shared(1)
     rarrived(24, yq_in.at[0])
     attn[:, cols(0)] = by_y(keep_q[0, 0], yq_in[0])
     attn[:, cols(1)] = by_y(yq_in[0], keep_q[0, 0])
@@ -906,8 +950,8 @@
             pltpu.VMEM((LAT, 2 * HS), BF),
             pltpu.VMEM((2, SIDE, 2 * HS), BF),
             pltpu.VMEM((2, TEXT, 2 * HS), BF),
-            pltpu.VMEM((2, SIDE, HS), BF),
-            pltpu.VMEM((2, TEXT, HS), BF),
+            pltpu.VMEM((2, SIDE + TEXT, HS), BF),
+            pltpu.VMEM((LAT + TEXT, HS), BF),
             pltpu.VMEM((BLOCKS, TR, 2 * HS), BF),
             pltpu.VMEM((BLOCKS, TR, HS), BF),
             pltpu.VMEM((NZ * TR, LAT + TEXT), BF),

time: 86.3 us -> 87.8 us (1.017)
  Pallas kernels: 84.8 us -> 86.3 us
    pallas_call x1, Pallas kernels: 82.8 us -> 84.3 us  [shards(): pl.pallas_call(fused_kernel, out_shape=result, in_specs=[hbm] * 9 + [smem...]
where the time goes in v7:
time: 87.8 us; the launch traced here: 87.1 us
  Pallas kernels  86.3 us (98%)
    pallas_call x1, Pallas kernels, shards(): pl.pallas_call(fused_kernel, out_shape=result, in_specs=[hbm] * 9 + [smem...  84.3 us
    pallas_call x1, Pallas kernels, shards(): pl.pallas_call(store_kernel, out_shape=result, in_specs=[hbm] * len(resul...  2.04 us

profile of v7, /device:TPU:0, one launch (start us, length us, event | category | flops | bytes accessed | tf_op | source)
XLA Modules:
  0.0 87.1 jit_solution(2673497802580552162)
XLA Ops:
  0.6 84.3 %shard_map.154 = (bf16[256,768]{1,0:T(8,128)(2,1)}, bf16[256,384]{1,0:T(8,128)(2,1)}, bf16[256,384]{1,0:T(8,128)(2,1)}, bf16[256,384]{1,0:T(8,128)(2,1)}, bf16[1...) custom-call(bf16[256,384]{1,0:T(8,128)(2,1)} %q_hbm.1, bf16[256,384]{1,0:T(8,128)(2,1)} %k_hbm.1, bf16[256,384]{1,0:T(8,128)(2,1)} %v_hbm.1, ...), custom_call_target="tpu_custom_call" | custom-call | tf_op jit(solution)/shard_map/pallas_call | solution.py:922
  84.9 2.0 %shard_map.155 = (bf16[256,768]{1,0:T(8,128)(2,1)}, bf16[256,384]{1,0:T(8,128)(2,1)}, bf16[256,384]{1,0:T(8,128)(2,1)}, bf16[256,384]{1,0:T(8,128)(2,1)}, bf16[1...) custom-call(bf16[256,768]{1,0:T(8,128)(2,1)} %get-tuple-element.12.refs_0_, bf16[256,384]{1,0:T(8,128)(2,1)} %get-tuple-element.13.refs_1_, ...), custom_call_target="tpu_custom_call" | custom-call | tf_op jit(solution)/shard_map/pallas_call | solution.py:1005

commit v8 on v7

--- a/solution.py
+++ b/solution.py
@@ -559,37 +559,33 @@
     left_of = (queries_t, grads_t)
     scale_of = (0.25, 0.5)
 
-    def key_grads_shared(d):
-        for t in range(2):
-            right = (slopes, weights)[t][:, d * 2 * TR : (d + 1) * 2 * TR]
-            total = (dot_nn(left_of[t][:, 2 * NZ * TR :], right) * scale_of[t]).astype(BF)
-            for r in range(2):
-                kvg_ref[t, kv_index(2 * d + r), 1, 0:TR] = total[:, r * TR : (r + 1) * TR].T
-
-    def key_grads_own(d):
-        mask = own_is_long(z, (x + d) % NX)
-        for t in range(2):
-            sides = []
-            for g in range(2):
-                rows = slice(g * SIDE, (g + 1) * SIDE)
-                right = (slopes_own, weights_own)[t][rows, d * TR : (d + 1) * TR]
-                total = dot_nn(left_of[t][:, rows], right) * scale_of[t]
-                sides.append(total.astype(BF).T)
-            mine, other = by_side(mask, sides[0], sides[1])
-            kvg_ref[t, kv_index(2 * d), 0, 0:TR] = mine
-            kvg_ref[t, kv_index(2 * d + 1), 0, 0:TR] = other
-
-    def key_grads_text(s):
-        for t in range(2):
-            if s == 0:
-                left = left_of[t][:, 0 : 2 * NZ * TR]
-                right = (slopes_own, weights_own)[t][:, own_text]
-            else:
-                left = left_of[t][:, 2 * NZ * TR :]
-                right = (slopes, weights)[t][:, shared_text]
-            text_rows = (dot_nn(left, right) * scale_of[t]).astype(BF).T
-            for n in range(NY * NX):
-                kvg_ref[t, kv_index(n), s, TR:BR] = text_rows[n * CR : (n + 1) * CR]
+    def key_grads_shared(t, d):
+        right = (slopes, weights)[t][:, d * 2 * TR : (d + 1) * 2 * TR]
+        total = (dot_nn(left_of[t][:, 2 * NZ * TR :], right) * scale_of[t]).astype(BF)
+        for r in range(2):
+            kvg_ref[t, kv_index(2 * d + r), 1, 0:TR] = total[:, r * TR : (r + 1) * TR].T
+
+    def key_grads_own(t, d):
+        sides = []
+        for g in range(2):
+            rows = slice(g * SIDE, (g + 1) * SIDE)
+            right = (slopes_own, weights_own)[t][rows, d * TR : (d + 1) * TR]
+            total = dot_nn(left_of[t][:, rows], right) * scale_of[t]
+            sides.append(total.astype(BF).T)
+        mine, other = by_side(own_is_long(z, (x + d) % NX), sides[0], sides[1])
+        kvg_ref[t, kv_index(2 * d), 0, 0:TR] = mine
+        kvg_ref[t, kv_index(2 * d + 1), 0, 0:TR] = other
+
+    def key_grads_text(t, s):
+        if s == 0:
+            left = left_of[t][:, 0 : 2 * NZ * TR]
+            right = (slopes_own, weights_own)[t][:, own_text]
+        else:
+            left = left_of[t][:, 2 * NZ * TR :]
+            right = (slopes, weights)[t][:, shared_text]
+        text_rows = (dot_nn(left, right) * scale_of[t]).astype(BF).T
+        for n in range(NY * NX):
+            kvg_ref[t, kv_index(n), s, TR:BR] = text_rows[n * CR : (n + 1) * CR]
 
 
     def z_far(t):
@@ -631,19 +627,26 @@
     ahead = ((xr, xl), (xl, xr))
     plane = (y, 1 - y)
 
-    def x_far(t, a):
-        src = kvg_ref.at[t, plane[a] * NX + xf]
-        rsend(x_base(t, a), src, x_in.at[t, a, 0], ring[t][0])
-
-    def x_near(t, a):
-        src = kvg_ref.at[t, plane[a] * NX + ahead[t][1]]
-        rsend(x_base(t, a) + 1, src, x_in.at[t, a, 1], ring[t][1])
-
-    def x_relay(t, a):
-        rarrived(x_base(t, a), x_in.at[t, a, 0])
-        mine = wide(kvg_ref[t, plane[a] * NX + ahead[t][0]])
-        x_sum[t, a] = (wide(x_in[t, a, 0]) + mine).astype(BF)
-        rsend(x_base(t, a) + 2, x_sum.at[t, a], x_in.at[t, a, 2], ring[t][0])
+    def x_far(t):
+        for a in (1, 0):
+            src = kvg_ref.at[t, plane[a] * NX + xf]
+            rsend(x_base(t, a), src, x_in.at[t, a, 0], ring[a][0])
+
+    def x_near(t):
+        for a in (1, 0):
+            src = kvg_ref.at[t, plane[a] * NX + ahead[a][1]]
+            rsend(x_base(t, a) + 1, src, x_in.at[t, a, 1], ring[a][1])
+
+    def x_relay(t):
+        for a in (1, 0):
+            rarrived(x_base(t, a), x_in.at[t, a, 0])
+            mine = wide(kvg_ref[t, plane[a] * NX + ahead[a][0]])
+            x_sum[t, a] = (wide(x_in[t, a, 0]) + mine).astype(BF)
+            rsend(x_base(t, a) + 2, x_sum.at[t, a], x_in.at[t, a, 2], ring[a][0])
+
+    def to_pair(t):
+        yk_out[t] = x_total(t, 1).astype(BF)
+        rsend(26 + t, yk_out.at[t], yk_in.at[t], "pair")
 
     def x_total(t, a):
         rarrived(x_base(t, a) + 1, x_in.at[t, a, 1])
@@ -749,9 +752,14 @@
 
     z_own_finish(1)
     take_shared(1, keep_grad)
-    slope_shared(0, True)
-    for n in (2, 6, 4):
-        slope_shared(n)
+    key_grads_text(1, 1)
+    for d in (2, 3, 1):
+        key_grads_shared(1, d)
+    z_pair_finish(1)
+    take_own(1, keep_grad)
+    key_grads_text(1, 0)
+    key_grads_own(1, 2)
+    x_far(1)
     x_near_finish(1, 1, pair_y)
     for n in (3, 7):
         take_value(n)
@@ -767,25 +775,28 @@
     mix_far(zd)
     z_near(0)
     mix_far(z)
-    z_pair_finish(1)
-    take_own(1, keep_grad)
+    key_grads_own(1, 3)
+    key_grads_own(1, 1)
+    x_relay(1)
+    x_near(1)
+    slope_shared(4, True)
+    slope_shared(5)
     slope_shared_text()
     slope_own_text()
     z_relay(0)
-    for s in range(2):
-        key_grads_text(s)
-    slope_shared(5)
     slope_own(2)
-    key_grads_own(2)
-    key_grads_shared(2)
-    for a in (1, 0):
-        for t in range(2):
-            x_far(t, a)
-    slope_shared(3)
+    for part_of in range(2):
+        key_grads_text(0, part_of)
+    key_grads_own(0, 2)
+    key_grads_shared(0, 2)
+    x_far(0)
+    key_grads_shared(1, 0)
+    key_grads_own(1, 0)
+    z_total(0, 1.0)
+    to_pair(1)
+    for n in (2, 3):
+        slope_shared(n)
     slope_own(1)
-    z_total(0, 1.0)
-    slope_shared(7)
-    slope_shared(1)
     rarrived(24, yq_in.at[0])
     attn[:, cols(0)] = by_y(keep_q[0, 0], yq_in[0])
     attn[:, cols(1)] = by_y(yq_in[0], keep_q[0, 0])
@@ -793,25 +804,22 @@
     part[0] = project(core_other)
     rsend(28, part.at[0], core_in.at[0], "core")
     part[2] = project(other_head)
-    key_grads_own(1)
-    key_grads_shared(1)
+    for n in (6, 7):
+        slope_shared(n)
+    slope_own(3)
     rarrived(28, core_in.at[0])
     pair_sum[...] = (wide(part[2]) + wide(core_in[0])).astype(BF)
     rsend(30, pair_sum.at[first], out_relay.at[0], "pair")
     rsend(31, pair_sum.at[second], out_relay.at[1], "back")
-    for a in (1, 0):
-        x_near(1, a)
-        x_relay(0, a)
+    for d in (1, 3):
+        key_grads_own(0, d)
+        key_grads_shared(0, d)
+    x_relay(0)
+    x_near(0)
     part[1] = project(core_head)
     rsend(29, part.at[1], core_in.at[1], "core")
-
-    slope_own(3)
-    key_grads_own(3)
-    key_grads_shared(3)
-    for a in (1, 0):
-        x_near(0, a)
-        x_relay(1, a)
-    part[3] = project(head)
+    for n in (0, 1):
+        slope_shared(n)
     for zq in (zf, zu, zd, z):
         slope_own_row(0, zq)
         finish_dq(zq)
@@ -823,12 +831,11 @@
     rsend(32, out_relay.at[0], far_in.at[first], "back")
     rarrived(31, out_relay.at[1])
     rsend(33, out_relay.at[1], far_in.at[second], "pair")
+    key_grads_own(0, 0)
+    key_grads_shared(0, 0)
     z_relay(1)
-    key_grads_own(0)
-    key_grads_shared(0)
-    for t in range(2):
-        yk_out[t] = x_total(t, 1).astype(BF)
-        rsend(26 + t, yk_out.at[t], yk_in.at[t], "pair")
+    part[3] = project(head)
+    to_pair(0)
     z_total(1, factor)
 
     stores = []

time: 87.8 us -> 85.1 us (0.969)
  Pallas kernels: 86.3 us -> 84.2 us
    pallas_call x1, Pallas kernels: 84.3 us -> 82.1 us  [shards(): pl.pallas_call(fused_kernel, out_shape=result, in_specs=[hbm] * 9 + [smem...]
where the time goes in v8:
time: 85.1 us; the launch traced here: 85 us
  Pallas kernels  84.2 us (99%)
    pallas_call x1, Pallas kernels, shards(): pl.pallas_call(fused_kernel, out_shape=result, in_specs=[hbm] * 9 + [smem...  82.1 us
    pallas_call x1, Pallas kernels, shards(): pl.pallas_call(store_kernel, out_shape=result, in_specs=[hbm] * len(resul...  2.04 us

profile of v8, /device:TPU:0, one launch (start us, length us, event | category | flops | bytes accessed | tf_op | source)
XLA Modules:
  0.0 85.0 jit_solution(1541523972622406465)
XLA Ops:
  0.6 82.1 %shard_map.154 = (bf16[256,768]{1,0:T(8,128)(2,1)}, bf16[256,384]{1,0:T(8,128)(2,1)}, bf16[256,384]{1,0:T(8,128)(2,1)}, bf16[256,384]{1,0:T(8,128)(2,1)}, bf16[1...) custom-call(bf16[256,384]{1,0:T(8,128)(2,1)} %q_hbm.1, bf16[256,384]{1,0:T(8,128)(2,1)} %k_hbm.1, bf16[256,384]{1,0:T(8,128)(2,1)} %v_hbm.1, ...), custom_call_target="tpu_custom_call" | custom-call | tf_op jit(solution)/shard_map/pallas_call | solution.py:929
  82.8 2.0 %shard_map.155 = (bf16[256,768]{1,0:T(8,128)(2,1)}, bf16[256,384]{1,0:T(8,128)(2,1)}, bf16[256,384]{1,0:T(8,128)(2,1)}, bf16[256,384]{1,0:T(8,128)(2,1)}, bf16[1...) custom-call(bf16[256,768]{1,0:T(8,128)(2,1)} %get-tuple-element.12.refs_0_, bf16[256,384]{1,0:T(8,128)(2,1)} %get-tuple-element.13.refs_1_, ...), custom_call_target="tpu_custom_call" | custom-call | tf_op jit(solution)/shard_map/pallas_call | solution.py:1012

commit v9 on v8

v9 whole, which is shorter than its diff:
```python
import jax
import jax.numpy as jnp
from jax import lax
from jax.experimental import pallas as pl
from jax.experimental.pallas import tpu as pltpu
from jax.sharding import PartitionSpec as P

MESH = pl.DeviceIdType.MESH
BF = jnp.bfloat16
F32 = jnp.float32

NX, NZ, NY = 4, 4, 2
HS = 128
NH = 3
TR = 256
CR = 16
BR = TR + CR
HALF = TR // 2
CLIPS = 4
CAP = 128
TILE = 64
MASKED = -32768.0
BLOCKS = NH * NZ
SIDE = NX * TR
SHARED_TEXT = BR
SHARED = BR + CR
CHUNK = BR + BR
TEXT = NY * NX * CR
VMEM_LIMIT = 58 * 1024 * 1024


def place():
    seq = lax.axis_index("seq")
    head = lax.axis_index("head")
    y = seq // (NZ * NX)
    z = (seq // NX) % NZ
    x = seq % NX
    return seq, head, y, z, x


def peers(seq, head, y, z, x):
    def at(yy, zz, xx):
        return (yy * NZ + zz) * NX + xx

    other_head = (head + 2) % 4
    core_head = head + 1 - 2 * (head % 2)
    return {
        "pair": (at(1 - y, z, x), head),
        "back": (at(1 - y, z, x), other_head),
        "core": (seq, core_head),
        "right": (at(y, z, (x + 1) % NX), head),
        "left": (at(y, z, (x + NX - 1) % NX), head),
        "up": (at(y, (z + 1) % NZ, x), head),
        "down": (at(y, (z + NZ - 1) % NZ, x), head),
    }


def greet(peer):
    barrier = pltpu.get_barrier_semaphore()
    for device in peer.values():
        pl.semaphore_signal(barrier, inc=1, device_id=device, device_id_type=MESH)
    pl.semaphore_wait(barrier, len(peer))


def sender(peer, send_sem, recv_sem, sent):
    def send(n, src, dst, to):
        copy = pltpu.make_async_remote_copy(
            src_ref=src,
            dst_ref=dst,
            send_sem=send_sem.at[n],
            recv_sem=recv_sem.at[n],
            device_id=peer[to],
            device_id_type=MESH,
        )
        copy.start()
        sent.append(copy)

    def arrived(n, dst):
        pltpu.make_async_remote_copy(
            src_ref=dst,
            dst_ref=dst,
            send_sem=send_sem.at[n],
            recv_sem=recv_sem.at[n],
            device_id=peer["core"],
            device_id_type=MESH,
        ).wait_recv()

    return send, arrived


def dot_nt(a, b):
    return lax.dot_general(a, b, (((1,), (1,)), ((), ())), preferred_element_type=F32)


def dot_nn(a, b):
    return lax.dot_general(a, b, (((1,), (0,)), ((), ())), preferred_element_type=F32)


def fused_kernel(
    q_hbm,
    k_hbm,
    v_hbm,
    tk_hbm,
    tv_hbm,
    go_hbm,
    w_hbm,
    tile_hbm,
    order_hbm,
    len_ref,
    bias_ref,
    out_hbm,
    gq_hbm,
    gk_hbm,
    gv_hbm,
    gtk_hbm,
    gtv_hbm,
    q_ref,
    k_ref,
    v_ref,
    tk_ref,
    tv_ref,
    go_ref,
    w_ref,
    tile_ref,
    order_ref,
    out_ref,
    gq_ref,
    gk_ref,
    gv_ref,
    gtk_ref,
    gtv_ref,
    qg_ref,
    kv_ref,
    st_pair,
    pair_out,
    pair_in,
    goall,
    go_relay,
    acc,
    kaug,
    vals,
    qaug,
    gsel,
    weights,
    slopes,
    queries_t,
    grads_t,
    oacc,
    qacc,
    oq_ref,
    kvg_ref,
    z_in,
    z_sum,
    x_in,
    x_sum,
    yq_out,
    yq_in,
    yk_out,
    yk_in,
    keep_q,
    attn,
    part,
    core_in,
    pair_sum,
    out_relay,
    far_in,
    g_send,
    g_recv,
    r_send,
    r_recv,
    local_sem,
    store_sem,
):
    seq, head, y, z, x = place()
    peer = peers(seq, head, y, z, x)
    zu, zd, zf = (z + 1) % NZ, (z + NZ - 1) % NZ, (z + 2) % NZ
    xr, xl, xf = (x + 1) % NX, (x + NX - 1) % NX, (x + 2) % NX
    other_head = (head + 2) % 4
    core_head = head + 1 - 2 * (head % 2)
    core_other = core_head + 2 - 4 * (core_head // 2)
    first, second = pl.ds(0, HALF), pl.ds(HALF, HALF)
    sent = []
    send, arrived = sender(peer, g_send, g_recv, sent)
    rsend, rarrived = sender(peer, r_send, r_recv, sent)
    cols = lambda h: slice(h * HS, (h + 1) * HS)
    by_y = lambda a, b: jnp.where(y == 0, a, b)
    wide = lambda a: a.astype(F32)
    factor = HS ** (-0.5)

    load = []
    for n, (src, dst) in enumerate(
        (
            (k_hbm, k_ref),
            (tk_hbm, tk_ref),
            (v_hbm, v_ref),
            (tv_hbm, tv_ref),
            (q_hbm, q_ref),
            (go_hbm, go_ref),
            (w_hbm, w_ref),
            (tile_hbm, tile_ref),
            (order_hbm, order_ref),
        )
    ):
        copy = pltpu.make_async_copy(src, dst, local_sem.at[n])
        copy.start()
        load.append(copy)

    greet(peer)


    def chunk_of(a, t, index):
        return kv_ref.at[t, index, pl.ds(0, (SHARED, CHUNK)[a])]

    def x_send(a, t, yy):
        chunk = chunk_of(a, t, yy * NX + x)
        send(10 + 6 * a + 2 * t, chunk, chunk, ("right", "left")[t])
        send(11 + 6 * a + 2 * t, chunk, chunk, ("left", "right")[t])

    def x_forward(a, t, yy):
        base = 10 + 6 * a
        chunk = chunk_of(a, t, yy * NX + (xl, xr)[t])
        arrived(base + 2 * t, chunk)
        send(base + 4 + t, chunk, chunk, ("right", "left")[t])

    def x_near_finish(a, t, yy):
        arrived(10 + 6 * a + 1 + 2 * t, chunk_of(a, t, yy * NX + (xr, xl)[t]))

    def x_far_finish(a, t, yy):
        arrived(10 + 6 * a + 4 + t, chunk_of(a, t, yy * NX + xf))

    def z_pair(t):
        base = 22 + 10 * t
        send(base + 0, qg_ref.at[t, z, 2], qg_ref.at[t, z, 2], "up")
        send(base + 1, qg_ref.at[t, z, 1 - y], qg_ref.at[t, z, 1 - y], "down")
        send(base + 2, qg_ref.at[t, z, 1 - y], qg_ref.at[t, z, 1 - y], "up")
        send(base + 3, qg_ref.at[t, z, 2], qg_ref.at[t, z, 2], "down")

    def z_pair_forward(t):
        base = 22 + 10 * t
        arrived(base + 0, qg_ref.at[t, zd, 2])
        send(base + 4, qg_ref.at[t, zd, 2], qg_ref.at[t, zd, 2], "up")
        arrived(base + 1, qg_ref.at[t, zu, 1 - y])
        send(base + 5, qg_ref.at[t, zu, 1 - y], qg_ref.at[t, zu, 1 - y], "down")

    def z_own(t):
        base = 22 + 10 * t
        send(base + 6, qg_ref.at[t, z, y], qg_ref.at[t, z, y], "up")
        send(base + 7, qg_ref.at[t, z, y], qg_ref.at[t, z, y], "down")

    def z_own_forward(t):
        base = 22 + 10 * t
        arrived(base + 6, qg_ref.at[t, zd, y])
        src = qg_ref.at[t, zd, y, first]
        send(base + 8, src, src, "up")
        arrived(base + 7, qg_ref.at[t, zu, y])
        src = qg_ref.at[t, zu, y, second]
        send(base + 9, src, src, "down")

    def z_pair_finish(t):
        base = 22 + 10 * t
        arrived(base + 2, qg_ref.at[t, zd, 1 - y])
        arrived(base + 3, qg_ref.at[t, zu, 2])
        arrived(base + 4, qg_ref.at[t, zf, 2])
        arrived(base + 5, qg_ref.at[t, zf, 1 - y])

    def z_own_finish(t):
        base = 22 + 10 * t
        arrived(base + 8, qg_ref.at[t, zf, y, first])
        arrived(base + 9, qg_ref.at[t, zf, y, second])

    def pair_rows(t, shared):
        arrived((6, 9)[t], pair_in.at[t])
        qg_ref[t, z, 1 - y] = pair_in[t, 0]
        mask = chunk_rows(z, x) >= long_start
        qg_ref[t, z, 2] = by_side(mask, shared, pair_in[t, 1])[0]

    def pair_keys(t, ref):
        index = (1 - y) * NX + x
        arrived(7 + t, kv_ref.at[t, index])
        mask = chunk_rows(z, x) >= long_start
        rows = pl.ds(SHARED, TR)
        kv_ref[t, index, rows] = by_side(mask, ref[:, cols(2)], kv_ref[t, index, rows])[0]
        x_send(1, t, 1 - y)

    def feature(n):
        return w_ref[:, pl.ds(pl.multiple_of(n * 768, 128), 768)]

    half_rows = NZ * NX * TR
    ends = [len_ref[0]]
    for c in range(1, CLIPS):
        ends.append(ends[-1] + len_ref[c])
    long_start = 0
    for c in range(1, CLIPS):
        long_start = jnp.where(len_ref[c] == half_rows, ends[c - 1], long_start)

    def clip_at(pos):
        total = 0
        for c in range(CLIPS - 1):
            total = total + jnp.where(pos >= ends[c], 1, 0)
        return total

    row_index = lax.broadcasted_iota(jnp.int32, (TR, HS), 0)

    def chunk_rows(zz, xx):
        return (zz * NX + xx) * TR + row_index

    def own_is_long(zz, xx):
        t = chunk_rows(zz, xx)
        return jnp.where(y == 0, t - long_start, long_start - 1 - t) >= 0

    def by_side(mask, mine, other):
        mine, other = wide(mine), wide(other)
        return jnp.where(mask, mine, other).astype(BF), jnp.where(mask, other, mine).astype(BF)

    lane = lax.broadcasted_iota(jnp.int32, (1, HS), 1)
    tiles_here = (lane % 64) // 16 == z
    clip_lane = ((z + 1) % NZ) * 16
    bias_lane = clip_lane + CLIPS
    bias_ones = jnp.where((lane >= bias_lane) & (lane < bias_lane + 3), 1.0, 0.0)

    def kv_index(n):
        return ((y + n % 2) % NY) * NX + (x + n // 2) % NX

    def key_columns(pos):
        hit = (tiles_here & ((pos >> 6) == lane)) | (clip_at(pos) == lane - clip_lane)
        return jnp.where(hit, 1.0, bias_ones).astype(BF)

    def key_side():
        for d in range(NX):
            t = chunk_rows(z, (x + d) % NX)
            rows = slice(d * TR, (d + 1) * TR)
            sides = by_side(t >= long_start, key_columns(t), key_columns(t + half_rows))
            for side, value in enumerate(sides + (by_y(*sides),)):
                kaug[side, rows, HS:] = value
        row = lax.broadcasted_iota(jnp.int32, (TEXT, HS), 0)
        n = row // CR
        plane = ((y + n % 2) % NY) * NZ + z
        text_row = (plane * NX + (x + n // 2) % NX) * CR + row % CR
        aug = jnp.broadcast_to(bias_ones, text_row.shape)
        for c in range(CLIPS):
            listed = jnp.where(order_ref[c : c + 1, :] == text_row, 1.0, 0.0)
            found = jnp.max(listed, axis=1, keepdims=True)
            aug = jnp.where(lane == clip_lane + c, found, aug)
        for g in range(NH):
            kaug[g, SIDE:, HS:] = aug.astype(BF)

    log_len = [
        jnp.log(jnp.full((1, HS), len_ref[c] + CAP, jnp.int32).astype(F32)) for c in range(CLIPS)
    ]

    def query_side(n, carry):
        g, zq = n // NZ, n % NZ
        t = chunk_rows(zq, x)
        side = jnp.where(g == 2, y, g)
        in_high = jnp.where(side == 0, long_start - 1 - t, t - long_start) >= 0
        pos = t + jnp.where(in_high, half_rows, 0)
        head_bias = bias_ref[jnp.where(g == 2, 2, y)]
        clip = clip_at(pos)
        offset = jnp.broadcast_to(log_len[CLIPS - 1], (TR, HS))
        for c in range(CLIPS - 2, -1, -1):
            offset = jnp.where(pos < ends[c], log_len[c], offset)
        total = (head_bias - offset) * (HS**0.5)
        hi = total.astype(BF).astype(F32)
        mid = (total - hi).astype(BF).astype(F32)
        low = total - hi - mid
        in_bias = jnp.where(lane == bias_lane, hi, jnp.where(lane == bias_lane + 1, mid, low))
        in_bias = jnp.where((lane >= bias_lane) & (lane < bias_lane + 3), in_bias, 0.0)
        in_clip = (lane >= clip_lane) & (lane < clip_lane + CLIPS) & (lane - clip_lane != clip)
        side = jnp.where(in_clip, MASKED, in_bias)
        for u in range(TR // TILE):
            rows = slice(u * TILE, (u + 1) * TILE)
            tile = (zq * NX + x) * (TR // TILE) + u
            off = []
            for p in range(NY):
                at = tile + p * (half_rows // TILE)
                mask_row = tile_ref[pl.ds(at, 1), :]
                off.append(jnp.where((mask_row == 0) & (lane != at) & tiles_here, 1.0, 0.0))
            masked = jnp.where(in_high[rows], off[1], off[0]) > 0.5
            qaug[n, rows, HS:] = jnp.where(masked, MASKED, side[rows]).astype(BF)
        return carry

    def keep_query(n, value):
        qaug[n, :, 0:HS] = value
        queries_t[:, n * TR : (n + 1) * TR] = value.T

    def keep_grad(n, value):
        gsel[n] = value
        grads_t[:, n * TR : (n + 1) * TR] = value.T

    def take_rows(t, keep):
        for zq in range(NZ):
            mask = own_is_long(zq, x)
            sides = by_side(mask, qg_ref[t, zq, y], qg_ref[t, zq, 1 - y])
            for g, value in enumerate(sides + (qg_ref[t, zq, 2],)):
                keep(g * NZ + zq, value)

    def take_column(t, d):
        lanes = slice(0, HS)
        ref = (kaug, vals)[t]
        mask = own_is_long(z, (x + d) % NX)
        mine, other = kv_index(2 * d), kv_index(2 * d + 1)
        sides = by_side(mask, kv_ref[t, mine, 0:TR], kv_ref[t, other, 0:TR])
        for g, value in enumerate(sides + (kv_ref[t, other, SHARED:CHUNK],)):
            ref[g, d * TR : (d + 1) * TR, lanes] = value
        for r in range(2):
            index = kv_index(2 * d + r)
            rows = slice(SIDE + (2 * d + r) * CR, SIDE + (2 * d + r + 1) * CR)
            for g in range(NH):
                low = SHARED_TEXT if g == 2 else TR
                ref[g, rows, lanes] = kv_ref[t, index, low : low + CR]

    def block_rows(n):
        return pl.ds(pl.multiple_of(n * TR, TR), TR)

    def weigh(block, columns):
        scores = dot_nt(qaug[block], kaug[block // NZ, columns, :])
        half = jnp.tanh(scores * (0.5 * factor))
        twice = 1.0 + half
        weights[block_rows(block), columns] = twice.astype(BF)
        slopes[block_rows(block), columns] = (twice * (1.0 - half)).astype(BF)

    def every_block(body):
        def step(zq, carry):
            for g in range(NH):
                body(g * NZ + zq)
            return carry

        lax.fori_loop(0, NZ, step, 0)

    def column(d):
        return slice(d * TR, (d + 1) * TR)

    text_columns = slice(SIDE, SIDE + TEXT)

    def score(d):
        take_column(0, d)
        every_block(lambda block: weigh(block, column(d)))

    def score_text():
        every_block(lambda block: weigh(block, text_columns))

    def mix(block, columns):
        return dot_nn(weights[block_rows(block), columns], vals[block // NZ, columns, :])

    def mix_near():
        def body(block):
            oacc[block] = mix(block, slice(0, 2 * TR)) + mix(block, column(3))

        every_block(body)

    def mix_far(zq):
        totals = []
        for g in range(NH):
            block = g * NZ + zq
            total = oacc[block] + mix(block, column(2)) + mix(block, text_columns)
            totals.append(total * 0.5)
        mine, other = by_side(own_is_long(zq, x), totals[0], totals[1])
        oq_ref[0, zq, y] = mine
        oq_ref[0, zq, 1 - y] = other
        oq_ref[0, zq, 2] = totals[2].astype(BF)

    def slope_step(block, columns, fresh=False):
        rows, g = block_rows(block), block // NZ
        slope = (dot_nt(gsel[block], vals[g, columns, :]) * wide(slopes[rows, columns])).astype(BF)
        slopes[rows, columns] = slope
        share = dot_nn(slope, kaug[g, columns, 0:HS])
        if fresh:
            qacc[block] = share
        else:
            qacc[block] += share

    def slope(d):
        every_block(lambda block: slope_step(block, column(d)))

    def slope_text():
        every_block(lambda block: slope_step(block, text_columns, True))

    def slope_row(d, zq):
        for g in range(NH):
            slope_step(g * NZ + zq, column(d))

    def finish_dq(zq):
        mine, other = by_side(own_is_long(zq, x), qacc[zq] * 0.25, qacc[NZ + zq] * 0.25)
        oq_ref[1, zq, y] = mine
        oq_ref[1, zq, 1 - y] = other
        oq_ref[1, zq, 2] = (qacc[2 * NZ + zq] * 0.25).astype(BF)

    left_of = (queries_t, grads_t)
    scale_of = (0.25, 0.5)

    def key_grads(t, d):
        sides = []
        for g in range(NH):
            rows = slice(g * SIDE, (g + 1) * SIDE)
            total = dot_nn(left_of[t][:, rows], (slopes, weights)[t][rows, column(d)])
            sides.append((total * scale_of[t]).astype(BF).T)
        mine, other = by_side(own_is_long(z, (x + d) % NX), sides[0], sides[1])
        kvg_ref[t, kv_index(2 * d), 0:TR] = mine
        kvg_ref[t, kv_index(2 * d + 1), 0:TR] = other
        kvg_ref[t, kv_index(2 * d + 1), SHARED:CHUNK] = sides[2]

    def key_grads_text(t):
        for low, high, at in ((0, 2 * SIDE, TR), (2 * SIDE, 3 * SIDE, SHARED_TEXT)):
            right = (slopes, weights)[t][low:high, text_columns]
            text_rows = (dot_nn(left_of[t][:, low:high], right) * scale_of[t]).astype(BF).T
            for n in range(NY * NX):
                kvg_ref[t, kv_index(n), at : at + CR] = text_rows[n * CR : (n + 1) * CR]


    def z_far(t):
        rsend(6 * t + 0, oq_ref.at[t, zf, :, first], z_in.at[t, 0], "up")
        rsend(6 * t + 3, oq_ref.at[t, zf, :, second], z_in.at[t, 3], "down")

    def z_near(t):
        rsend(6 * t + 1, oq_ref.at[t, zd, :, first], z_in.at[t, 1], "down")
        rsend(6 * t + 4, oq_ref.at[t, zu, :, second], z_in.at[t, 4], "up")

    def z_relay(t):
        base = 6 * t
        rarrived(base + 0, z_in.at[t, 0])
        z_sum[t, 0] = (wide(z_in[t, 0]) + wide(oq_ref[t, zu, :, first])).astype(BF)
        rsend(base + 2, z_sum.at[t, 0], z_in.at[t, 2], "up")
        rarrived(base + 3, z_in.at[t, 3])
        z_sum[t, 1] = (wide(z_in[t, 3]) + wide(oq_ref[t, zd, :, second])).astype(BF)
        rsend(base + 5, z_sum.at[t, 1], z_in.at[t, 5], "down")

    def z_total(t, scale):
        base = 6 * t
        for n in (1, 2, 4, 5):
            rarrived(base + n, z_in.at[t, n])
        for rows, one, two in ((first, 1, 2), (second, 4, 5)):

            def total(j):
                value = wide(oq_ref[t, z, j, rows]) + wide(z_in[t, one, j]) + wide(z_in[t, two, j])
                return (value * scale).astype(BF) if scale != 1.0 else value.astype(BF)

            yq_out[t, 0, rows] = total(1 - y)
            yq_out[t, 1, rows] = total(2)
            keep_q[t, rows] = total(y)
        rsend(24 + t, yq_out.at[t], yq_in.at[t], "pair")

    def x_base(t, a):
        return 12 + 6 * t + 3 * a

    ring = (("right", "left"), ("left", "right"))
    ahead = ((xr, xl), (xl, xr))
    plane = (y, 1 - y)

    def sums_of(a):
        return pl.ds(0, (SHARED, CHUNK)[a])

    def x_far(t):
        for a in (1, 0):
            src = kvg_ref.at[t, plane[a] * NX + xf, sums_of(a)]
            rsend(x_base(t, a), src, x_in.at[t, a, 0, sums_of(a)], ring[a][0])

    def x_near(t):
        for a in (1, 0):
            src = kvg_ref.at[t, plane[a] * NX + ahead[a][1], sums_of(a)]
            rsend(x_base(t, a) + 1, src, x_in.at[t, a, 1, sums_of(a)], ring[a][1])

    def x_relay(t):
        for a in (1, 0):
            rows = sums_of(a)
            rarrived(x_base(t, a), x_in.at[t, a, 0, rows])
            mine = wide(kvg_ref[t, plane[a] * NX + ahead[a][0], rows])
            x_sum[t, a, rows] = (wide(x_in[t, a, 0, rows]) + mine).astype(BF)
            rsend(x_base(t, a) + 2, x_sum.at[t, a, rows], x_in.at[t, a, 2, rows], ring[a][0])

    def to_pair(t):
        yk_out[t] = x_total(t, 1).astype(BF)
        rsend(26 + t, yk_out.at[t], yk_in.at[t], "pair")

    def x_total(t, a):
        rows = sums_of(a)
        rarrived(x_base(t, a) + 1, x_in.at[t, a, 1, rows])
        rarrived(x_base(t, a) + 2, x_in.at[t, a, 2, rows])
        value = wide(kvg_ref[t, plane[a] * NX + x, rows])
        value = value + wide(x_in[t, a, 1, rows]) + wide(x_in[t, a, 2, rows])
        return value * factor if t == 0 else value

    def take_attn(t, ref):
        rarrived(24 + t, yq_in.at[t])
        ref[:, cols(0)] = by_y(keep_q[t], yq_in[t, 0])
        ref[:, cols(1)] = by_y(yq_in[t, 0], keep_q[t])
        mask = chunk_rows(z, x) >= long_start
        ref[:, cols(2)] = by_side(mask, yq_out[t, 1], yq_in[t, 1])[0]

    def project(n):
        return dot_nn(attn[...], feature(n)).astype(BF)

    send(1, go_hbm.at[second], go_relay.at[1], "back")
    load[4].wait()
    pair_out[0, 0] = by_y(q_ref[:, cols(1)], q_ref[:, cols(0)])
    pair_out[0, 1] = q_ref[:, cols(2)]
    send(6, pair_out.at[0], pair_in.at[0], "pair")
    qg_ref[0, z, y] = by_y(q_ref[:, cols(0)], q_ref[:, cols(1)])
    z_own(0)
    c = y * NX + x
    pair_y = 1 - y
    for t, (ref, text) in enumerate(((k_ref, tk_ref), (v_ref, tv_ref))):
        load[2 * t].wait()
        load[2 * t + 1].wait()
        st_pair[t, 0:TR] = by_y(ref[:, cols(1)], ref[:, cols(0)])
        st_pair[t, TR:BR] = by_y(text[:, cols(1)], text[:, cols(0)])
        st_pair[t, SHARED_TEXT:SHARED] = text[:, cols(2)]
        st_pair[t, SHARED:CHUNK] = ref[:, cols(2)]
        if t == 0:
            send(7, st_pair.at[0], kv_ref.at[0, c], "pair")
            send(0, go_hbm.at[first], go_relay.at[0], "pair")
        kv_ref[t, c, 0:TR] = by_y(ref[:, cols(0)], ref[:, cols(1)])
        kv_ref[t, c, TR:BR] = by_y(text[:, cols(0)], text[:, cols(1)])
        kv_ref[t, c, SHARED_TEXT:SHARED] = text[:, cols(2)]
        x_send(0, t, y)
    send(2, go_hbm, goall.at[head], "core")
    load[7].wait()
    load[8].wait()
    key_side()
    pair_rows(0, q_ref[:, cols(2)])
    z_pair(0)
    lax.fori_loop(0, BLOCKS, query_side, 0)
    arrived(1, go_relay.at[1])
    send(4, go_relay.at[1], goall.at[other_head, second], "pair")
    z_own_forward(0)
    pair_keys(0, k_ref)
    load[5].wait()
    load[6].wait()
    acc[...] = dot_nt(go_ref[...], feature(head))
    x_forward(0, 0, y)
    x_forward(0, 1, y)
    z_pair_forward(0)
    z_own_finish(0)
    z_pair_finish(0)
    take_rows(0, keep_query)
    arrived(0, go_relay.at[0])
    send(3, go_relay.at[0], goall.at[head, first], "back")
    send(8, st_pair.at[1], kv_ref.at[1, c], "pair")
    x_forward(1, 0, pair_y)
    score(0)
    arrived(2, goall.at[core_head])
    acc[...] += dot_nt(goall[core_head], feature(core_head))
    x_near_finish(0, 0, y)
    x_near_finish(1, 0, pair_y)
    score(1)
    arrived(3, goall.at[other_head, first])
    arrived(4, goall.at[other_head, second])
    send(5, goall.at[other_head], goall.at[other_head], "core")
    acc[...] += dot_nt(goall[other_head], feature(other_head))
    score(3)
    arrived(5, goall.at[core_other])
    grad = (acc[...] + dot_nt(goall[core_other], feature(core_other))).astype(BF)
    pair_out[1, 0] = by_y(grad[:, cols(1)], grad[:, cols(0)])
    pair_out[1, 1] = grad[:, cols(2)]
    send(9, pair_out.at[1], pair_in.at[1], "pair")
    qg_ref[1, z, y] = by_y(grad[:, cols(0)], grad[:, cols(1)])
    z_own(1)
    pair_keys(1, v_ref)
    x_far_finish(0, 0, y)
    x_far_finish(1, 0, pair_y)
    score(2)
    pair_rows(1, pair_out[1, 1])
    z_pair(1)
    z_own_forward(1)
    score_text()
    x_forward(1, 1, pair_y)
    z_pair_forward(1)
    x_near_finish(0, 1, y)
    x_far_finish(0, 1, y)
    take_column(1, 0)

    z_own_finish(1)
    z_pair_finish(1)
    take_rows(1, keep_grad)
    key_grads_text(1)
    key_grads(1, 2)
    x_far(1)
    x_near_finish(1, 1, pair_y)
    take_column(1, 1)
    take_column(1, 3)
    mix_near()
    x_far_finish(1, 1, pair_y)
    take_column(1, 2)
    mix_far(zf)
    z_far(0)
    mix_far(zu)
    mix_far(zd)
    z_near(0)
    mix_far(z)
    key_grads(1, 3)
    key_grads(1, 1)
    x_relay(1)
    x_near(1)
    slope_text()
    z_relay(0)
    slope(2)
    key_grads_text(0)
    key_grads(0, 2)
    x_far(0)
    key_grads(1, 0)
    z_total(0, 1.0)
    to_pair(1)
    slope(1)
    take_attn(0, attn)
    part[0] = project(core_other)
    rsend(28, part.at[0], core_in.at[0], "core")
    part[2] = project(other_head)
    slope(3)
    rarrived(28, core_in.at[0])
    pair_sum[...] = (wide(part[2]) + wide(core_in[0])).astype(BF)
    rsend(30, pair_sum.at[first], out_relay.at[0], "pair")
    rsend(31, pair_sum.at[second], out_relay.at[1], "back")
    key_grads(0, 1)
    key_grads(0, 3)
    x_relay(0)
    x_near(0)
    part[1] = project(core_head)
    rsend(29, part.at[1], core_in.at[1], "core")
    for zq in (zf, zu, zd, z):
        slope_row(0, zq)
        finish_dq(zq)
        if zq is zf:
            z_far(1)
        elif zq is zd:
            z_near(1)
    key_grads(0, 0)
    rarrived(30, out_relay.at[0])
    rsend(32, out_relay.at[0], far_in.at[first], "back")
    rarrived(31, out_relay.at[1])
    rsend(33, out_relay.at[1], far_in.at[second], "pair")
    z_relay(1)
    part[3] = project(head)
    to_pair(0)
    z_total(1, factor)

    stores = []

    def store(src, dst):
        copy = pltpu.make_async_copy(src, dst, store_sem.at[len(stores)])
        copy.start()
        stores.append(copy)

    results = ((gk_ref, gtk_ref, gk_hbm, gtk_hbm), (gv_ref, gtv_ref, gv_hbm, gtv_hbm))
    rarrived(29, core_in.at[1])
    rarrived(32, far_in.at[first])
    rarrived(33, far_in.at[second])
    out_ref[...] = (wide(part[3]) + wide(core_in[1]) + wide(far_in[...])).astype(BF)
    store(out_ref, out_hbm)
    for t, (ref, text, to, text_to) in enumerate(results):
        own = x_total(t, 0)
        rarrived(26 + t, yk_in.at[t])
        mine, other = own[0:BR].astype(BF), yk_in[t, 0:BR]
        mask = chunk_rows(z, x) >= long_start
        both = by_side(mask, yk_out[t, SHARED:CHUNK], yk_in[t, SHARED:CHUNK])[0]
        for h, value in ((0, by_y(mine, other)), (1, by_y(other, mine))):
            ref[:, cols(h)] = value[0:TR]
            text[:, cols(h)] = value[TR:BR]
        ref[:, cols(2)] = both
        text[:, cols(2)] = (own[BR:SHARED] + wide(yk_in[t, SHARED_TEXT:SHARED])).astype(BF)
        store(ref, to)
        store(text, text_to)
    take_attn(1, gq_ref)
    store(gq_ref, gq_hbm)
    for copy in sent:
        copy.wait_send()
    for copy in stores:
        copy.wait()


def store_kernel(*refs):
    count = (len(refs) - 2) // 3
    held, result, buffers = refs[:count], refs[count : 2 * count], refs[2 * count : 3 * count]
    load_sem, store_sem = refs[-2:]
    loads = [
        pltpu.make_async_copy(held[n], buffers[n], load_sem.at[n]) for n in range(count)
    ]
    stores = [
        pltpu.make_async_copy(buffers[n], result[n], store_sem.at[n]) for n in range(count)
    ]
    for copy in loads:
        copy.start()
    for load, copy in zip(loads, stores):
        load.wait()
        copy.start()
    for copy in stores:
        copy.wait()


def shards(
    queries,
    keys,
    values,
    text_keys,
    text_values,
    head_bias,
    out_weight,
    grad_out,
    clip_lengths,
    tile_mask,
    caption_order,
):
    smem = pl.BlockSpec(memory_space=pltpu.SMEM)
    hbm = pl.BlockSpec(memory_space=pltpu.HBM)
    dma = pltpu.SemaphoreType.DMA
    qg_shape = (2, NZ, NH, TR, HS)
    kv_shape = (2, NY * NX, CHUNK, HS)
    out_cols = grad_out.shape[1]
    order = caption_order.reshape(CLIPS, CAP)
    token = pltpu.VMEM((TR, NH * HS), BF)
    text = pltpu.VMEM((CR, NH * HS), BF)
    wide_out = pltpu.VMEM((TR, out_cols), BF)
    halves = pltpu.VMEM((2, HALF, out_cols), BF)
    token_shape = jax.ShapeDtypeStruct((TR, NH * HS), BF)
    text_shape = jax.ShapeDtypeStruct((CR, NH * HS), BF)
    result = (
        jax.ShapeDtypeStruct((TR, out_cols), BF),
        token_shape,
        token_shape,
        token_shape,
        text_shape,
        text_shape,
    )
    held = pl.pallas_call(
        fused_kernel,
        out_shape=result,
        in_specs=[hbm] * 9 + [smem] * 2,
        out_specs=(hbm,) * len(result),
        scratch_shapes=[
            token,
            token,
            token,
            text,
            text,
            wide_out,
            pltpu.VMEM(out_weight.shape, BF),
            pltpu.VMEM(tile_mask.shape, jnp.int32),
            pltpu.VMEM(order.shape, jnp.int32),
            wide_out,
            token,
            token,
            token,
            text,
            text,
            pltpu.VMEM(qg_shape, BF),
            pltpu.VMEM(kv_shape, BF),
            pltpu.VMEM((2, CHUNK, HS), BF),
            pltpu.VMEM((2, 2, TR, HS), BF),
            pltpu.VMEM((2, 2, TR, HS), BF),
            pltpu.VMEM((4, TR, out_cols), BF),
            halves,
            pltpu.VMEM((TR, NH * HS), F32),
            pltpu.VMEM((NH, SIDE + TEXT, 2 * HS), BF),
            pltpu.VMEM((NH, SIDE + TEXT, HS), BF),
            pltpu.VMEM((BLOCKS, TR, 2 * HS), BF),
            pltpu.VMEM((BLOCKS, TR, HS), BF),
            pltpu.VMEM((BLOCKS * TR, SIDE + TEXT), BF),
            pltpu.VMEM((BLOCKS * TR, SIDE + TEXT), BF),
            pltpu.VMEM((HS, BLOCKS * TR), BF),
            pltpu.VMEM((HS, BLOCKS * TR), BF),
            pltpu.VMEM((BLOCKS, TR, HS), F32),
            pltpu.VMEM((BLOCKS, TR, HS), F32),
            pltpu.VMEM(qg_shape, BF),
            pltpu.VMEM(kv_shape, BF),
            pltpu.VMEM((2, 6, NH, HALF, HS), BF),
            pltpu.VMEM((2, 2, NH, HALF, HS), BF),
            pltpu.VMEM((2, NY, 3, CHUNK, HS), BF),
            pltpu.VMEM((2, NY, CHUNK, HS), BF),
            pltpu.VMEM((2, 2, TR, HS), BF),
            pltpu.VMEM((2, 2, TR, HS), BF),
            pltpu.VMEM((2, CHUNK, HS), BF),
            pltpu.VMEM((2, CHUNK, HS), BF),
            pltpu.VMEM((2, TR, HS), BF),
            token,
            pltpu.VMEM((4, TR, out_cols), BF),
            pltpu.VMEM((2, TR, out_cols), BF),
            wide_out,
            halves,
            wide_out,
            dma((42,)),
            dma((42,)),
            dma((34,)),
            dma((34,)),
            dma((9,)),
            dma((len(result),)),
        ],
        compiler_params=pltpu.CompilerParams(
            collective_id=0, has_side_effects=True, vmem_limit_bytes=VMEM_LIMIT
        ),
    )(
        queries,
        keys,
        values,
        text_keys,
        text_values,
        grad_out,
        out_weight,
        tile_mask,
        order,
        clip_lengths,
        head_bias,
    )
    return pl.pallas_call(
        store_kernel,
        out_shape=result,
        in_specs=[hbm] * len(result),
        out_specs=(hbm,) * len(result),
        scratch_shapes=[pltpu.VMEM(array.shape, array.dtype) for array in result]
        + [dma((len(result),)), dma((len(result),))],
        compiler_params=pltpu.CompilerParams(vmem_limit_bytes=VMEM_LIMIT),
    )(*held)


def solution(mesh):
    in_specs = (
        P("seq", "head"),
        P("seq", "head"),
        P("seq", "head"),
        P("seq", "head"),
        P("seq", "head"),
        P("head"),
        P("head", None),
        P("seq", "head"),
        P(),
        P(),
        P(),
    )
    out_specs = (P("seq", "head"),) * 6
    return jax.shard_map(shards, mesh=mesh, in_specs=in_specs, out_specs=out_specs, check_vma=False)
```

time: 85.1 us -> 81.4 us (0.957)
  Pallas kernels: 84.2 us -> 80.5 us
    pallas_call x1, Pallas kernels: 82.1 us -> 78.4 us  [shards(): pl.pallas_call(fused_kernel, out_shape=result, in_specs=[hbm] * 9 + [smem...]
where the time goes in v9:
time: 81.4 us; the launch traced here: 81.3 us
  Pallas kernels  80.5 us (99%)
    pallas_call x1, Pallas kernels, shards(): pl.pallas_call(fused_kernel, out_shape=result, in_specs=[hbm] * 9 + [smem...  78.4 us
    pallas_call x1, Pallas kernels, shards(): pl.pallas_call(store_kernel, out_shape=result, in_specs=[hbm] * len(resul...  2.04 us

profile of v9, /device:TPU:0, one launch (start us, length us, event | category | flops | bytes accessed | tf_op | source)
XLA Modules:
  0.0 81.3 jit_solution(13100754555605803655)
XLA Ops:
  0.6 78.4 %shard_map.154 = (bf16[256,768]{1,0:T(8,128)(2,1)}, bf16[256,384]{1,0:T(8,128)(2,1)}, bf16[256,384]{1,0:T(8,128)(2,1)}, bf16[256,384]{1,0:T(8,128)(2,1)}, bf16[1...) custom-call(bf16[256,384]{1,0:T(8,128)(2,1)} %q_hbm.1, bf16[256,384]{1,0:T(8,128)(2,1)} %k_hbm.1, bf16[256,384]{1,0:T(8,128)(2,1)} %v_hbm.1, ...), custom_call_target="tpu_custom_call" | custom-call | tf_op jit(solution)/shard_map/pallas_call | solution.py:822
  79.1 2.0 %shard_map.155 = (bf16[256,768]{1,0:T(8,128)(2,1)}, bf16[256,384]{1,0:T(8,128)(2,1)}, bf16[256,384]{1,0:T(8,128)(2,1)}, bf16[256,384]{1,0:T(8,128)(2,1)}, bf16[1...) custom-call(bf16[256,768]{1,0:T(8,128)(2,1)} %get-tuple-element.12.refs_0_, bf16[256,384]{1,0:T(8,128)(2,1)} %get-tuple-element.13.refs_1_, ...), custom_call_target="tpu_custom_call" | custom-call | tf_op jit(solution)/shard_map/pallas_call | solution.py:901

commit v10 on v9

--- a/solution.py
+++ b/solution.py
@@ -607,7 +607,6 @@
         st_pair[t, SHARED:CHUNK] = ref[:, cols(2)]
         if t == 0:
             send(7, st_pair.at[0], kv_ref.at[0, c], "pair")
-            send(0, go_hbm.at[first], go_relay.at[0], "pair")
         kv_ref[t, c, 0:TR] = by_y(ref[:, cols(0)], ref[:, cols(1)])
         kv_ref[t, c, TR:BR] = by_y(text[:, cols(0)], text[:, cols(1)])
         kv_ref[t, c, SHARED_TEXT:SHARED] = text[:, cols(2)]
@@ -618,9 +617,8 @@
     key_side()
     pair_rows(0, q_ref[:, cols(2)])
     z_pair(0)
+    send(0, go_hbm.at[first], go_relay.at[0], "pair")
     lax.fori_loop(0, BLOCKS, query_side, 0)
-    arrived(1, go_relay.at[1])
-    send(4, go_relay.at[1], goall.at[other_head, second], "pair")
     z_own_forward(0)
     pair_keys(0, k_ref)
     load[5].wait()
@@ -634,6 +632,8 @@
     take_rows(0, keep_query)
     arrived(0, go_relay.at[0])
     send(3, go_relay.at[0], goall.at[head, first], "back")
+    arrived(1, go_relay.at[1])
+    send(4, go_relay.at[1], goall.at[other_head, second], "pair")
     send(8, st_pair.at[1], kv_ref.at[1, c], "pair")
     x_forward(1, 0, pair_y)
     score(0)
@@ -642,11 +642,12 @@
     x_near_finish(0, 0, y)
     x_near_finish(1, 0, pair_y)
     score(1)
+    score(3)
     arrived(3, goall.at[other_head, first])
     arrived(4, goall.at[other_head, second])
     send(5, goall.at[other_head], goall.at[other_head], "core")
     acc[...] += dot_nt(goall[other_head], feature(other_head))
-    score(3)
+    pair_keys(1, v_ref)
     arrived(5, goall.at[core_other])
     grad = (acc[...] + dot_nt(goall[core_other], feature(core_other))).astype(BF)
     pair_out[1, 0] = by_y(grad[:, cols(1)], grad[:, cols(0)])
@@ -654,30 +655,22 @@
     send(9, pair_out.at[1], pair_in.at[1], "pair")
     qg_ref[1, z, y] = by_y(grad[:, cols(0)], grad[:, cols(1)])
     z_own(1)
-    pair_keys(1, v_ref)
     x_far_finish(0, 0, y)
     x_far_finish(1, 0, pair_y)
     score(2)
+    x_forward(1, 1, pair_y)
     pair_rows(1, pair_out[1, 1])
     z_pair(1)
     z_own_forward(1)
     score_text()
-    x_forward(1, 1, pair_y)
-    z_pair_forward(1)
     x_near_finish(0, 1, y)
     x_far_finish(0, 1, y)
     take_column(1, 0)
-
-    z_own_finish(1)
-    z_pair_finish(1)
-    take_rows(1, keep_grad)
-    key_grads_text(1)
-    key_grads(1, 2)
-    x_far(1)
     x_near_finish(1, 1, pair_y)
     take_column(1, 1)
     take_column(1, 3)
     mix_near()
+    z_pair_forward(1)
     x_far_finish(1, 1, pair_y)
     take_column(1, 2)
     mix_far(zf)
@@ -686,19 +679,24 @@
     mix_far(zd)
     z_near(0)
     mix_far(z)
+
+    z_own_finish(1)
+    z_pair_finish(1)
+    take_rows(1, keep_grad)
+    key_grads_text(1)
+    key_grads(1, 2)
+    x_far(1)
+    z_relay(0)
     key_grads(1, 3)
     key_grads(1, 1)
-    x_relay(1)
     x_near(1)
     slope_text()
-    z_relay(0)
     slope(2)
+    x_relay(1)
+    z_total(0, 1.0)
     key_grads_text(0)
     key_grads(0, 2)
     x_far(0)
-    key_grads(1, 0)
-    z_total(0, 1.0)
-    to_pair(1)
     slope(1)
     take_attn(0, attn)
     part[0] = project(core_other)
@@ -713,8 +711,6 @@
     key_grads(0, 3)
     x_relay(0)
     x_near(0)
-    part[1] = project(core_head)
-    rsend(29, part.at[1], core_in.at[1], "core")
     for zq in (zf, zu, zd, z):
         slope_row(0, zq)
         finish_dq(zq)
@@ -722,12 +718,16 @@
             z_far(1)
         elif zq is zd:
             z_near(1)
-    key_grads(0, 0)
+    key_grads(1, 0)
+    to_pair(1)
     rarrived(30, out_relay.at[0])
     rsend(32, out_relay.at[0], far_in.at[first], "back")
     rarrived(31, out_relay.at[1])
     rsend(33, out_relay.at[1], far_in.at[second], "pair")
     z_relay(1)
+    key_grads(0, 0)
+    part[1] = project(core_head)
+    rsend(29, part.at[1], core_in.at[1], "core")
     part[3] = project(head)
     to_pair(0)
     z_total(1, factor)

time: 81.4 us -> 78.1 us (0.959)
  Pallas kernels: 80.5 us -> 77.1 us
    pallas_call x1, Pallas kernels: 78.4 us -> 75.1 us  [shards(): pl.pallas_call(fused_kernel, out_shape=result, in_specs=[hbm] * 9 + [smem...]
where the time goes in v10:
time: 78.1 us; the launch traced here: 77.9 us
  Pallas kernels  77.1 us (99%)
  between operations  0.8 us (1%)
    pallas_call x1, Pallas kernels, shards(): pl.pallas_call(fused_kernel, out_shape=result, in_specs=[hbm] * 9 + [smem...  75.1 us
    pallas_call x1, Pallas kernels, shards(): pl.pallas_call(store_kernel, out_shape=result, in_specs=[hbm] * len(resul...  2.04 us

profile of v10, /device:TPU:0, one launch (start us, length us, event | category | flops | bytes accessed | tf_op | source)
XLA Modules:
  0.0 77.9 jit_solution(1696683783966490081)
XLA Ops:
  0.6 75.1 %shard_map.154 = (bf16[256,768]{1,0:T(8,128)(2,1)}, bf16[256,384]{1,0:T(8,128)(2,1)}, bf16[256,384]{1,0:T(8,128)(2,1)}, bf16[256,384]{1,0:T(8,128)(2,1)}, bf16[1...) custom-call(bf16[256,384]{1,0:T(8,128)(2,1)} %q_hbm.1, bf16[256,384]{1,0:T(8,128)(2,1)} %k_hbm.1, bf16[256,384]{1,0:T(8,128)(2,1)} %v_hbm.1, ...), custom_call_target="tpu_custom_call" | custom-call | tf_op jit(solution)/shard_map/pallas_call | solution.py:822
  75.7 2.0 %shard_map.155 = (bf16[256,768]{1,0:T(8,128)(2,1)}, bf16[256,384]{1,0:T(8,128)(2,1)}, bf16[256,384]{1,0:T(8,128)(2,1)}, bf16[256,384]{1,0:T(8,128)(2,1)}, bf16[1...) custom-call(bf16[256,768]{1,0:T(8,128)(2,1)} %get-tuple-element.12.refs_0_, bf16[256,384]{1,0:T(8,128)(2,1)} %get-tuple-element.13.refs_1_, ...), custom_call_target="tpu_custom_call" | custom-call | tf_op jit(solution)/shard_map/pallas_call | solution.py:901

commit v11 on v10

--- a/solution.py
+++ b/solution.py
@@ -615,9 +615,9 @@
     load[7].wait()
     load[8].wait()
     key_side()
+    send(0, go_hbm.at[first], go_relay.at[0], "pair")
     pair_rows(0, q_ref[:, cols(2)])
     z_pair(0)
-    send(0, go_hbm.at[first], go_relay.at[0], "pair")
     lax.fori_loop(0, BLOCKS, query_side, 0)
     z_own_forward(0)
     pair_keys(0, k_ref)
@@ -634,7 +634,6 @@
     send(3, go_relay.at[0], goall.at[head, first], "back")
     arrived(1, go_relay.at[1])
     send(4, go_relay.at[1], goall.at[other_head, second], "pair")
-    send(8, st_pair.at[1], kv_ref.at[1, c], "pair")
     x_forward(1, 0, pair_y)
     score(0)
     arrived(2, goall.at[core_head])
@@ -642,12 +641,12 @@
     x_near_finish(0, 0, y)
     x_near_finish(1, 0, pair_y)
     score(1)
+    send(8, st_pair.at[1], kv_ref.at[1, c], "pair")
     score(3)
     arrived(3, goall.at[other_head, first])
     arrived(4, goall.at[other_head, second])
     send(5, goall.at[other_head], goall.at[other_head], "core")
     acc[...] += dot_nt(goall[other_head], feature(other_head))
-    pair_keys(1, v_ref)
     arrived(5, goall.at[core_other])
     grad = (acc[...] + dot_nt(goall[core_other], feature(core_other))).astype(BF)
     pair_out[1, 0] = by_y(grad[:, cols(1)], grad[:, cols(0)])
@@ -658,14 +657,15 @@
     x_far_finish(0, 0, y)
     x_far_finish(1, 0, pair_y)
     score(2)
-    x_forward(1, 1, pair_y)
+    pair_keys(1, v_ref)
+    score_text()
     pair_rows(1, pair_out[1, 1])
     z_pair(1)
     z_own_forward(1)
-    score_text()
     x_near_finish(0, 1, y)
     x_far_finish(0, 1, y)
     take_column(1, 0)
+    x_forward(1, 1, pair_y)
     x_near_finish(1, 1, pair_y)
     take_column(1, 1)
     take_column(1, 3)
@@ -702,6 +702,8 @@
     part[0] = project(core_other)
     rsend(28, part.at[0], core_in.at[0], "core")
     part[2] = project(other_head)
+    key_grads(1, 0)
+    to_pair(1)
     slope(3)
     rarrived(28, core_in.at[0])
     pair_sum[...] = (wide(part[2]) + wide(core_in[0])).astype(BF)
@@ -718,17 +720,15 @@
             z_far(1)
         elif zq is zd:
             z_near(1)
-    key_grads(1, 0)
-    to_pair(1)
+    part[1] = project(core_head)
+    rsend(29, part.at[1], core_in.at[1], "core")
+    part[3] = project(head)
     rarrived(30, out_relay.at[0])
     rsend(32, out_relay.at[0], far_in.at[first], "back")
     rarrived(31, out_relay.at[1])
     rsend(33, out_relay.at[1], far_in.at[second], "pair")
     z_relay(1)
     key_grads(0, 0)
-    part[1] = project(core_head)
-    rsend(29, part.at[1], core_in.at[1], "core")
-    part[3] = project(head)
     to_pair(0)
     z_total(1, factor)
 

time: 78.1 us -> 79.6 us (1.019)
  Pallas kernels: 77.1 us -> 78.6 us
    pallas_call x1, Pallas kernels: 75.1 us -> 76.6 us  [shards(): pl.pallas_call(fused_kernel, out_shape=result, in_specs=[hbm] * 9 + [smem...]
where the time goes in v11:
time: 79.6 us; the launch traced here: 79.4 us
  Pallas kernels  78.6 us (99%)
  between operations  0.8 us (1%)
    pallas_call x1, Pallas kernels, shards(): pl.pallas_call(fused_kernel, out_shape=result, in_specs=[hbm] * 9 + [smem...  76.6 us
    pallas_call x1, Pallas kernels, shards(): pl.pallas_call(store_kernel, out_shape=result, in_specs=[hbm] * len(resul...  2.04 us

profile of v11, /device:TPU:0, one launch (start us, length us, event | category | flops | bytes accessed | tf_op | source)
XLA Modules:
  0.0 79.4 jit_solution(13755151267679255032)
XLA Ops:
  0.6 76.6 %shard_map.154 = (bf16[256,768]{1,0:T(8,128)(2,1)}, bf16[256,384]{1,0:T(8,128)(2,1)}, bf16[256,384]{1,0:T(8,128)(2,1)}, bf16[256,384]{1,0:T(8,128)(2,1)}, bf16[1...) custom-call(bf16[256,384]{1,0:T(8,128)(2,1)} %q_hbm.1, bf16[256,384]{1,0:T(8,128)(2,1)} %k_hbm.1, bf16[256,384]{1,0:T(8,128)(2,1)} %v_hbm.1, ...), custom_call_target="tpu_custom_call" | custom-call | tf_op jit(solution)/shard_map/pallas_call | solution.py:822
  77.2 2.0 %shard_map.155 = (bf16[256,768]{1,0:T(8,128)(2,1)}, bf16[256,384]{1,0:T(8,128)(2,1)}, bf16[256,384]{1,0:T(8,128)(2,1)}, bf16[256,384]{1,0:T(8,128)(2,1)}, bf16[1...) custom-call(bf16[256,768]{1,0:T(8,128)(2,1)} %get-tuple-element.12.refs_0_, bf16[256,384]{1,0:T(8,128)(2,1)} %get-tuple-element.13.refs_1_, ...), custom_call_target="tpu_custom_call" | custom-call | tf_op jit(solution)/shard_map/pallas_call | solution.py:901

commit v12 on v11

--- a/solution.py
+++ b/solution.py
@@ -691,28 +691,24 @@
     key_grads(1, 1)
     x_near(1)
     slope_text()
+    z_total(0, 1.0)
     slope(2)
     x_relay(1)
-    z_total(0, 1.0)
     key_grads_text(0)
     key_grads(0, 2)
     x_far(0)
-    slope(1)
+    key_grads(1, 0)
     take_attn(0, attn)
     part[0] = project(core_other)
     rsend(28, part.at[0], core_in.at[0], "core")
     part[2] = project(other_head)
-    key_grads(1, 0)
     to_pair(1)
-    slope(3)
+    slope(1)
     rarrived(28, core_in.at[0])
     pair_sum[...] = (wide(part[2]) + wide(core_in[0])).astype(BF)
     rsend(30, pair_sum.at[first], out_relay.at[0], "pair")
     rsend(31, pair_sum.at[second], out_relay.at[1], "back")
-    key_grads(0, 1)
-    key_grads(0, 3)
-    x_relay(0)
-    x_near(0)
+    slope(3)
     for zq in (zf, zu, zd, z):
         slope_row(0, zq)
         finish_dq(zq)
@@ -720,17 +716,21 @@
             z_far(1)
         elif zq is zd:
             z_near(1)
+    key_grads(0, 1)
+    key_grads(0, 3)
+    x_relay(0)
+    x_near(0)
     part[1] = project(core_head)
     rsend(29, part.at[1], core_in.at[1], "core")
-    part[3] = project(head)
     rarrived(30, out_relay.at[0])
     rsend(32, out_relay.at[0], far_in.at[first], "back")
     rarrived(31, out_relay.at[1])
     rsend(33, out_relay.at[1], far_in.at[second], "pair")
     z_relay(1)
     key_grads(0, 0)
+    part[3] = project(head)
+    z_total(1, factor)
     to_pair(0)
-    z_total(1, factor)
 
     stores = []
 

time: 79.6 us -> 81.4 us (1.023)
  Pallas kernels: 78.6 us -> 80.5 us
    pallas_call x1, Pallas kernels: 76.6 us -> 78.4 us  [shards(): pl.pallas_call(fused_kernel, out_shape=result, in_specs=[hbm] * 9 + [smem...]
where the time goes in v12:
time: 81.4 us; the launch traced here: 81.3 us
  Pallas kernels  80.5 us (99%)
    pallas_call x1, Pallas kernels, shards(): pl.pallas_call(fused_kernel, out_shape=result, in_specs=[hbm] * 9 + [smem...  78.4 us
    pallas_call x1, Pallas kernels, shards(): pl.pallas_call(store_kernel, out_shape=result, in_specs=[hbm] * len(resul...  2.04 us

profile of v12, /device:TPU:0, one launch (start us, length us, event | category | flops | bytes accessed | tf_op | source)
XLA Modules:
  0.0 81.3 jit_solution(17529169885868757434)
XLA Ops:
  0.6 78.4 %shard_map.154 = (bf16[256,768]{1,0:T(8,128)(2,1)}, bf16[256,384]{1,0:T(8,128)(2,1)}, bf16[256,384]{1,0:T(8,128)(2,1)}, bf16[256,384]{1,0:T(8,128)(2,1)}, bf16[1...) custom-call(bf16[256,384]{1,0:T(8,128)(2,1)} %q_hbm.1, bf16[256,384]{1,0:T(8,128)(2,1)} %k_hbm.1, bf16[256,384]{1,0:T(8,128)(2,1)} %v_hbm.1, ...), custom_call_target="tpu_custom_call" | custom-call | tf_op jit(solution)/shard_map/pallas_call | solution.py:822
  79.1 2.0 %shard_map.155 = (bf16[256,768]{1,0:T(8,128)(2,1)}, bf16[256,384]{1,0:T(8,128)(2,1)}, bf16[256,384]{1,0:T(8,128)(2,1)}, bf16[256,384]{1,0:T(8,128)(2,1)}, bf16[1...) custom-call(bf16[256,768]{1,0:T(8,128)(2,1)} %get-tuple-element.12.refs_0_, bf16[256,384]{1,0:T(8,128)(2,1)} %get-tuple-element.13.refs_1_, ...), custom_call_target="tpu_custom_call" | custom-call | tf_op jit(solution)/shard_map/pallas_call | solution.py:901

commit v13 on v11

--- a/solution.py
+++ b/solution.py
@@ -615,9 +615,9 @@
     load[7].wait()
     load[8].wait()
     key_side()
-    send(0, go_hbm.at[first], go_relay.at[0], "pair")
     pair_rows(0, q_ref[:, cols(2)])
     z_pair(0)
+    send(0, go_hbm.at[first], go_relay.at[0], "pair")
     lax.fori_loop(0, BLOCKS, query_side, 0)
     z_own_forward(0)
     pair_keys(0, k_ref)
@@ -634,6 +634,7 @@
     send(3, go_relay.at[0], goall.at[head, first], "back")
     arrived(1, go_relay.at[1])
     send(4, go_relay.at[1], goall.at[other_head, second], "pair")
+    send(8, st_pair.at[1], kv_ref.at[1, c], "pair")
     x_forward(1, 0, pair_y)
     score(0)
     arrived(2, goall.at[core_head])
@@ -641,12 +642,12 @@
     x_near_finish(0, 0, y)
     x_near_finish(1, 0, pair_y)
     score(1)
-    send(8, st_pair.at[1], kv_ref.at[1, c], "pair")
     score(3)
     arrived(3, goall.at[other_head, first])
     arrived(4, goall.at[other_head, second])
     send(5, goall.at[other_head], goall.at[other_head], "core")
     acc[...] += dot_nt(goall[other_head], feature(other_head))
+    pair_keys(1, v_ref)
     arrived(5, goall.at[core_other])
     grad = (acc[...] + dot_nt(goall[core_other], feature(core_other))).astype(BF)
     pair_out[1, 0] = by_y(grad[:, cols(1)], grad[:, cols(0)])
@@ -657,15 +658,14 @@
     x_far_finish(0, 0, y)
     x_far_finish(1, 0, pair_y)
     score(2)
-    pair_keys(1, v_ref)
-    score_text()
+    x_forward(1, 1, pair_y)
     pair_rows(1, pair_out[1, 1])
     z_pair(1)
     z_own_forward(1)
+    score_text()
     x_near_finish(0, 1, y)
     x_far_finish(0, 1, y)
     take_column(1, 0)
-    x_forward(1, 1, pair_y)
     x_near_finish(1, 1, pair_y)
     take_column(1, 1)
     take_column(1, 3)

time: 79.6 us -> 76.7 us (0.964)
  Pallas kernels: 78.6 us -> 75.8 us
    pallas_call x1, Pallas kernels: 76.6 us -> 73.7 us  [shards(): pl.pallas_call(fused_kernel, out_shape=result, in_specs=[hbm] * 9 + [smem...]
where the time goes in v13:
time: 76.7 us; the launch traced here: 76.6 us
  Pallas kernels  75.8 us (99%)
  between operations  0.8 us (1%)
    pallas_call x1, Pallas kernels, shards(): pl.pallas_call(fused_kernel, out_shape=result, in_specs=[hbm] * 9 + [smem...  73.7 us
    pallas_call x1, Pallas kernels, shards(): pl.pallas_call(store_kernel, out_shape=result, in_specs=[hbm] * len(resul...  2.04 us

profile of v13, /device:TPU:0, one launch (start us, length us, event | category | flops | bytes accessed | tf_op | source)
XLA Modules:
  0.0 76.6 jit_solution(13346235483970601616)
XLA Ops:
  0.6 73.7 %shard_map.154 = (bf16[256,768]{1,0:T(8,128)(2,1)}, bf16[256,384]{1,0:T(8,128)(2,1)}, bf16[256,384]{1,0:T(8,128)(2,1)}, bf16[256,384]{1,0:T(8,128)(2,1)}, bf16[1...) custom-call(bf16[256,384]{1,0:T(8,128)(2,1)} %q_hbm.1, bf16[256,384]{1,0:T(8,128)(2,1)} %k_hbm.1, bf16[256,384]{1,0:T(8,128)(2,1)} %v_hbm.1, ...), custom_call_target="tpu_custom_call" | custom-call | tf_op jit(solution)/shard_map/pallas_call | solution.py:822
  74.4 2.0 %shard_map.155 = (bf16[256,768]{1,0:T(8,128)(2,1)}, bf16[256,384]{1,0:T(8,128)(2,1)}, bf16[256,384]{1,0:T(8,128)(2,1)}, bf16[256,384]{1,0:T(8,128)(2,1)}, bf16[1...) custom-call(bf16[256,768]{1,0:T(8,128)(2,1)} %get-tuple-element.12.refs_0_, bf16[256,384]{1,0:T(8,128)(2,1)} %get-tuple-element.13.refs_1_, ...), custom_call_target="tpu_custom_call" | custom-call | tf_op jit(solution)/shard_map/pallas_call | solution.py:901
